TPU v7x, 256 devices: a whole 4x4x8 slice. The times are simulated.
256 devices in a mesh: seq: 64 (over x, z, core), head: 4 (over y).
Axes of the slice: x: 4, y: 4, z: 8, core: 2. Of those that a mesh axis runs over, the one named last changes fastest.
Arguments:
- tokens: bfloat16 [65536, 1024], P('seq'), may hold values from -48 to 48
- cotangent: bfloat16 [65536, 1024], P('seq'), may hold values from -16 to 16
- w_query: bfloat16 [1024, 1024], P(None, 'head'), may hold values from -1 to 1
- w_key: bfloat16 [1024, 1024], P(None, 'head'), may hold values from -1 to 1
- w_value: bfloat16 [1024, 1024], P(None, 'head'), may hold values from -0.1875 to 0.1875
- w_out: bfloat16 [1024, 1024], P('head'), may hold values from -0.1875 to 0.1875
Outputs:
- layer_out: bfloat16 [65536, 1024], P('seq', 'head')
- grad_tokens: bfloat16 [65536, 1024], P('seq', 'head')
- grad_w_query: float32 [1024, 1024], P('seq', 'head')
- grad_w_key: float32 [1024, 1024], P('seq', 'head')
- grad_w_value: float32 [1024, 1024], P('seq', 'head')
- grad_w_out: float32 [1024, 1024], P('head', 'seq')
All inputs are finite; a program needn't handle non-finite values.
Results may differ from a plain program's by a relative error of at most 0.017.
The roundings to bfloat16 on the way count: a program that leaves them out, or rounds other values in their place, can miss the bound.
Values may be sent and summed in bfloat16 or wider, within the bound.
No kernel may reach another device: no remote copies, remote signals or barrier semaphores. Data moves between devices by JAX's collectives and lax.ppermute only.
A program may use at most 192 MiB of HBM per device.

v0:
```python
import math

import jax
import jax.numpy as jnp
from jax import lax
from jax.sharding import PartitionSpec as P

HEAD_DIM = 64
BLOCK = 256


def partner(value, axis, bit):
    mask = 2**bit
    pairs = [(source, source ^ mask) for source in range(lax.axis_size(axis))]
    return lax.ppermute(value, axis, pairs)


def product(former, latter):
    return jnp.dot(former, latter, preferred_element_type=jnp.float32)


def contract_rows(former, latter):
    return lax.dot_general(
        former, latter, (((0,), (0,)), ((), ())), preferred_element_type=jnp.float32
    )


def contract_cols(former, latter):
    return lax.dot_general(
        former, latter, (((1,), (1,)), ((), ())), preferred_element_type=jnp.float32
    )


def coarsen(key_rows, factor):
    grouped = key_rows.astype(jnp.float32).reshape(
        key_rows.shape[0] // factor, factor, key_rows.shape[1]
    )
    return (jnp.sum(grouped, axis=1) * (1.0 / factor)).astype(jnp.bfloat16)


def expand(coarse_rows, factor):
    return jnp.repeat(coarse_rows, factor, axis=0) * (1.0 / factor)


def key_offsets():
    return jnp.concatenate(
        [
            jnp.zeros((2 * BLOCK,), jnp.float32),
            jnp.full((BLOCK,), math.log(2.0), jnp.float32),
            jnp.full((BLOCK,), math.log(4.0), jnp.float32),
            jnp.full((BLOCK,), math.log(8.0), jnp.float32),
        ]
    )


def gather_keys(key_value, half_index, level_two, level_three):
    pair_span = 2 * BLOCK
    near_rows = key_value[half_index * pair_span : (half_index + 1) * pair_span]
    far_rows = key_value[(1 - half_index) * pair_span : (2 - half_index) * pair_span]
    return jnp.concatenate([near_rows, coarsen(far_rows, 2), level_two, level_three], axis=0)


def split_heads(matrix):
    return matrix.reshape(matrix.shape[0], matrix.shape[1] // HEAD_DIM, HEAD_DIM)


def probabilities(part_query, key_rows, offsets):
    scores = jnp.einsum(
        "qhd,khd->hqk",
        split_heads(part_query),
        split_heads(key_rows),
        preferred_element_type=jnp.float32,
    )
    scores = scores * (1.0 / math.sqrt(HEAD_DIM)) + offsets
    row_max = jnp.max(scores, axis=-1, keepdims=True)
    raised = jnp.exp(scores - row_max)
    return raised / jnp.sum(raised, axis=-1, keepdims=True)


def group_forward(queries, key_value, level_two, level_three):
    feature_width = queries.shape[1]
    pair_span = 2 * BLOCK
    offsets = key_offsets()
    outputs = []
    for half_index in range(2):
        key_rows = gather_keys(key_value, half_index, level_two, level_three)
        part_query = queries[half_index * pair_span : (half_index + 1) * pair_span]
        attention = probabilities(part_query, key_rows[:, :feature_width], offsets)
        weights = attention.astype(jnp.bfloat16)
        blended = jnp.einsum(
            "hqk,khd->qhd",
            weights,
            split_heads(key_rows[:, feature_width:]),
            preferred_element_type=jnp.float32,
        )
        outputs.append(blended.reshape(pair_span, feature_width))
    return jnp.concatenate(outputs, axis=0).astype(jnp.bfloat16)


def attention_grads(attention, part_query, key_rows, part_grad, feature_width):
    query_count = part_query.shape[0]
    key_count = key_rows.shape[0]
    query_heads = split_heads(part_query)
    key_heads = split_heads(key_rows[:, :feature_width])
    value_heads = split_heads(key_rows[:, feature_width:])
    grad_heads = split_heads(part_grad)
    weights = attention.astype(jnp.bfloat16)
    grad_attention = jnp.einsum(
        "qhd,khd->hqk", grad_heads, value_heads, preferred_element_type=jnp.float32
    )
    row_inner = jnp.sum(attention * grad_attention, axis=-1, keepdims=True)
    grad_scores = (attention * (grad_attention - row_inner) * (1.0 / math.sqrt(HEAD_DIM))).astype(
        jnp.bfloat16
    )
    grad_query = jnp.einsum(
        "hqk,khd->qhd", grad_scores, key_heads, preferred_element_type=jnp.float32
    )
    grad_keys = jnp.einsum(
        "hqk,qhd->khd", grad_scores, query_heads, preferred_element_type=jnp.float32
    )
    grad_values = jnp.einsum(
        "hqk,qhd->khd", weights, grad_heads, preferred_element_type=jnp.float32
    )
    grad_key_value = jnp.concatenate(
        [
            grad_keys.reshape(key_count, feature_width),
            grad_values.reshape(key_count, feature_width),
        ],
        axis=1,
    )
    return (grad_query.reshape(query_count, feature_width), grad_key_value)


def group_backward(queries, key_value, level_two, level_three, d_attended):
    feature_width = queries.shape[1]
    pair_span = 2 * BLOCK
    offsets = key_offsets()
    halves = []
    for half_index in range(2):
        key_rows = gather_keys(key_value, half_index, level_two, level_three)
        part_query = queries[half_index * pair_span : (half_index + 1) * pair_span]
        part_grad = d_attended[half_index * pair_span : (half_index + 1) * pair_span]
        attention = probabilities(part_query, key_rows[:, :feature_width], offsets)
        halves.append(attention_grads(attention, part_query, key_rows, part_grad, feature_width))
    first_half = halves[0][1]
    second_half = halves[1][1]
    grad_query = jnp.concatenate([halves[0][0], halves[1][0]], axis=0)
    grad_own = jnp.concatenate(
        [
            first_half[:pair_span] + expand(second_half[pair_span : pair_span + BLOCK], 2),
            second_half[:pair_span] + expand(first_half[pair_span : pair_span + BLOCK], 2),
        ],
        axis=0,
    )
    grad_two = (
        first_half[pair_span + BLOCK : pair_span + 2 * BLOCK]
        + second_half[pair_span + BLOCK : pair_span + 2 * BLOCK]
    )
    grad_three = first_half[pair_span + 2 * BLOCK :] + second_half[pair_span + 2 * BLOCK :]
    return (grad_query, grad_own, grad_two, grad_three)


def send_coarse(payload, bit_number):
    return partner(payload, "seq", bit_number)


def return_coarse(payload, bit_number):
    return partner(payload.astype(jnp.bfloat16), "seq", bit_number).astype(payload.dtype)


def sum_weights(stacked):
    return lax.psum_scatter(stacked, "seq", scatter_dimension=1, tiled=True)


def on_device(tokens, cotangent, w_query, w_key, w_value, w_out):
    queries = product(tokens, w_query).astype(jnp.bfloat16)
    key_proj = product(tokens, w_key).astype(jnp.bfloat16)
    values = product(tokens, w_value).astype(jnp.bfloat16)
    key_value = jnp.concatenate([key_proj, values], axis=1)
    feature_width = w_query.shape[1]
    is_lower = lax.axis_index("seq") % 2 == 0
    own_two = coarsen(key_value, 4)
    own_three = coarsen(key_value, 8)
    level_two = send_coarse(own_two, 0)
    partner_three = send_coarse(own_three, 0)
    pair_three = jnp.where(
        is_lower,
        jnp.concatenate([own_three, partner_three], axis=0),
        jnp.concatenate([partner_three, own_three], axis=0),
    )
    level_three = send_coarse(pair_three, 1)
    attended = group_forward(queries, key_value, level_two, level_three)
    layer_out = lax.psum_scatter(
        product(attended, w_out).astype(jnp.bfloat16), "head", scatter_dimension=1, tiled=True
    )
    grad_scale = 1.0 / math.sqrt(lax.axis_size("seq") * tokens.shape[0])
    out_term = contract_rows(cotangent, attended) * grad_scale
    d_attended = contract_cols(cotangent, w_out).astype(jnp.bfloat16)
    grad_query, grad_own, grad_two, grad_three = group_backward(
        queries, key_value, level_two, level_three, d_attended
    )
    half_rows = BLOCK // 2
    from_pair = return_coarse(grad_three, 1)
    own_share = jnp.where(is_lower, from_pair[:half_rows], from_pair[half_rows:])
    peer_share = jnp.where(is_lower, from_pair[half_rows:], from_pair[:half_rows])
    got_two = return_coarse(grad_two, 0)
    got_three = own_share + return_coarse(peer_share, 0)
    grad_key_value = grad_own + expand(got_two, 4) + expand(got_three, 8)
    query_grad = grad_query.astype(jnp.bfloat16)
    key_grad = grad_key_value[:, :feature_width].astype(jnp.bfloat16)
    value_grad = grad_key_value[:, feature_width:].astype(jnp.bfloat16)
    input_part = (
        contract_cols(query_grad, w_query)
        + contract_cols(key_grad, w_key)
        + contract_cols(value_grad, w_value)
    )
    grad_tokens = lax.psum_scatter(
        input_part.astype(jnp.bfloat16), "head", scatter_dimension=1, tiled=True
    )
    proj_terms = [
        contract_rows(tokens, query_grad) * grad_scale,
        contract_rows(tokens, key_grad) * grad_scale,
        contract_rows(tokens, value_grad) * grad_scale,
    ]
    summed = sum_weights(jnp.stack(proj_terms + [out_term]))
    out_summed = summed[3]
    return (layer_out, grad_tokens, summed[0], summed[1], summed[2], out_summed.T)


def solution(mesh):
    return jax.shard_map(
        on_device,
        mesh=mesh,
        in_specs=(
            P("seq", None),
            P("seq", None),
            P(None, "head"),
            P(None, "head"),
            P(None, "head"),
            P("head", None),
        ),
        out_specs=(
            P("seq", "head"),
            P("seq", "head"),
            P("seq", "head"),
            P("seq", "head"),
            P("seq", "head"),
            P("head", "seq"),
        ),
        check_vma=False,
    )
```

profile of v0, /device:TPU:24, one launch (start us, length us, event | category | flops | bytes accessed | tf_op | source)
XLA Modules:
  0.0 445.6 jit_solution(9172456980743894442)
XLA Ops:
  26.6 3.3 reduce_sum.70
  37.6 3.3 reduce_sum.77
  48.0 6.4 %fusion.98 = f32[4,512,1280]{2,1,0:T(8,128)} fusion(bf16[512,4,64]{0,2,1:T(8,128)(2,1)} %bitcast.115, bf16[1280,4,64]{0,2,1:T(8,128)(2,1)S(1)} %bitcast.109), kind=kOutput, calls=%fused_computation.138 | convolution fusion | flops 335544320 | bytes 11403264 | tf_op jit(solution)/shard_map/qhd,khd->hqk/dot_general | solution.py:108
  54.4 8.1 %fusion.95 = (f32[4,512]{1,0:T(4,128)S(1)}, f32[4,512,1280]{2,1,0:T(8,128)}) fusion(f32[1280]{0:T(1024)S(1)} %copy-done.19, bf16[512,4,64]{0,2,1:T(8,128)(2,1)} %bitcast.141, bf16[1280,4,64]{0,2,1:T(8,128)(2,1)} %bitcast.125), kind=kOutput, calls=%fused_computation.135 | convolution fusion | flops 346031360 | bytes 11416576 | tf_op jit(solution)/shard_map/sub | solution.py:76
  62.5 5.2 %fusion.49 = bf16[4,64,512]{2,1,0:T(8,128)(2,1)} fusion(bf16[1280,4,64]{0,2,1:T(8,128)(2,1)S(1)} %bitcast.110, f32[4,512]{1,0:T(4,128)S(1)} %get-tuple-element.38, f32[1280]{0:T(1024)S(1)} %copy-done.19, bf16[512,4,64]{0,2,1:T(8,128)(2,1)} %bitcast.142, bf16[1280,4,64]{0,2,1:T(8,128)(2,1)} %bitcast.126), kind=kOutput, calls=%fused_computation.71 | convolution fusion | flops 684330240 | bytes 1848320 | tf_op jit(solution)/shard_map/hqk,khd->qhd/dot_general | solution.py:90
  67.8 19.5 %fusion.52 = bf16[4,64,512]{2,1,0:T(8,128)(2,1)} fusion(bf16[1280,4,64]{0,2,1:T(8,128)(2,1)} %bitcast.127, f32[4,512,1280]{2,1,0:T(8,128)} %fusion.98, f32[4,512,1280]{2,1,0:T(8,128)} %get-tuple-element.39, f32[4,512]{1,0:T(4,128)S(1)} %get-tuple-element.38), kind=kOutput, calls=%fused_computation.72 | convolution fusion | flops 354028800 | bytes 21897216 | tf_op jit(solution)/shard_map/hqk,khd->qhd/dot_general | solution.py:115
  87.2 20.2 %fusion.23 = f32[4,64,1280]{2,1,0:T(8,128)} fusion(bf16[512,4,64]{0,2,1:T(8,128)(2,1)S(1)} %bitcast.144, f32[4,512,1280]{2,1,0:T(8,128)} %fusion.98, f32[4,512,1280]{2,1,0:T(8,128)} %get-tuple-element.39, f32[4,512]{1,0:T(4,128)S(1)} %get-tuple-element.38), kind=kOutput, calls=%fused_computation.24 | convolution fusion | flops 353897728 | bytes 22552576 | tf_op jit(solution)/shard_map/hqk,qhd->khd/dot_general | solution.py:118
  107.4 5.7 %fusion.28 = f32[4,64,1280]{2,1,0:T(8,128)} fusion(bf16[512,4,64]{0,2,1:T(8,128)(2,1)} %bitcast.116, f32[4,512]{1,0:T(4,128)S(1)} %get-tuple-element.38, f32[1280]{0:T(1024)S(1)} %copy-done.19, bf16[512,4,64]{0,2,1:T(8,128)(2,1)} %bitcast.143, bf16[1280,4,64]{0,2,1:T(8,128)(2,1)} %bitcast.128), kind=kOutput, calls=%fused_computation.38 | convolution fusion | flops 684199168 | bytes 2503680 | tf_op jit(solution)/shard_map/hqk,qhd->khd/dot_general | solution.py:121
  114.5 6.6 %fusion.97 = f32[4,512,1280]{2,1,0:T(8,128)} fusion(bf16[512,4,64]{0,2,1:T(8,128)(2,1)} %bitcast.113, bf16[1280,4,64]{0,2,1:T(8,128)(2,1)S(1)} %bitcast.111), kind=kOutput, calls=%fused_computation.137 | convolution fusion | flops 335544320 | bytes 11403264 | tf_op jit(solution)/shard_map/qhd,khd->hqk/dot_general | solution.py:108
  121.1 7.8 %fusion.96 = (f32[4,512]{1,0:T(4,128)S(1)}, f32[4,512,1280]{2,1,0:T(8,128)}) fusion(f32[1280]{0:T(1024)S(1)} %copy-done.19, bf16[512,4,64]{0,2,1:T(8,128)(2,1)} %bitcast.137, bf16[1280,4,64]{0,2,1:T(8,128)(2,1)S(1)} %bitcast.121), kind=kOutput, calls=%fused_computation.136 | convolution fusion | flops 346031360 | bytes 11416576 | tf_op jit(solution)/shard_map/sub | solution.py:76
  128.9 5.0 %fusion.46 = bf16[4,64,512]{2,1,0:T(8,128)(2,1)} fusion(bf16[1280,4,64]{0,2,1:T(8,128)(2,1)S(1)} %bitcast.112, f32[4,512]{1,0:T(4,128)S(1)} %get-tuple-element.40, f32[1280]{0:T(1024)S(1)} %copy-done.19, bf16[512,4,64]{0,2,1:T(8,128)(2,1)} %bitcast.138, bf16[1280,4,64]{0,2,1:T(8,128)(2,1)S(1)} %bitcast.122), kind=kOutput, calls=%fused_computation.70 | convolution fusion | flops 684330240 | bytes 1848320 | tf_op jit(solution)/shard_map/hqk,khd->qhd/dot_general | solution.py:90
  133.9 24.7 %fusion.55 = bf16[4,64,512]{2,1,0:T(8,128)(2,1)} fusion(bf16[1280,4,64]{0,2,1:T(8,128)(2,1)S(1)} %bitcast.123, f32[4,512,1280]{2,1,0:T(8,128)} %fusion.97, f32[4,512,1280]{2,1,0:T(8,128)} %get-tuple-element.41, f32[4,512]{1,0:T(4,128)S(1)} %get-tuple-element.40), kind=kOutput, calls=%fused_computation.73 | convolution fusion | flops 354028800 | bytes 21897216 | tf_op jit(solution)/shard_map/hqk,khd->qhd/dot_general | solution.py:115
  158.6 20.0 %fusion.17 = f32[4,64,1280]{2,1,0:T(8,128)} fusion(bf16[512,4,64]{0,2,1:T(8,128)(2,1)S(1)} %bitcast.139, f32[4,512,1280]{2,1,0:T(8,128)} %fusion.97, f32[4,512,1280]{2,1,0:T(8,128)} %get-tuple-element.41, f32[4,512]{1,0:T(4,128)S(1)} %get-tuple-element.40), kind=kOutput, calls=%fused_computation.22 | convolution fusion | flops 353897728 | bytes 22552576 | tf_op jit(solution)/shard_map/hqk,qhd->khd/dot_general | solution.py:118
  178.6 4.4 fusion.32
  183.0 2.8 copy.46
  185.8 2.8 copy.47
  190.4 2.8 copy.45
  198.9 2.9 mul.117
  206.9 2.9 mul.115
  221.3 3.0 mul.119
  224.3 2.8 fusion.37
  230.9 5.2 %copy.48 = f32[4,1024,256]{2,0,1:T(4,128)} copy(f32[4,1024,256]{1,2,0:T(8,128)} %pad_maximum_fusion) | data formatting | bytes 8388608 | tf_op jit(solution)/shard_map/stack | solution.py:225
  236.2 3.3 convolution_convert_fusion
  245.7 188.5 %all-reduce.3.cloned.1.call-done = f32[4,1024,256]{2,0,1:T(4,128)} async-done(((f32[4,1024,256]{2,0,1:T(4,128)}), f32[4,1024,256]{2,0,1:T(4,128)}) %all-reduce.3.cloned.1.call-update) | async-done | bytes 4194320
  (109 shorter events, 71.4 us)
Async XLA Ops:
  8.0 426.2 %all-reduce.3.cloned.1.call-start = ((), (), s32[]{:S(2)}) async-start(), calls=%async_computation.4 | async-start | bytes 8388608
  11.4 6.1 %copy-start.1 = (bf16[1024,256]{1,0:T(8,128)(2,1)}, bf16[1024,256]{1,0:T(8,128)(2,1)S(1)}, u32[]{:S(2)}) copy-start(bf16[1024,256]{1,0:T(8,128)(2,1)S(1)} %convolution_convert_fusion.4) | copy-start | bytes 1572868
  12.1 6.6 %copy-start.2 = (bf16[1024,256]{1,0:T(8,128)(2,1)}, bf16[1024,256]{1,0:T(8,128)(2,1)S(1)}, u32[]{:S(2)}) copy-start(bf16[1024,256]{1,0:T(8,128)(2,1)S(1)} %convolution_convert_fusion.3) | copy-start | bytes 1572868
  12.9 18.9 %collective-permute-start.1 = (bf16[128,512]{1,0:T(8,128)(2,1)S(1)}, bf16[128,512]{1,0:T(8,128)(2,1)S(1)}, u32[]{:S(2)}, u32[]{:S(2)}) collective-permute-start(bf16[128,512]{1,0:T(8,128)(2,1)S(1)} %multiply_convert_fusion.5), channel_id=1, source_target_pairs={{0,4},{4,0},{8,12},{12,8},{16,20},{20,16},{24,28},{28,24},{32,36},... | collective-permute-start | bytes 393224 | tf_op jit(solution)/shard_map/ppermute | solution.py:15
  18.3 23.7 %collective-permute-start = (bf16[256,512]{1,0:T(8,128)(2,1)}, bf16[256,512]{1,0:T(8,128)(2,1)}, u32[]{:S(2)}, u32[]{:S(2)}) collective-permute-start(bf16[256,512]{1,0:T(8,128)(2,1)} %multiply_convert_fusion.3), channel_id=1, source_target_pairs={{0,4},{4,0},{8,12},{12,8},{16,20},{20,16},{24,28},{28,24},{32,36},... | collective-permute-start | bytes 786440 | tf_op jit(solution)/shard_map/ppermute | solution.py:15
  20.0 3.4 copy-start.8
  32.5 9.4 %collective-permute-start.2 = (bf16[256,512]{1,0:T(8,128)(2,1)}, bf16[256,512]{1,0:T(8,128)(2,1)}, u32[]{:S(2)}, u32[]{:S(2)}) collective-permute-start(bf16[256,512]{1,0:T(8,128)(2,1)} %maximum_select_fusion), channel_id=1, source_target_pairs={{0,8},{4,12},{8,0},{12,4},{16,24},{20,28},{24,16},{28,20},{32,40},... | collective-permute-start | bytes 786440 | tf_op jit(solution)/shard_map/ppermute | solution.py:15
  48.0 6.4 %copy-start.19 = (f32[1280]{0:T(1024)S(1)}, f32[1280]{0:T(1024)}, u32[]{:S(2)}) copy-start(f32[1280]{0:T(1024)} %constant.36.clone.1) | copy-start | bytes 15364
  67.8 19.5 %copy-start.16 = (bf16[512,256]{0,1:T(8,128)(2,1)S(1)}, bf16[512,256]{0,1:T(8,128)(2,1)}, u32[]{:S(2)}) copy-start(bf16[512,256]{0,1:T(8,128)(2,1)} %get-tuple-element.35) | copy-start | bytes 786436
  107.4 5.8 %copy-start.3 = (bf16[1280,256]{1,0:T(8,128)(2,1)S(1)}, bf16[1280,256]{1,0:T(8,128)(2,1)}, u32[]{:S(2)}) copy-start(bf16[1280,256]{1,0:T(8,128)(2,1)} %get-tuple-element.26) | copy-start | bytes 1966084
  114.5 6.6 %copy-start.7 = (bf16[1280,256]{0,1:T(8,128)(2,1)S(1)}, bf16[1280,256]{0,1:T(8,128)(2,1)}, u32[]{:S(2)}) copy-start(bf16[1280,256]{0,1:T(8,128)(2,1)} %copy.41) | copy-start | bytes 1966084
  133.9 24.7 %copy-start.15 = (bf16[512,256]{0,1:T(8,128)(2,1)S(1)}, bf16[512,256]{0,1:T(8,128)(2,1)}, u32[]{:S(2)}) copy-start(bf16[512,256]{0,1:T(8,128)(2,1)} %get-tuple-element.34) | copy-start | bytes 786436
  158.6 20.0 %copy-start.4 = (bf16[512,256]{0,1:T(8,128)(2,1)S(1)}, bf16[512,256]{0,1:T(8,128)(2,1)}, u32[]{:S(2)}) copy-start(bf16[512,256]{0,1:T(8,128)(2,1)} %get-tuple-element.32) | copy-start | bytes 786436
  195.8 21.1 %collective-permute-start.4 = (bf16[256,512]{1,0:T(8,128)(2,1)}, bf16[256,512]{1,0:T(8,128)(2,1)}, u32[]{:S(2)}, u32[]{:S(2)}) collective-permute-start(bf16[256,512]{1,0:T(8,128)(2,1)} %get-tuple-element.18), channel_id=1, source_target_pairs={{0,8},{4,12},{8,0},{12,4},{16,24},{20,28},{24,16},{28,20},{32,40},... | collective-permute-start | bytes 786440 | tf_op jit(solution)/shard_map/ppermute | solution.py:15
  197.3 21.3 %collective-permute-start.3 = (bf16[256,512]{1,0:T(8,128)(2,1)}, bf16[256,512]{1,0:T(8,128)(2,1)}, u32[]{:S(2)}, u32[]{:S(2)}) collective-permute-start(bf16[256,512]{1,0:T(8,128)(2,1)} %get-tuple-element.19), channel_id=1, source_target_pairs={{0,4},{4,0},{8,12},{12,8},{16,20},{20,16},{24,28},{28,24},{32,36},... | collective-permute-start | bytes 786440 | tf_op jit(solution)/shard_map/ppermute | solution.py:15
  209.8 5.4 %copy-start.13 = (bf16[4,64,512]{2,1,0:T(8,128)(2,1)S(1)}, bf16[4,64,512]{2,1,0:T(8,128)(2,1)}, u32[]{:S(2)}) copy-start(bf16[4,64,512]{2,1,0:T(8,128)(2,1)} %fusion.49) | copy-start | bytes 786436
  209.8 5.4 %copy-start.14 = (bf16[4,64,512]{2,1,0:T(8,128)(2,1)S(1)}, bf16[4,64,512]{2,1,0:T(8,128)(2,1)}, u32[]{:S(2)}) copy-start(bf16[4,64,512]{2,1,0:T(8,128)(2,1)} %fusion.46) | copy-start | bytes 786436
  209.8 5.4 %copy-start.17 = (bf16[1024,1024]{1,0:T(8,128)(2,1)S(1)}, bf16[1024,1024]{1,0:T(8,128)(2,1)}, u32[]{:S(2)}) copy-start(bf16[1024,1024]{1,0:T(8,128)(2,1)} %param.7) | copy-start | bytes 6291460
  218.0 6.2 %collective-permute-start.5 = (bf16[128,512]{1,0:T(8,128)(2,1)S(1)}, bf16[128,512]{1,0:T(8,128)(2,1)S(1)}, u32[]{:S(2)}, u32[]{:S(2)}) collective-permute-start(bf16[128,512]{1,0:T(8,128)(2,1)S(1)} %select_convert_fusion), channel_id=1, source_target_pairs={{0,4},{4,0},{8,12},{12,8},{16,20},{20,16},{24,28},{28,24},{32,36},... | collective-permute-start | bytes 393224 | tf_op jit(solution)/shard_map/ppermute | solution.py:15
  224.3 4.3 copy-start.5
  224.3 4.3 copy-start.6
  236.1 3.5 copy-start.12
  236.2 201.6 %reduce-scatter.3.cloned.1.call-start = ((), (), s32[]{:S(2)}) async-start(), calls=%async_computation.2 | async-start | bytes 2621440 | tf_op jit(solution)/shard_map/reduce_scatter | solution.py:193
  239.6 198.2 %reduce-scatter.5.cloned.1.call-start = ((), (), s32[]{:S(2)}) async-start(), calls=%async_computation.3 | async-start | bytes 2621440 | tf_op jit(solution)/shard_map/reduce_scatter | solution.py:217
  (5 other events, 10.2 us)
Sparse Core Ops, SparseCore 0:
  236.3 197.9 all-reduce.2
Sparse Core Ops, SparseCore 1:
  239.7 32.0 reduce-scatter.2
  275.0 31.9 reduce-scatter.4
where the time goes:
time: 454 us; the launch traced here: 446 us
  waiting for transfers between devices  189 us (42%)
  matrix products  154 us (34%)
  local copies, waits for them, and re-layouts  49.3 us (11%)
  other arithmetic  31.2 us (7%)
  between operations  17 us (4%)
  starting transfers between devices  5.34 us (1%)
    unnamed x4, waiting for transfers between devices  189 us
    dot_general x2, matrix products, attention_grads(): jnp.einsum('hqk,khd->qhd', grad_scores, key_heads, preferred_element_type...  44.1 us
    dot_general x2, matrix products, attention_grads(): jnp.einsum('hqk,qhd->khd', grad_scores, query_heads, preferred_element_ty...  40.2 us
    sub x2, matrix products, probabilities(): raised = jnp.exp(scores - row_max)  15.9 us
    dot_general x2, matrix products, attention_grads(): jnp.einsum('qhd,khd->hqk', grad_heads, value_heads, preferred_element_typ...  12.9 us
    dot_general x2, matrix products, group_forward(): jnp.einsum('hqk,khd->qhd', weights, split_heads(key_rows[:, feature_width...  10.3 us
    dot_general x2, matrix products, attention_grads(): jnp.einsum('hqk,qhd->khd', weights, grad_heads, preferred_element_type=jn...  10.2 us
    reduce_sum x4, other arithmetic, coarsen(): return (jnp.sum(grouped, axis=1) * (1.0 / factor)).astype(jnp.bfloat16)  9.9 us
  transfers between devices with their start and end apart: 9, of which 1 were waited for; matrix products, arithmetic and copies ran while one was open for 14% of the time, Pallas kernels for 0%

commit v1 on v0

v1 whole, which is shorter than its diff:
```python
import functools
import math

import jax
import jax.numpy as jnp
from jax import lax
from jax.experimental import pallas as pl
from jax.experimental.pallas import tpu as pltpu
from jax.sharding import PartitionSpec as P

HEAD_DIM = 64
BLOCK = 256
SPAN = 2 * BLOCK
KEYS = 5 * BLOCK
ROWS = 4 * BLOCK
WIDTH = 1024
COLS = 256
MIB = 1024 * 1024
OFFSETS = (0.0, 0.0, 1.0, 2.0, 3.0)
SCORE_SCALE = 1.0 / (math.log(2.0) * math.sqrt(HEAD_DIM))
INV_ROOT = 1.0 / math.sqrt(HEAD_DIM)
bf16 = jnp.bfloat16
f32 = jnp.float32


def dot_nn(a, b):
    return lax.dot_general(a, b, (((1,), (0,)), ((), ())), preferred_element_type=f32)


def dot_nt(a, b):
    return lax.dot_general(a, b, (((1,), (1,)), ((), ())), preferred_element_type=f32)


def params(mib):
    return pltpu.CompilerParams(vmem_limit_bytes=mib * MIB)


def shape(dims, dtype=bf16):
    return jax.ShapeDtypeStruct(dims, dtype)


def cost(macs, nbytes):
    return pl.CostEstimate(flops=2 * macs, bytes_accessed=nbytes, transcendentals=0)


def run_matrix(rows, cols, shift, expand):
    i = lax.broadcasted_iota(jnp.int32, (rows, cols), 0)
    j = lax.broadcasted_iota(jnp.int32, (rows, cols), 1)
    inside = (i >> shift) == j if expand else i == (j >> shift)
    return jnp.where(inside, 2.0**-shift, 0.0).astype(bf16)


def kv_kernel(x_ref, wk_ref, wv_ref, kv_ref, c2_ref, c4_ref, c8_ref):
    x = x_ref[...]
    kv_ref[:, :COLS] = dot_nn(x, wk_ref[...]).astype(bf16)
    kv_ref[:, COLS:] = dot_nn(x, wv_ref[...]).astype(bf16)
    kv = kv_ref[...]
    for shift, ref in ((1, c2_ref), (2, c4_ref), (3, c8_ref)):
        average = run_matrix(BLOCK >> shift, BLOCK, shift, False)
        ref[...] = dot_nn(average, kv).astype(bf16)


def project_kv(tokens, w_key, w_value):
    whole = pl.BlockSpec((WIDTH, COLS), lambda i: (0, 0))
    return pl.pallas_call(
        kv_kernel,
        grid=(4,),
        in_specs=[pl.BlockSpec((BLOCK, WIDTH), lambda i: (i, 0)), whole, whole],
        out_specs=[pl.BlockSpec((BLOCK >> s, 2 * COLS), lambda i: (i, 0)) for s in range(4)],
        out_shape=[shape((ROWS >> s, 2 * COLS)) for s in range(4)],
        compiler_params=params(24),
        cost_estimate=cost(ROWS * WIDTH * 2 * COLS, 6 * MIB),
        name="project_kv",
    )(tokens, w_key, w_value)


def q_kernel(x_ref, c_ref, wq_ref, wo_ref, q_ref, da_ref):
    q_ref[...] = dot_nn(x_ref[...], wq_ref[...]).astype(bf16)
    da_ref[...] = dot_nt(c_ref[...], wo_ref[...]).astype(bf16)


def project_q(tokens, cotangent, w_query, w_out):
    rows = pl.BlockSpec((BLOCK, WIDTH), lambda i: (i, 0))
    out = pl.BlockSpec((BLOCK, COLS), lambda i: (i, 0))
    return pl.pallas_call(
        q_kernel,
        grid=(4,),
        in_specs=[
            rows,
            rows,
            pl.BlockSpec((WIDTH, COLS), lambda i: (0, 0)),
            pl.BlockSpec((COLS, WIDTH), lambda i: (0, 0)),
        ],
        out_specs=[out, out],
        out_shape=[shape((ROWS, COLS))] * 2,
        compiler_params=params(24),
        cost_estimate=cost(ROWS * WIDTH * 2 * COLS, 7 * MIB),
        name="project_q",
    )(tokens, cotangent, w_query, w_out)


def entry_rows(refs, kb, lo):
    near, c2, l2, l3a, l3b = refs
    if kb < 2:
        return near[kb * BLOCK : (kb + 1) * BLOCK, lo : lo + 128]
    if kb == 2:
        return c2[:, lo : lo + 128]
    if kb == 3:
        return l2[:, lo : lo + 128]
    return jnp.concatenate([l3a[:, lo : lo + 128], l3b[:, lo : lo + 128]], axis=0)


def only_head(ref, head):
    lane = lax.broadcasted_iota(jnp.int32, (SPAN, 128), 1)
    keep = lane < HEAD_DIM if head % 2 == 0 else lane >= HEAD_DIM
    pair = head // 2 * 128
    return jnp.where(keep, ref[:, pair : pair + 128], jnp.zeros((), bf16))


def fold(values, combine):
    return combine(values.reshape(BLOCK // 8, 8, SPAN), axis=0)


def forward_kernel(*refs):
    entries, q_ref, ot_ref, stat_ref = refs[:5], refs[5], refs[6], refs[7]
    t_s, vt_s, qm_s = refs[8:]
    for kb in range(5):
        rows = slice(kb * BLOCK, (kb + 1) * BLOCK)
        for pair in range(2):
            vt_s[pair * 128 : pair * 128 + 128, rows] = entry_rows(
                entries, kb, COLS + pair * 128
            ).T
    for head in range(4):
        qm_s[head] = only_head(q_ref, head)
    for head in range(4):
        lo = head // 2 * 128
        slot = head % 2
        tops = []
        for kb in range(5):
            rows = slice(kb * BLOCK, (kb + 1) * BLOCK)
            t = dot_nt(entry_rows(entries, kb, lo), qm_s[head]) * SCORE_SCALE
            t_s[slot, rows] = t
            tops.append(fold(t, jnp.max) + OFFSETS[kb])
        top = jnp.max(functools.reduce(jnp.maximum, tops), axis=0, keepdims=True)
        total = jnp.zeros((8, SPAN), f32)
        for kb in range(5):
            rows = slice(kb * BLOCK, (kb + 1) * BLOCK)
            raised = jnp.exp2(t_s[slot, rows] + (OFFSETS[kb] - top))
            t_s[slot, rows] = raised
            total = total + fold(raised, jnp.sum)
        total = jnp.sum(total, axis=0, keepdims=True)
        inverse = 1.0 / total
        out = jnp.zeros((HEAD_DIM, SPAN), f32)
        mine = slice(head * HEAD_DIM, (head + 1) * HEAD_DIM)
        for kb in range(5):
            rows = slice(kb * BLOCK, (kb + 1) * BLOCK)
            weights = (t_s[slot, rows] * inverse).astype(bf16)
            out = out + dot_nn(vt_s[mine, rows], weights)
        ot_ref[mine] = out.astype(bf16)
        stat_ref[head : head + 1] = top
        stat_ref[head + 4 : head + 5] = inverse


def entry_specs():
    return [
        pl.BlockSpec((SPAN, 2 * COLS), lambda i: (i, 0)),
        pl.BlockSpec((BLOCK, 2 * COLS), lambda i: (1 - i, 0)),
        pl.BlockSpec((BLOCK, 2 * COLS), lambda i: (0, 0)),
        pl.BlockSpec((BLOCK // 2, 2 * COLS), lambda i: (0, 0)),
        pl.BlockSpec((BLOCK // 2, 2 * COLS), lambda i: (0, 0)),
    ]


def attend(entries, queries):
    return pl.pallas_call(
        forward_kernel,
        grid=(2,),
        in_specs=entry_specs() + [pl.BlockSpec((SPAN, COLS), lambda i: (i, 0))],
        out_specs=[
            pl.BlockSpec((COLS, SPAN), lambda i: (0, i)),
            pl.BlockSpec((8, SPAN), lambda i: (0, i)),
        ],
        out_shape=[shape((COLS, ROWS)), shape((8, ROWS), f32)],
        scratch_shapes=[
            pltpu.VMEM((2, KEYS, SPAN), f32),
            pltpu.VMEM((COLS, KEYS), bf16),
            pltpu.VMEM((4, SPAN, 128), bf16),
        ],
        compiler_params=params(40),
        cost_estimate=cost(4 * 2 * 4 * ROWS * KEYS * 64, 4 * MIB),
        name="attend",
    )(*entries, queries)


def split_product(matrix, values):
    high = values.astype(bf16)
    low = (values - high.astype(f32)).astype(bf16)
    return dot_nn(matrix, high) + dot_nn(matrix, low)


def backward_kernel(*refs):
    entries, q_ref, da_ref, stat_ref = refs[:5], refs[5], refs[6], refs[7]
    qgt_ref, own_ref, g2_ref, g3_ref = refs[8:12]
    a_s, p_s, kt_s, qm_s, dm_s, grad_s, far_s = refs[12:]
    for kb in range(5):
        rows = slice(kb * BLOCK, (kb + 1) * BLOCK)
        for pair in range(2):
            kt_s[pair * 128 : pair * 128 + 128, rows] = entry_rows(entries, kb, pair * 128).T
    for head in range(4):
        qm_s[head] = only_head(q_ref, head)
        dm_s[head] = only_head(da_ref, head)
    for head in range(4):
        lo = head // 2 * 128
        slot = head % 2
        top = stat_ref[head : head + 1]
        inverse = stat_ref[head + 4 : head + 5]
        inner = jnp.zeros((8, SPAN), f32)
        for kb in range(5):
            rows = slice(kb * BLOCK, (kb + 1) * BLOCK)
            t = dot_nt(entry_rows(entries, kb, lo), qm_s[head]) * SCORE_SCALE
            a = jnp.exp2(t + (OFFSETS[kb] - top)) * inverse
            p = dot_nt(entry_rows(entries, kb, COLS + lo), dm_s[head])
            a_s[slot, rows] = a
            p_s[slot, rows] = p
            inner = inner + fold(a * p, jnp.sum)
        inner = jnp.sum(inner, axis=0, keepdims=True)
        query_grad = jnp.zeros((HEAD_DIM, SPAN), f32)
        mine = slice(head * HEAD_DIM, (head + 1) * HEAD_DIM)
        for kb in range(5):
            rows = slice(kb * BLOCK, (kb + 1) * BLOCK)
            a = a_s[slot, rows]
            weights = a.astype(bf16)
            scores = (a * (p_s[slot, rows] - inner)).astype(bf16)
            query_grad = query_grad + dot_nn(kt_s[mine, rows], scores)
            dk = dot_nn(scores, qm_s[head])
            dv = dot_nn(weights, dm_s[head])
            if head % 2 == 0:
                grad_s[rows, lo : lo + 128] = dk
                grad_s[rows, COLS + lo : COLS + lo + 128] = dv
            else:
                dk = (grad_s[rows, lo : lo + 128] + dk) * INV_ROOT
                grad_s[rows, lo : lo + 128] = dk
                grad_s[rows, COLS + lo : COLS + lo + 128] += dv
        qgt_ref[mine] = (query_grad * INV_ROOT).astype(bf16)
    spread = run_matrix(SPAN, BLOCK, 1, True)
    sibling = split_product(spread, grad_s[SPAN : SPAN + BLOCK])

    @pl.when(pl.program_id(0) == 0)
    def _():
        own_ref[:SPAN] = grad_s[:SPAN]
        own_ref[SPAN:] = sibling
        far_s[...] = grad_s[SPAN + BLOCK :]

    @pl.when(pl.program_id(0) == 1)
    def _():
        own_ref[:SPAN] += sibling
        own_ref[SPAN:] += grad_s[:SPAN]
        g2_ref[...] = (far_s[:BLOCK] + grad_s[SPAN + BLOCK : SPAN + 2 * BLOCK]).astype(bf16)
        g3_ref[...] = (far_s[BLOCK:] + grad_s[SPAN + 2 * BLOCK :]).astype(bf16)


def attend_grads(entries, queries, d_attended, stats):
    part = pl.BlockSpec((SPAN, COLS), lambda i: (i, 0))
    coarse = pl.BlockSpec((BLOCK, 2 * COLS), lambda i: (0, 0))
    return pl.pallas_call(
        backward_kernel,
        grid=(2,),
        in_specs=entry_specs() + [part, part, pl.BlockSpec((8, SPAN), lambda i: (0, i))],
        out_specs=[
            pl.BlockSpec((COLS, SPAN), lambda i: (0, i)),
            pl.BlockSpec((ROWS, 2 * COLS), lambda i: (0, 0)),
            coarse,
            coarse,
        ],
        out_shape=[
            shape((COLS, ROWS)),
            shape((ROWS, 2 * COLS), f32),
            shape((BLOCK, 2 * COLS)),
            shape((BLOCK, 2 * COLS)),
        ],
        scratch_shapes=[
            pltpu.VMEM((2, KEYS, SPAN), f32),
            pltpu.VMEM((2, KEYS, SPAN), f32),
            pltpu.VMEM((COLS, KEYS), bf16),
            pltpu.VMEM((4, SPAN, 128), bf16),
            pltpu.VMEM((4, SPAN, 128), bf16),
            pltpu.VMEM((KEYS, 2 * COLS), f32),
            pltpu.VMEM((2 * BLOCK, 2 * COLS), f32),
        ],
        compiler_params=params(48),
        cost_estimate=cost(4 * 5 * 4 * ROWS * KEYS * 64, 8 * MIB),
        name="attend_grads",
    )(*entries, queries, d_attended, stats)


def ring_columns(step):
    first = step < 2
    return jnp.where(first, 2, 1), jnp.where(first, 3, 2), jnp.where(first, 1, 3)


def ring_specs():
    spec = pl.BlockSpec((BLOCK, COLS), lambda i, s: (i, 0))
    return [spec] * 4, [shape((ROWS, COLS))] * 4


def out_kernel(at_ref, ot_ref, w_ref, right_ref, left_ref, hold_ref, mine_ref):
    step = pl.program_id(0)
    here = at_ref[0]
    rows = ot_ref[...].T
    for offset, ref in zip(ring_columns(step) + (0,), (right_ref, left_ref, hold_ref, mine_ref)):
        start = pl.multiple_of(((here + offset) & 3) * COLS, COLS)
        ref[...] = dot_nn(rows, w_ref[:, pl.ds(start, COLS)]).astype(bf16)


def project_out(at, attended_t, w_out):
    out_specs, out_shape = ring_specs()
    return pl.pallas_call(
        out_kernel,
        grid_spec=pltpu.PrefetchScalarGridSpec(
            num_scalar_prefetch=1,
            grid=(4,),
            in_specs=[
                pl.BlockSpec((COLS, BLOCK), lambda i, s: (0, i)),
                pl.BlockSpec((COLS, WIDTH), lambda i, s: (0, 0)),
            ],
            out_specs=out_specs,
        ),
        out_shape=out_shape,
        compiler_params=params(24),
        cost_estimate=cost(ROWS * WIDTH * COLS, 4 * MIB),
        name="project_out",
    )(at, attended_t, w_out)


def input_kernel(
    at_ref, own_ref, got2_ref, got3a_ref, got3b_ref, qgt_ref, wq_ref, wk_ref, wv_ref,
    right_ref, left_ref, hold_ref, mine_ref, kvg_ref,
):
    step = pl.program_id(0)
    here = at_ref[0]
    spread4 = run_matrix(BLOCK, BLOCK >> 2, 2, True)
    spread8 = run_matrix(BLOCK, BLOCK >> 3, 3, True)
    total = own_ref[...] + dot_nn(spread4, got2_ref[...])
    total = total + (dot_nn(spread8, got3a_ref[...]) + dot_nn(spread8, got3b_ref[...]))
    kvg = total.astype(bf16)
    kvg_ref[...] = kvg
    query_grad = qgt_ref[...].T
    for offset, ref in zip(ring_columns(step) + (0,), (right_ref, left_ref, hold_ref, mine_ref)):
        start = pl.multiple_of(((here + offset) & 3) * COLS, COLS)
        cols = pl.ds(start, COLS)
        part = dot_nt(query_grad, wq_ref[cols, :])
        part = part + dot_nt(kvg[:, :COLS], wk_ref[cols, :])
        part = part + dot_nt(kvg[:, COLS:], wv_ref[cols, :])
        ref[...] = part.astype(bf16)


def project_input(at, own, got2, got3a, got3b, query_grad_t, w_query, w_key, w_value):
    out_specs, out_shape = ring_specs()
    whole = pl.BlockSpec((WIDTH, COLS), lambda i, s: (0, 0))
    return pl.pallas_call(
        input_kernel,
        grid_spec=pltpu.PrefetchScalarGridSpec(
            num_scalar_prefetch=1,
            grid=(4,),
            in_specs=[
                pl.BlockSpec((BLOCK, 2 * COLS), lambda i, s: (i, 0)),
                pl.BlockSpec((BLOCK >> 2, 2 * COLS), lambda i, s: (i, 0)),
                pl.BlockSpec((BLOCK >> 3, 2 * COLS), lambda i, s: (i, 0)),
                pl.BlockSpec((BLOCK >> 3, 2 * COLS), lambda i, s: (i, 0)),
                pl.BlockSpec((COLS, BLOCK), lambda i, s: (0, i)),
                whole,
                whole,
                whole,
            ],
            out_specs=out_specs + [pl.BlockSpec((BLOCK, 2 * COLS), lambda i, s: (i, 0))],
        ),
        out_shape=out_shape + [shape((ROWS, 2 * COLS))],
        compiler_params=params(32),
        cost_estimate=cost(3 * ROWS * WIDTH * COLS, 8 * MIB),
        name="project_input",
    )(at, own, got2, got3a, got3b, query_grad_t, w_query, w_key, w_value)


def shifted(value, axis, by):
    size = lax.axis_size(axis)
    return lax.ppermute(value, axis, [(i, (i + by) % size) for i in range(size)])


def swapped(value, bits):
    return lax.ppermute(value, "seq", [(i, i ^ bits) for i in range(lax.axis_size("seq"))])


def add(*terms):
    return sum(term.astype(f32) for term in terms).astype(bf16)


def head_sum(right, left, hold, mine):
    half = ROWS // 2
    got_right = shifted(right, "head", 1)
    got_left = shifted(left, "head", -1)
    more_right = shifted(add(hold[:half], got_right[:half]), "head", 1)
    more_left = shifted(add(hold[half:], got_left[half:]), "head", -1)
    return jnp.concatenate(
        [
            add(mine[:half], got_left[:half], more_right),
            add(mine[half:], got_right[half:], more_left),
        ],
        axis=0,
    )


def weight_kernel(at_ref, x_ref, c_ref, ot_ref, qgt_ref, kvg_ref, mine_ref, other_ref, g_s):
    core = at_ref[1]
    for index in range(4):
        if index == 0:
            grad_t = dot_nn(qgt_ref[...], x_ref[...])
        elif index < 3:
            cols = kvg_ref[:, (index - 1) * COLS : index * COLS]
            grad_t = dot_nn(cols.T, x_ref[...])
        else:
            grad_t = dot_nn(ot_ref[...], c_ref[...])
        g_s[...] = grad_t.astype(bf16).T.reshape(64, 16, COLS)
        rows = slice(index * 16, (index + 1) * 16)
        for block in range(32):
            mine_ref[block, rows] = g_s[2 * block + core]
            other_ref[block, rows] = g_s[2 * block + 1 - core]


def weight_grads(at, tokens, cotangent, attended_t, query_grad_t, kv_grad):
    vmem = pl.BlockSpec(memory_space=pltpu.VMEM)
    return pl.pallas_call(
        weight_kernel,
        in_specs=[pl.BlockSpec(memory_space=pltpu.SMEM)] + [vmem] * 5,
        out_specs=[vmem] * 2,
        out_shape=[shape((32, 64, COLS))] * 2,
        scratch_shapes=[pltpu.VMEM((64, 16, COLS), bf16)],
        compiler_params=params(40),
        cost_estimate=cost(4 * ROWS * WIDTH * COLS, 8 * MIB),
        name="weight_grads",
    )(at, tokens, cotangent, attended_t, query_grad_t, kv_grad)


def stage_kernel(at_ref, kept_ref, got_ref, *outs, picks):
    total_s = outs[-1]
    total_s[...] = (kept_ref[...].astype(f32) + got_ref[...].astype(f32)).astype(bf16)
    for pick, ref in zip(picks, outs[:-1]):
        for block, source in enumerate(pick(at_ref)):
            ref[block] = total_s[source]


def stage(at, kept, got, picks, counts, name):
    vmem = pl.BlockSpec(memory_space=pltpu.VMEM)
    rest = kept.shape[1:]
    return pl.pallas_call(
        functools.partial(stage_kernel, picks=picks),
        in_specs=[pl.BlockSpec(memory_space=pltpu.SMEM)] + [vmem] * 2,
        out_specs=[vmem] * len(counts),
        out_shape=[shape((count, *rest)) for count in counts],
        scratch_shapes=[pltpu.VMEM(kept.shape, bf16)],
        compiler_params=params(24),
        name=name,
    )(at, kept, got)


def x_blocks(offset, first, count):
    return lambda at: [((at[2] + offset) & 3) * 8 + first + block for block in range(count)]


def z_blocks(bit, count, flip):
    def pick(at):
        mine = (at[3] >> bit) & 1
        return [2 * block + (1 - mine if flip else mine) for block in range(count)]

    return pick


def seq_sum(at, mine, other):
    got = swapped(other, 1)
    far_a, far_b, ahead, behind, here = stage(
        at,
        mine,
        got,
        [x_blocks(2, 0, 4), x_blocks(2, 4, 4), x_blocks(1, 0, 8), x_blocks(3, 0, 8)]
        + [x_blocks(0, 0, 8)],
        [4, 4, 8, 8, 8],
        "sum_cores",
    )
    got_a = shifted(far_a, "seq", 16)
    got_b = shifted(far_b, "seq", -16)
    ahead = jnp.concatenate([add(ahead[:4], got_a), ahead[4:]], axis=0)
    behind = jnp.concatenate([behind[:4], add(behind[4:], got_b)], axis=0)
    got_a = shifted(ahead, "seq", 16)
    got_b = shifted(behind, "seq", -16)
    kept, got = here, got_a.astype(f32) + got_b.astype(f32)
    for bit, count in ((0, 4), (1, 2), (2, 1)):
        kept, away = stage(
            at,
            kept,
            got,
            [z_blocks(bit, count, False), z_blocks(bit, count, True)],
            [count, count],
            f"sum_z{bit}",
        )
        got = swapped(away, 2 << bit)
    return kept[0].astype(f32) + got[0].astype(f32)


def on_device(tokens, cotangent, w_query, w_key, w_value, w_out):
    place = lax.axis_index("seq")
    at = jnp.stack([lax.axis_index("head"), place % 2, place // 16, place // 2 % 8])
    at = at.astype(jnp.int32)
    key_value, own_2, own_4, own_8 = project_kv(tokens, w_key, w_value)
    level_two = swapped(own_4, 1)
    level_three_a = swapped(own_8, 2)
    level_three_b = swapped(own_8, 3)
    queries, d_attended = project_q(tokens, cotangent, w_query, w_out)
    entries = (key_value, own_2, level_two, level_three_a, level_three_b)
    attended_t, stats = attend(entries, queries)
    layer_out = head_sum(*project_out(at, attended_t, w_out))
    query_grad_t, own, grad_2, grad_3 = attend_grads(entries, queries, d_attended, stats)
    got_2 = swapped(grad_2, 1)
    got_3a = swapped(grad_3[: BLOCK // 2], 2)
    got_3b = swapped(grad_3[BLOCK // 2 :], 3)
    *parts, kv_grad = project_input(
        at, own, got_2, got_3a, got_3b, query_grad_t, w_query, w_key, w_value
    )
    grad_tokens = head_sum(*parts)
    mine, other = weight_grads(at, tokens, cotangent, attended_t, query_grad_t, kv_grad)
    scale = 1.0 / math.sqrt(lax.axis_size("seq") * tokens.shape[0])
    summed = seq_sum(at, mine, other) * scale
    return (
        layer_out,
        grad_tokens,
        summed[:16],
        summed[16:32],
        summed[32:48],
        summed[48:].T,
    )


def solution(mesh):
    return jax.shard_map(
        on_device,
        mesh=mesh,
        in_specs=(
            P("seq", None),
            P("seq", None),
            P(None, "head"),
            P(None, "head"),
            P(None, "head"),
            P("head", None),
        ),
        out_specs=(
            P("seq", "head"),
            P("seq", "head"),
            P("seq", "head"),
            P("seq", "head"),
            P("seq", "head"),
            P("head", "seq"),
        ),
        check_vma=False,
    )
```

time: 454 us -> 132 us (0.29); the launches traced: 446 us -> 131 us
  matrix products: 154 us -> 0 us
  waiting for transfers between devices: 189 us -> 37.4 us
  Pallas kernels: 0 us -> 45.3 us
  local copies, waits for them, and re-layouts: 49.3 us -> 10.7 us
  other arithmetic: 31.2 us -> 2.61 us
  starting transfers between devices: 5.34 us -> 33.9 us
  between operations: 17 us -> 0.87 us
    unnamed x4 -> x0, waiting for transfers between devices: 189 us -> none
    dot_general x22 -> x0, matrix products: 138 us -> none  [the longest x2 44.1 us: attention_grads(): jnp.einsum('hqk,khd->qhd', grad_scores, key_heads, preferred_element_type...]
    pallas_call x0 -> x11, Pallas kernels: none -> 45.3 us  [the longest x1 18.2 us: attend_grads(): pl.pallas_call(backward_kernel, grid=(2,), in_specs=entry_specs() + [part...]
    ppermute x6 -> x22, waiting for transfers between devices: 0.02 us -> 37.4 us  [the longest x12 19.9 us: shifted(): lax.ppermute(value, axis, [(i, (i + by) % size) for i in range(size)])]
    ppermute x6 -> x22, starting transfers between devices: 5.22 us -> 33.9 us  [the longest x10 17.3 us: swapped(): lax.ppermute(value, 'seq', [(i, i ^ bits) for i in range(lax.axis_size('s...]
    sub x2 -> x0, matrix products: 15.9 us -> none  [probabilities(): raised = jnp.exp(scores - row_max)]
    reshape x6 -> x0, local copies, waits for them, and re-layouts: 13.4 us -> none  [the longest x2 5.59 us: attention_grads(): grad_values.reshape(key_count, feature_width)]
    reduce_sum x4 -> x0, other arithmetic: 9.9 us -> none  [coarsen(): return (jnp.sum(grouped, axis=1) * (1.0 / factor)).astype(jnp.bfloat16)]
  transfers between devices with their start and end apart: 9 -> 22, of which waited for: 1 -> 12; matrix products, arithmetic and copies ran while one was open for 14% -> 3% of each run, Pallas kernels for 0% -> 4%
where the time goes in v1:
time: 132 us; the launch traced here: 131 us
  Pallas kernels  45.3 us (34%)
  waiting for transfers between devices  37.4 us (28%)
  starting transfers between devices  33.9 us (26%)
  local copies, waits for them, and re-layouts  10.7 us (8%)
  other arithmetic  2.61 us (2%)
    ppermute x12, waiting for transfers between devices, shifted(): lax.ppermute(value, axis, [(i, (i + by) % size) for i in range(size)])  19.9 us
    pallas_call x1, Pallas kernels, attend_grads(): pl.pallas_call(backward_kernel, grid=(2,), in_specs=entry_specs() + [part...  18.2 us
    ppermute x10, waiting for transfers between devices, swapped(): lax.ppermute(value, 'seq', [(i, i ^ bits) for i in range(lax.axis_size('s...  17.5 us
    ppermute x10, starting transfers between devices, swapped(): lax.ppermute(value, 'seq', [(i, i ^ bits) for i in range(lax.axis_size('s...  17.3 us
    ppermute x12, starting transfers between devices, shifted(): lax.ppermute(value, axis, [(i, (i + by) % size) for i in range(size)])  16.6 us
    pallas_call x1, Pallas kernels, attend(): pl.pallas_call(forward_kernel, grid=(2,), in_specs=entry_specs() + [pl.Bl...  9.51 us
    unnamed x28, local copies, waits for them, and re-layouts  9.31 us
    pallas_call x1, Pallas kernels, project_input(): pl.pallas_call(input_kernel, grid_spec=pltpu.PrefetchScalarGridSpec(num_s...  5.09 us
  transfers between devices with their start and end apart: 22, of which 12 were waited for; matrix products, arithmetic and copies ran while one was open for 3% of the time, Pallas kernels for 4%

profile of v1, /device:TPU:24, one launch (start us, length us, event | category | flops | bytes accessed | tf_op | source)
XLA Modules:
  0.0 130.7 jit_solution(13833876061162853246)
XLA Ops:
  4.3 2.6 %project_kv.1 = (bf16[1024,512]{1,0:T(8,128)(2,1)S(1)}, bf16[512,512]{1,0:T(8,128)(2,1)S(1)}, bf16[256,512]{1,0:T(8,128)(2,1)S(1)}, bf16[128,512]{1,0:T(8,128)(2,1)S(1)}) custom-call(bf16[1024,1024]{1,0:T(8,128)(2,1)S(1)} %copy-done, bf16[1024,256]{1,0:T(8,128)(2,1)S(1)} %copy-done.5, bf16[1024,256]{1,0:T(8,128)(2,1)S(1)} %copy-done.7), custom_call_target="tpu_custom_call" | custom-call | flops 1073741824 | bytes 6291456 | tf_op jit(solution)/shard_map/project_kv/pallas_call | solution.py:65
  7.0 2.0 %collective-permute-start.2 = (bf16[128,512]{1,0:T(8,128)(2,1)S(1)}, bf16[128,512]{1,0:T(8,128)(2,1)S(1)}, u32[]{:S(2)}, u32[]{:S(2)}) collective-permute-start(bf16[128,512]{1,0:T(8,128)(2,1)S(1)} %get-tuple-element.43), channel_id=1, source_target_pairs={{0,12},{4,8},{8,4},{12,0},{16,28},{20,24},{24,20},{28,16},{32,44},... | collective-permute-start | bytes 393224 | tf_op jit(solution)/shard_map/ppermute | solution.py:390
  11.0 1.9 %collective-permute-done.2.refs_4_ = bf16[128,512]{1,0:T(8,128)(2,1)S(1)} collective-permute-done((bf16[128,512]{1,0:T(8,128)(2,1)S(1)}, bf16[128,512]{1,0:T(8,128)(2,1)S(1)}, u32[]{:S(2)}, u32[]{:S(2)}) %collective-permute-start.2) | collective-permute-done | bytes 131104 | tf_op jit(solution)/shard_map/ppermute | solution.py:390
  12.9 3.0 %collective-permute-done.1.refs_3_ = bf16[128,512]{1,0:T(8,128)(2,1)S(1)} collective-permute-done((bf16[128,512]{1,0:T(8,128)(2,1)S(1)}, bf16[128,512]{1,0:T(8,128)(2,1)S(1)}, u32[]{:S(2)}, u32[]{:S(2)}) %collective-permute-start.1) | collective-permute-done | bytes 131104 | tf_op jit(solution)/shard_map/ppermute | solution.py:390
  15.9 9.5 %attend.1 = (bf16[256,1024]{1,0:T(8,128)(2,1)S(1)}, f32[8,1024]{1,0:T(8,128)S(1)}) custom-call(bf16[1024,512]{1,0:T(8,128)(2,1)S(1)} %get-tuple-element.40.refs_0_, bf16[512,512]{1,0:T(8,128)(2,1)S(1)} %get-tuple-element.41.refs_1_, bf16[256,512]{1,0:T(8,128)(2,1)S(1)} %collective-permute-done.refs_2_, bf16[128,512]{1,0:T(8,128)(2,1)S(1)} %collective-permute-done.1.refs_3_, ...), custom_call_target="tpu_custom_call" | custom-call | flops 5368709120 | bytes 4194304 | tf_op jit(solution)/shard_map/attend/pallas_call | solution.py:175
  26.2 18.2 %attend_grads.1 = (bf16[256,1024]{1,0:T(8,128)(2,1)S(1)}, f32[1024,512]{1,0:T(8,128)}, bf16[256,512]{1,0:T(8,128)(2,1)S(1)}, bf16[256,512]{1,0:T(8,128)(2,1)S(1)}) custom-call(bf16[1024,512]{1,0:T(8,128)(2,1)S(1)} %get-tuple-element.40.refs_0_, bf16[512,512]{1,0:T(8,128)(2,1)S(1)} %get-tuple-element.41.refs_1_, ...), custom_call_target="tpu_custom_call" | custom-call | flops 13421772800 | bytes 8388608 | tf_op jit(solution)/shard_map/attend_grads/pallas_call | solution.py:265
  47.3 3.8 %collective-permute-done.9.got3b_ref = bf16[128,512]{1,0:T(8,128)(2,1)S(1)} collective-permute-done((bf16[128,512]{1,0:T(8,128)(2,1)}, bf16[128,512]{1,0:T(8,128)(2,1)S(1)}, u32[]{:S(2)}, u32[]{:S(2)}) %collective-permute-start.9) | collective-permute-done | bytes 131104 | tf_op jit(solution)/shard_map/ppermute | solution.py:390
  51.1 3.1 %collective-permute-done.8.got3a_ref = bf16[128,512]{1,0:T(8,128)(2,1)} collective-permute-done((bf16[128,512]{1,0:T(8,128)(2,1)}, bf16[128,512]{1,0:T(8,128)(2,1)}, u32[]{:S(2)}, u32[]{:S(2)}) %collective-permute-start.8) | collective-permute-done | bytes 131104 | tf_op jit(solution)/shard_map/ppermute | solution.py:390
  58.9 5.1 %project_input.1 = (bf16[1024,256]{1,0:T(8,128)(2,1)S(1)}, bf16[1024,256]{1,0:T(8,128)(2,1)S(1)}, bf16[1024,256]{1,0:T(8,128)(2,1)S(1)}, bf16[1024,256]{1,0:T(8,128)(2,1)S(1)}, bf16[1024,512]{1,0:T(8,128)(2,1)S(1)}) custom-call(s32[4]{0:T(128)S(1)} %pad_add_fusion.at_ref, f32[1024,512]{1,0:T(8,128)S(1)} %copy-done.9, ...), custom_call_target="tpu_custom_call" | custom-call | flops 1610612736 | bytes 8388608 | tf_op jit(solution)/shard_map/project_input/pallas_call | solution.py:360
  64.1 3.1 %weight_grads.1 = (bf16[32,64,256]{2,1,0:T(8,128)(2,1)S(1)}, bf16[32,64,256]{2,1,0:T(8,128)(2,1)S(1)}) custom-call(s32[4]{0:T(128)S(1)} %pad_add_fusion.at_ref, bf16[1024,1024]{1,0:T(8,128)(2,1)S(1)} %copy-done.1, bf16[1024,1024]{1,0:T(8,128)(2,1)S(1)} %copy-done.2, bf16[256,1024]{1,0:T(8,128)(2,1)S(1)} %copy-done.11, bf16[256,1024]{1,0:T(8,128)(2,1)S(1)} %copy-done.13, ...), custom_call_target="tpu_custom_call" | custom-call | flops 2147483648 | bytes 8388608 | tf_op jit(solution)/shard_map/weight_grads/pallas_call | solution.py:431
  67.3 2.6 %collective-permute-done.14.got_ref = bf16[32,64,256]{2,1,0:T(8,128)(2,1)S(1)} collective-permute-done((bf16[32,64,256]{2,1,0:T(8,128)(2,1)S(1)}, bf16[32,64,256]{2,1,0:T(8,128)(2,1)S(1)}, u32[]{:S(2)}, u32[]{:S(2)}) %collective-permute-start.14) | collective-permute-done | bytes 1048608 | tf_op jit(solution)/shard_map/ppermute | solution.py:390
  71.1 2.8 %collective-permute-start.17 = (bf16[4,64,256]{2,1,0:T(8,128)(2,1)S(1)}, bf16[4,64,256]{2,1,0:T(8,128)(2,1)S(1)}, u32[]{:S(2)}, u32[]{:S(2)}) collective-permute-start(bf16[4,64,256]{2,1,0:T(8,128)(2,1)S(1)} %get-tuple-element.67), channel_id=1, source_target_pairs={{0,192},{4,196},{8,200},{12,204},{16,208},{20,212},{24,216},{28,22... | collective-permute-start | bytes 393224 | tf_op jit(solution)/shard_map/ppermute | solution.py:386
  74.0 2.0 %project_out.1 = (bf16[1024,256]{1,0:T(8,128)(2,1)S(1)}, bf16[1024,256]{1,0:T(8,128)(2,1)S(1)}, bf16[1024,256]{1,0:T(8,128)(2,1)S(1)}, bf16[1024,256]{1,0:T(8,128)(2,1)S(1)}) custom-call(s32[4]{0:T(128)S(1)} %pad_add_fusion.at_ref, bf16[256,1024]{1,0:T(8,128)(2,1)S(1)} %copy-done.11, bf16[256,1024]{1,0:T(8,128)(2,1)S(1)} %copy-done.4), custom_call_target="tpu_custom_call" | custom-call | flops 536870912 | bytes 4194304 | tf_op jit(solution)/shard_map/project_out/pallas_call | solution.py:317
  76.8 2.5 %collective-permute-start.4 = (bf16[1024,256]{1,0:T(8,128)(2,1)S(1)}, bf16[1024,256]{1,0:T(8,128)(2,1)S(1)}, u32[]{:S(2)}, u32[]{:S(2)}) collective-permute-start(bf16[1024,256]{1,0:T(8,128)(2,1)S(1)} %get-tuple-element.49), channel_id=1, source_target_pairs={{0,1},{1,2},{2,3},{3,0},{4,5},{5,6},{6,7},{7,4},{8,9},{9,10},{10,1... | collective-permute-start | bytes 1572872 | tf_op jit(solution)/shard_map/ppermute | solution.py:386
  79.2 3.2 %collective-permute-start.11 = (bf16[1024,256]{1,0:T(8,128)(2,1)S(1)}, bf16[1024,256]{1,0:T(8,128)(2,1)S(1)}, u32[]{:S(2)}, u32[]{:S(2)}) collective-permute-start(bf16[1024,256]{1,0:T(8,128)(2,1)S(1)} %get-tuple-element.59), channel_id=1, source_target_pairs={{0,1},{1,2},{2,3},{3,0},{4,5},{5,6},{6,7},{7,4},{8,9},{9,10},{10,1... | collective-permute-start | bytes 1572872 | tf_op jit(solution)/shard_map/ppermute | solution.py:386
  82.7 6.1 %collective-permute-done.15 = bf16[4,64,256]{2,1,0:T(8,128)(2,1)S(1)} collective-permute-done((bf16[4,64,256]{2,1,0:T(8,128)(2,1)S(1)}, bf16[4,64,256]{2,1,0:T(8,128)(2,1)S(1)}, u32[]{:S(2)}, u32[]{:S(2)}) %collective-permute-start.15) | collective-permute-done | bytes 131104 | tf_op jit(solution)/shard_map/ppermute | solution.py:386
  88.9 3.2 %collective-permute-done.3 = bf16[1024,256]{1,0:T(8,128)(2,1)S(1)} collective-permute-done((bf16[1024,256]{1,0:T(8,128)(2,1)S(1)}, bf16[1024,256]{1,0:T(8,128)(2,1)S(1)}, u32[]{:S(2)}, u32[]{:S(2)}) %collective-permute-start.3) | collective-permute-done | bytes 524320 | tf_op jit(solution)/shard_map/ppermute | solution.py:386
  92.2 3.4 %collective-permute-start.5 = (bf16[512,256]{1,0:T(8,128)(2,1)S(1)}, bf16[512,256]{1,0:T(8,128)(2,1)S(1)}, u32[]{:S(2)}, u32[]{:S(2)}) collective-permute-start(bf16[512,256]{1,0:T(8,128)(2,1)S(1)} %get-tuple-element.80), channel_id=1, source_target_pairs={{0,1},{1,2},{2,3},{3,0},{4,5},{5,6},{6,7},{7,4},{8,9},{9,10},{10,1... | collective-permute-start | bytes 786440 | tf_op jit(solution)/shard_map/ppermute | solution.py:386
  95.5 6.6 %collective-permute-done.10 = bf16[1024,256]{1,0:T(8,128)(2,1)S(1)} collective-permute-done((bf16[1024,256]{1,0:T(8,128)(2,1)S(1)}, bf16[1024,256]{1,0:T(8,128)(2,1)S(1)}, u32[]{:S(2)}, u32[]{:S(2)}) %collective-permute-start.10) | collective-permute-done | bytes 524320 | tf_op jit(solution)/shard_map/ppermute | solution.py:386
  103.0 3.8 %collective-permute-start.12 = (bf16[512,256]{1,0:T(8,128)(2,1)S(1)}, bf16[512,256]{1,0:T(8,128)(2,1)S(1)}, u32[]{:S(2)}, u32[]{:S(2)}) collective-permute-start(bf16[512,256]{1,0:T(8,128)(2,1)S(1)} %get-tuple-element.76), channel_id=1, source_target_pairs={{0,1},{1,2},{2,3},{3,0},{4,5},{5,6},{6,7},{7,4},{8,9},{9,10},{10,1... | collective-permute-start | bytes 786440 | tf_op jit(solution)/shard_map/ppermute | solution.py:386
  109.3 3.3 %collective-permute-done.6 = bf16[512,256]{1,0:T(8,128)(2,1)S(1)} collective-permute-done((bf16[512,256]{1,0:T(8,128)(2,1)S(1)}, bf16[512,256]{1,0:T(8,128)(2,1)S(1)}, u32[]{:S(2)}, u32[]{:S(2)}) %collective-permute-start.6) | collective-permute-done | bytes 262176 | tf_op jit(solution)/shard_map/ppermute | solution.py:386
  114.2 3.4 %collective-permute-start.20 = (bf16[2,64,256]{2,1,0:T(8,128)(2,1)S(1)}, bf16[2,64,256]{2,1,0:T(8,128)(2,1)S(1)}, u32[]{:S(2)}, u32[]{:S(2)}) collective-permute-start(bf16[2,64,256]{2,1,0:T(8,128)(2,1)S(1)} %get-tuple-element.71), channel_id=1, source_target_pairs={{0,16},{4,20},{8,24},{12,28},{16,0},{20,4},{24,8},{28,12},{32,48},... | collective-permute-start | bytes 196616 | tf_op jit(solution)/shard_map/ppermute | solution.py:390
  117.8 2.0 %collective-permute-done.20.got_ref = bf16[2,64,256]{2,1,0:T(8,128)(2,1)S(1)} collective-permute-done((bf16[2,64,256]{2,1,0:T(8,128)(2,1)S(1)}, bf16[2,64,256]{2,1,0:T(8,128)(2,1)S(1)}, u32[]{:S(2)}, u32[]{:S(2)}) %collective-permute-start.20) | collective-permute-done | bytes 65568 | tf_op jit(solution)/shard_map/ppermute | solution.py:390
  120.4 7.8 %collective-permute-start.21 = (bf16[1,64,256]{2,1,0:T(8,128)(2,1)S(1)}, bf16[1,64,256]{2,1,0:T(8,128)(2,1)S(1)}, u32[]{:S(2)}, u32[]{:S(2)}) collective-permute-start(bf16[1,64,256]{2,1,0:T(8,128)(2,1)S(1)} %get-tuple-element.73), channel_id=1, source_target_pairs={{0,32},{4,36},{8,40},{12,44},{16,48},{20,52},{24,56},{28,60},{32,0... | collective-permute-start | bytes 98312 | tf_op jit(solution)/shard_map/ppermute | solution.py:390
  (76 shorter events, 24.9 us)
Async XLA Ops:
  6.9 9.0 %collective-permute-start = (bf16[256,512]{1,0:T(8,128)(2,1)S(1)}, bf16[256,512]{1,0:T(8,128)(2,1)S(1)}, u32[]{:S(2)}, u32[]{:S(2)}) collective-permute-start(bf16[256,512]{1,0:T(8,128)(2,1)S(1)} %get-tuple-element.42), channel_id=1, source_target_pairs={{0,4},{4,0},{8,12},{12,8},{16,20},{20,16},{24,28},{28,24},{32,36},... | collective-permute-start | bytes 786440 | tf_op jit(solution)/shard_map/ppermute | solution.py:390
  7.0 5.9 %collective-permute-start.2 = (bf16[128,512]{1,0:T(8,128)(2,1)S(1)}, bf16[128,512]{1,0:T(8,128)(2,1)S(1)}, u32[]{:S(2)}, u32[]{:S(2)}) collective-permute-start(bf16[128,512]{1,0:T(8,128)(2,1)S(1)} %get-tuple-element.43), channel_id=1, source_target_pairs={{0,12},{4,8},{8,4},{12,0},{16,28},{20,24},{24,20},{28,16},{32,44},... | collective-permute-start | bytes 393224 | tf_op jit(solution)/shard_map/ppermute | solution.py:390
  9.1 6.8 %collective-permute-start.1 = (bf16[128,512]{1,0:T(8,128)(2,1)S(1)}, bf16[128,512]{1,0:T(8,128)(2,1)S(1)}, u32[]{:S(2)}, u32[]{:S(2)}) collective-permute-start(bf16[128,512]{1,0:T(8,128)(2,1)S(1)} %get-tuple-element.43), channel_id=1, source_target_pairs={{0,8},{4,12},{8,0},{12,4},{16,24},{20,28},{24,16},{28,20},{32,40},... | collective-permute-start | bytes 393224 | tf_op jit(solution)/shard_map/ppermute | solution.py:390
  44.4 9.8 %collective-permute-start.7 = (bf16[256,512]{1,0:T(8,128)(2,1)S(1)}, bf16[256,512]{1,0:T(8,128)(2,1)}, u32[]{:S(2)}, u32[]{:S(2)}) collective-permute-start(bf16[256,512]{1,0:T(8,128)(2,1)S(1)} %get-tuple-element.53), channel_id=1, source_target_pairs={{0,4},{4,0},{8,12},{12,8},{16,20},{20,16},{24,28},{28,24},{32,36},... | collective-permute-start | bytes 786440 | tf_op jit(solution)/shard_map/ppermute | solution.py:390
  45.3 5.8 %collective-permute-start.9 = (bf16[128,512]{1,0:T(8,128)(2,1)}, bf16[128,512]{1,0:T(8,128)(2,1)S(1)}, u32[]{:S(2)}, u32[]{:S(2)}) collective-permute-start(bf16[128,512]{1,0:T(8,128)(2,1)} %get-tuple-element.82), channel_id=1, source_target_pairs={{0,12},{4,8},{8,4},{12,0},{16,28},{20,24},{24,20},{28,16},{32,44},... | collective-permute-start | bytes 393224 | tf_op jit(solution)/shard_map/ppermute | solution.py:390
  47.0 7.2 %collective-permute-start.8 = (bf16[128,512]{1,0:T(8,128)(2,1)}, bf16[128,512]{1,0:T(8,128)(2,1)}, u32[]{:S(2)}, u32[]{:S(2)}) collective-permute-start(bf16[128,512]{1,0:T(8,128)(2,1)} %get-tuple-element.83), channel_id=1, source_target_pairs={{0,8},{4,12},{8,0},{12,4},{16,24},{20,28},{24,16},{28,20},{32,40},... | collective-permute-start | bytes 393224 | tf_op jit(solution)/shard_map/ppermute | solution.py:390
  58.9 5.1 %copy-start.1 = (bf16[1024,1024]{1,0:T(8,128)(2,1)S(1)}, bf16[1024,1024]{1,0:T(8,128)(2,1)}, u32[]{:S(2)}) copy-start(bf16[1024,1024]{1,0:T(8,128)(2,1)} %x_ref.5) | copy-start | bytes 6291460
  58.9 5.1 %copy-start.11 = (bf16[256,1024]{1,0:T(8,128)(2,1)S(1)}, bf16[256,1024]{1,0:T(8,128)(2,1)}, u32[]{:S(2)}) copy-start(bf16[256,1024]{1,0:T(8,128)(2,1)} %copy-done.10) | copy-start | bytes 1572868
  67.2 2.7 %collective-permute-start.14 = (bf16[32,64,256]{2,1,0:T(8,128)(2,1)S(1)}, bf16[32,64,256]{2,1,0:T(8,128)(2,1)S(1)}, u32[]{:S(2)}, u32[]{:S(2)}) collective-permute-start(bf16[32,64,256]{2,1,0:T(8,128)(2,1)S(1)} %get-tuple-element.62), channel_id=1, source_target_pairs={{0,4},{4,0},{8,12},{12,8},{16,20},{20,16},{24,28},{28,24},{32,36},... | collective-permute-start | bytes 3145736 | tf_op jit(solution)/shard_map/ppermute | solution.py:390
  71.1 11.4 %collective-permute-start.17 = (bf16[4,64,256]{2,1,0:T(8,128)(2,1)S(1)}, bf16[4,64,256]{2,1,0:T(8,128)(2,1)S(1)}, u32[]{:S(2)}, u32[]{:S(2)}) collective-permute-start(bf16[4,64,256]{2,1,0:T(8,128)(2,1)S(1)} %get-tuple-element.67), channel_id=1, source_target_pairs={{0,192},{4,196},{8,200},{12,204},{16,208},{20,212},{24,216},{28,22... | collective-permute-start | bytes 393224 | tf_op jit(solution)/shard_map/ppermute | solution.py:386
  75.9 16.1 %collective-permute-start.3 = (bf16[1024,256]{1,0:T(8,128)(2,1)S(1)}, bf16[1024,256]{1,0:T(8,128)(2,1)S(1)}, u32[]{:S(2)}, u32[]{:S(2)}) collective-permute-start(bf16[1024,256]{1,0:T(8,128)(2,1)S(1)} %get-tuple-element.47), channel_id=1, source_target_pairs={{0,3},{1,0},{2,1},{3,2},{4,7},{5,4},{6,5},{7,6},{8,11},{9,8},{10,9... | collective-permute-start | bytes 1572872 | tf_op jit(solution)/shard_map/ppermute | solution.py:386
  76.8 15.3 %collective-permute-start.4 = (bf16[1024,256]{1,0:T(8,128)(2,1)S(1)}, bf16[1024,256]{1,0:T(8,128)(2,1)S(1)}, u32[]{:S(2)}, u32[]{:S(2)}) collective-permute-start(bf16[1024,256]{1,0:T(8,128)(2,1)S(1)} %get-tuple-element.49), channel_id=1, source_target_pairs={{0,1},{1,2},{2,3},{3,0},{4,5},{5,6},{6,7},{7,4},{8,9},{9,10},{10,1... | collective-permute-start | bytes 1572872 | tf_op jit(solution)/shard_map/ppermute | solution.py:386
  79.2 22.9 %collective-permute-start.10 = (bf16[1024,256]{1,0:T(8,128)(2,1)S(1)}, bf16[1024,256]{1,0:T(8,128)(2,1)S(1)}, u32[]{:S(2)}, u32[]{:S(2)}) collective-permute-start(bf16[1024,256]{1,0:T(8,128)(2,1)S(1)} %get-tuple-element.57), channel_id=1, source_target_pairs={{0,3},{1,0},{2,1},{3,2},{4,7},{5,4},{6,5},{7,6},{8,11},{9,8},{10,9... | collective-permute-start | bytes 1572872 | tf_op jit(solution)/shard_map/ppermute | solution.py:386
  79.2 23.6 %collective-permute-start.11 = (bf16[1024,256]{1,0:T(8,128)(2,1)S(1)}, bf16[1024,256]{1,0:T(8,128)(2,1)S(1)}, u32[]{:S(2)}, u32[]{:S(2)}) collective-permute-start(bf16[1024,256]{1,0:T(8,128)(2,1)S(1)} %get-tuple-element.59), channel_id=1, source_target_pairs={{0,1},{1,2},{2,3},{3,0},{4,5},{5,6},{6,7},{7,4},{8,9},{9,10},{10,1... | collective-permute-start | bytes 1572872 | tf_op jit(solution)/shard_map/ppermute | solution.py:386
  82.5 6.3 %collective-permute-start.15 = (bf16[4,64,256]{2,1,0:T(8,128)(2,1)S(1)}, bf16[4,64,256]{2,1,0:T(8,128)(2,1)S(1)}, u32[]{:S(2)}, u32[]{:S(2)}) collective-permute-start(bf16[4,64,256]{2,1,0:T(8,128)(2,1)S(1)} %get-tuple-element.65), channel_id=1, source_target_pairs={{0,64},{4,68},{8,72},{12,76},{16,80},{20,84},{24,88},{28,92},{32,9... | collective-permute-start | bytes 393224 | tf_op jit(solution)/shard_map/ppermute | solution.py:386
  88.8 18.0 %collective-permute-start.18 = (bf16[8,64,256]{2,1,0:T(8,128)(2,1)S(1)}, bf16[8,64,256]{2,1,0:T(8,128)(2,1)S(1)}, u32[]{:S(2)}, u32[]{:S(2)}) collective-permute-start(bf16[8,64,256]{2,1,0:T(8,128)(2,1)S(1)} %pad_maximum_fusion.3), channel_id=1, source_target_pairs={{0,192},{4,196},{8,200},{12,204},{16,208},{20,212},{24,216},{28,22... | collective-permute-start | bytes 786440 | tf_op jit(solution)/shard_map/ppermute | solution.py:386
  92.0 14.7 %collective-permute-start.16 = (bf16[8,64,256]{2,1,0:T(8,128)(2,1)S(1)}, bf16[8,64,256]{2,1,0:T(8,128)(2,1)S(1)}, u32[]{:S(2)}, u32[]{:S(2)}) collective-permute-start(bf16[8,64,256]{2,1,0:T(8,128)(2,1)S(1)} %pad_maximum_fusion.2), channel_id=1, source_target_pairs={{0,64},{4,68},{8,72},{12,76},{16,80},{20,84},{24,88},{28,92},{32,9... | collective-permute-start | bytes 786440 | tf_op jit(solution)/shard_map/ppermute | solution.py:386
  92.2 17.1 %collective-permute-start.5 = (bf16[512,256]{1,0:T(8,128)(2,1)S(1)}, bf16[512,256]{1,0:T(8,128)(2,1)S(1)}, u32[]{:S(2)}, u32[]{:S(2)}) collective-permute-start(bf16[512,256]{1,0:T(8,128)(2,1)S(1)} %get-tuple-element.80), channel_id=1, source_target_pairs={{0,1},{1,2},{2,3},{3,0},{4,5},{5,6},{6,7},{7,4},{8,9},{9,10},{10,1... | collective-permute-start | bytes 786440 | tf_op jit(solution)/shard_map/ppermute | solution.py:386
  102.1 10.5 %collective-permute-start.6 = (bf16[512,256]{1,0:T(8,128)(2,1)S(1)}, bf16[512,256]{1,0:T(8,128)(2,1)S(1)}, u32[]{:S(2)}, u32[]{:S(2)}) collective-permute-start(bf16[512,256]{1,0:T(8,128)(2,1)S(1)} %get-tuple-element.81), channel_id=1, source_target_pairs={{0,3},{1,0},{2,1},{3,2},{4,7},{5,4},{6,5},{7,6},{8,11},{9,8},{10,9... | collective-permute-start | bytes 786440 | tf_op jit(solution)/shard_map/ppermute | solution.py:386
  103.0 14.6 %collective-permute-start.12 = (bf16[512,256]{1,0:T(8,128)(2,1)S(1)}, bf16[512,256]{1,0:T(8,128)(2,1)S(1)}, u32[]{:S(2)}, u32[]{:S(2)}) collective-permute-start(bf16[512,256]{1,0:T(8,128)(2,1)S(1)} %get-tuple-element.76), channel_id=1, source_target_pairs={{0,1},{1,2},{2,3},{3,0},{4,5},{5,6},{6,7},{7,4},{8,9},{9,10},{10,1... | collective-permute-start | bytes 786440 | tf_op jit(solution)/shard_map/ppermute | solution.py:386
  106.8 10.8 %collective-permute-start.13 = (bf16[512,256]{1,0:T(8,128)(2,1)S(1)}, bf16[512,256]{1,0:T(8,128)(2,1)S(1)}, u32[]{:S(2)}, u32[]{:S(2)}) collective-permute-start(bf16[512,256]{1,0:T(8,128)(2,1)S(1)} %get-tuple-element.77), channel_id=1, source_target_pairs={{0,3},{1,0},{2,1},{3,2},{4,7},{5,4},{6,5},{7,6},{8,11},{9,8},{10,9... | collective-permute-start | bytes 786440 | tf_op jit(solution)/shard_map/ppermute | solution.py:386
  107.5 6.1 %collective-permute-start.19 = (bf16[4,64,256]{2,1,0:T(8,128)(2,1)S(1)}, bf16[4,64,256]{2,1,0:T(8,128)(2,1)S(1)}, u32[]{:S(2)}, u32[]{:S(2)}) collective-permute-start(bf16[4,64,256]{2,1,0:T(8,128)(2,1)S(1)} %get-tuple-element.69), channel_id=1, source_target_pairs={{0,8},{4,12},{8,0},{12,4},{16,24},{20,28},{24,16},{28,20},{32,40},... | collective-permute-start | bytes 393224 | tf_op jit(solution)/shard_map/ppermute | solution.py:390
  114.2 5.6 %collective-permute-start.20 = (bf16[2,64,256]{2,1,0:T(8,128)(2,1)S(1)}, bf16[2,64,256]{2,1,0:T(8,128)(2,1)S(1)}, u32[]{:S(2)}, u32[]{:S(2)}) collective-permute-start(bf16[2,64,256]{2,1,0:T(8,128)(2,1)S(1)} %get-tuple-element.71), channel_id=1, source_target_pairs={{0,16},{4,20},{8,24},{12,28},{16,0},{20,4},{24,8},{28,12},{32,48},... | collective-permute-start | bytes 196616 | tf_op jit(solution)/shard_map/ppermute | solution.py:390
  120.4 9.7 %collective-permute-start.21 = (bf16[1,64,256]{2,1,0:T(8,128)(2,1)S(1)}, bf16[1,64,256]{2,1,0:T(8,128)(2,1)S(1)}, u32[]{:S(2)}, u32[]{:S(2)}) collective-permute-start(bf16[1,64,256]{2,1,0:T(8,128)(2,1)S(1)} %get-tuple-element.73), channel_id=1, source_target_pairs={{0,32},{4,36},{8,40},{12,44},{16,48},{20,52},{24,56},{28,60},{32,0... | collective-permute-start | bytes 98312 | tf_op jit(solution)/shard_map/ppermute | solution.py:390
  (12 other events, 24.6 us)

commit v2 on v1

v2 whole, which is shorter than its diff:
```python
import functools
import math

import jax
import jax.numpy as jnp
from jax import lax
from jax.experimental import pallas as pl
from jax.experimental.pallas import tpu as pltpu
from jax.sharding import PartitionSpec as P

HEAD_DIM = 64
BLOCK = 256
SPAN = 2 * BLOCK
KEYS = 5 * BLOCK
ROWS = 4 * BLOCK
WIDTH = 1024
COLS = 256
MIB = 1024 * 1024
OFFSETS = (0.0, 0.0, 1.0, 2.0, 3.0)
SCORE_SCALE = 1.0 / (math.log(2.0) * math.sqrt(HEAD_DIM))
INV_ROOT = 1.0 / math.sqrt(HEAD_DIM)
bf16 = jnp.bfloat16
f32 = jnp.float32


def dot_nn(a, b):
    return lax.dot_general(a, b, (((1,), (0,)), ((), ())), preferred_element_type=f32)


def dot_nt(a, b):
    return lax.dot_general(a, b, (((1,), (1,)), ((), ())), preferred_element_type=f32)


def params(mib):
    return pltpu.CompilerParams(vmem_limit_bytes=mib * MIB)


def shape(dims, dtype=bf16):
    return jax.ShapeDtypeStruct(dims, dtype)


def cost(macs, nbytes):
    return pl.CostEstimate(flops=2 * macs, bytes_accessed=nbytes, transcendentals=0)


def run_matrix(rows, cols, shift, expand):
    i = lax.broadcasted_iota(jnp.int32, (rows, cols), 0)
    j = lax.broadcasted_iota(jnp.int32, (rows, cols), 1)
    inside = (i >> shift) == j if expand else i == (j >> shift)
    return jnp.where(inside, 2.0**-shift, 0.0).astype(bf16)


class Copies:
    def __init__(self, sems):
        self.sems = sems
        self.count = 0

    def start(self, source, target):
        copy = pltpu.make_async_copy(source, target, self.sems.at[self.count])
        self.count += 1
        copy.start()
        return copy


def row_block(ref, index, count):
    return ref.at[pl.ds(index * count, count)]


def any_spec():
    return pl.BlockSpec(memory_space=pl.ANY)


def kv_kernel(
    x_hbm, wk_hbm, wv_hbm, kv_hbm, c2_hbm, c4_hbm, c8_hbm,
    x_s, wk_s, wv_s, kv_s, c2_s, c4_s, c8_s, in_sems, out_sems,
):
    fetch, store = Copies(in_sems), Copies(out_sems)
    wk = [fetch.start(row_block(wk_hbm, i, SPAN), row_block(wk_s, i, SPAN)) for i in range(2)]
    x = [fetch.start(row_block(x_hbm, i, BLOCK), row_block(x_s, i, BLOCK)) for i in range(2)]
    wv = [fetch.start(row_block(wv_hbm, i, SPAN), row_block(wv_s, i, SPAN)) for i in range(2)]
    x += [fetch.start(row_block(x_hbm, i, BLOCK), row_block(x_s, i, BLOCK)) for i in (2, 3)]
    averages = [run_matrix(BLOCK >> shift, BLOCK, shift, False) for shift in range(4)]
    stores = []
    for half in range(2):
        if half == 0:
            for copy in wk:
                copy.wait()
        for copy in x[2 * half : 2 * half + 2]:
            copy.wait()
        rows = slice(half * SPAN, (half + 1) * SPAN)
        kv_s[rows, :COLS] = dot_nn(x_s[rows], wk_s[...]).astype(bf16)
        if half == 0:
            for copy in wv:
                copy.wait()
        kv_s[rows, COLS:] = dot_nn(x_s[rows], wv_s[...]).astype(bf16)
        for shift, ref, out in ((3, c8_s, c8_hbm), (2, c4_s, c4_hbm), (1, c2_s, c2_hbm)):
            count = BLOCK >> shift
            for index in (2 * half, 2 * half + 1):
                kv = kv_s[index * BLOCK : (index + 1) * BLOCK]
                mean = dot_nn(averages[shift], kv).astype(bf16)
                ref[index * count : (index + 1) * count] = mean
            stores.append(
                store.start(row_block(ref, half, 2 * count), row_block(out, half, 2 * count))
            )
        stores.append(store.start(row_block(kv_s, half, SPAN), row_block(kv_hbm, half, SPAN)))
    for copy in stores:
        copy.wait()


def project_kv(tokens, w_key, w_value):
    outs = [(ROWS >> s, 2 * COLS) for s in range(4)]
    return pl.pallas_call(
        kv_kernel,
        in_specs=[any_spec()] * 3,
        out_specs=[any_spec()] * 4,
        out_shape=[shape(dims) for dims in outs],
        scratch_shapes=[
            pltpu.VMEM((ROWS, WIDTH), bf16),
            pltpu.VMEM((WIDTH, COLS), bf16),
            pltpu.VMEM((WIDTH, COLS), bf16),
        ]
        + [pltpu.VMEM(dims, bf16) for dims in outs]
        + [pltpu.SemaphoreType.DMA((8,)), pltpu.SemaphoreType.DMA((8,))],
        compiler_params=params(60),
        cost_estimate=cost(ROWS * WIDTH * 2 * COLS, 6 * MIB),
        name="project_kv",
    )(tokens, w_key, w_value)


def q_kernel(
    x_hbm, c_hbm, wq_hbm, wo_hbm, q_hbm, da_hbm,
    x_s, c_s, wq_s, wo_s, q_s, da_s, in_sems, out_sems,
):
    fetch, store = Copies(in_sems), Copies(out_sems)
    wq = [fetch.start(row_block(wq_hbm, i, SPAN), row_block(wq_s, i, SPAN)) for i in range(2)]
    x = [fetch.start(row_block(x_hbm, i, SPAN), row_block(x_s, i, SPAN)) for i in range(2)]
    wo = [fetch.start(row_block(wo_hbm, i, 128), row_block(wo_s, i, 128)) for i in range(2)]
    c = [fetch.start(row_block(c_hbm, i, SPAN), row_block(c_s, i, SPAN)) for i in range(2)]
    stores = []
    for weights, inputs, w_s, in_s, out_s, out, dot in (
        (wq, x, wq_s, x_s, q_s, q_hbm, dot_nn),
        (wo, c, wo_s, c_s, da_s, da_hbm, dot_nt),
    ):
        for copy in weights:
            copy.wait()
        for half in range(2):
            inputs[half].wait()
            rows = slice(half * SPAN, (half + 1) * SPAN)
            out_s[rows] = dot(in_s[rows], w_s[...]).astype(bf16)
            stores.append(store.start(row_block(out_s, half, SPAN), row_block(out, half, SPAN)))
    for copy in stores:
        copy.wait()


def project_q(tokens, cotangent, w_query, w_out):
    return pl.pallas_call(
        q_kernel,
        in_specs=[any_spec()] * 4,
        out_specs=[any_spec()] * 2,
        out_shape=[shape((ROWS, COLS))] * 2,
        scratch_shapes=[
            pltpu.VMEM((ROWS, WIDTH), bf16),
            pltpu.VMEM((ROWS, WIDTH), bf16),
            pltpu.VMEM((WIDTH, COLS), bf16),
            pltpu.VMEM((COLS, WIDTH), bf16),
            pltpu.VMEM((ROWS, COLS), bf16),
            pltpu.VMEM((ROWS, COLS), bf16),
            pltpu.SemaphoreType.DMA((8,)),
            pltpu.SemaphoreType.DMA((4,)),
        ],
        compiler_params=params(60),
        cost_estimate=cost(ROWS * WIDTH * 2 * COLS, 7 * MIB),
        name="project_q",
    )(tokens, cotangent, w_query, w_out)


def entry_rows(refs, kb, lo):
    near, c2, l2, l3a, l3b = refs
    if kb < 2:
        return near[kb * BLOCK : (kb + 1) * BLOCK, lo : lo + 128]
    if kb == 2:
        return c2[:, lo : lo + 128]
    if kb == 3:
        return l2[:, lo : lo + 128]
    return jnp.concatenate([l3a[:, lo : lo + 128], l3b[:, lo : lo + 128]], axis=0)


def only_head(ref, head):
    lane = lax.broadcasted_iota(jnp.int32, (SPAN, 128), 1)
    keep = lane < HEAD_DIM if head % 2 == 0 else lane >= HEAD_DIM
    pair = head // 2 * 128
    return jnp.where(keep, ref[:, pair : pair + 128], jnp.zeros((), bf16))


def fold(values, combine):
    return combine(values.reshape(BLOCK // 8, 8, SPAN), axis=0)


def forward_kernel(*refs):
    entries, q_ref, da_ref, ot_ref, stat_ref = refs[:5], *refs[5:9]
    t_s, vt_s, qm_s, dm_s = refs[9:]
    for kb in range(5):
        rows = slice(kb * BLOCK, (kb + 1) * BLOCK)
        for pair in range(2):
            vt_s[pair * 128 : pair * 128 + 128, rows] = entry_rows(
                entries, kb, COLS + pair * 128
            ).T
    for head in range(4):
        qm_s[head] = only_head(q_ref, head)
        dm_s[head] = only_head(da_ref, head)
    for head in range(4):
        lo = head // 2 * 128
        slot = head % 2
        tops = []
        for kb in range(5):
            rows = slice(kb * BLOCK, (kb + 1) * BLOCK)
            t = dot_nt(entry_rows(entries, kb, lo), qm_s[head]) * SCORE_SCALE
            t_s[slot, rows] = t
            tops.append(fold(t, jnp.max) + OFFSETS[kb])
        top = jnp.max(functools.reduce(jnp.maximum, tops), axis=0, keepdims=True)
        total = jnp.zeros((8, SPAN), f32)
        inner = jnp.zeros((8, SPAN), f32)
        out = jnp.zeros((HEAD_DIM, SPAN), f32)
        mine = slice(head * HEAD_DIM, (head + 1) * HEAD_DIM)
        for kb in range(5):
            rows = slice(kb * BLOCK, (kb + 1) * BLOCK)
            raised = jnp.exp2(t_s[slot, rows] + (OFFSETS[kb] - top))
            p = dot_nt(entry_rows(entries, kb, COLS + lo), dm_s[head])
            total = total + fold(raised, jnp.sum)
            inner = inner + fold(raised * p, jnp.sum)
            out = out + dot_nn(vt_s[mine, rows], raised.astype(bf16))
        total = jnp.sum(total, axis=0, keepdims=True)
        inverse = 1.0 / total
        ot_ref[mine] = (out * inverse).astype(bf16)
        stat_ref[head : head + 1] = top + jnp.log2(total)
        stat_ref[head + 4 : head + 5] = jnp.sum(inner, axis=0, keepdims=True) * inverse


def attend(entries, queries, d_attended):
    part = pl.BlockSpec((SPAN, COLS), lambda i: (i, 0))
    return pl.pallas_call(
        forward_kernel,
        grid=(2,),
        in_specs=[
            pl.BlockSpec((SPAN, 2 * COLS), lambda i: (i, 0)),
            pl.BlockSpec((BLOCK, 2 * COLS), lambda i: (1 - i, 0)),
            pl.BlockSpec((BLOCK, 2 * COLS), lambda i: (0, 0)),
            pl.BlockSpec((BLOCK // 2, 2 * COLS), lambda i: (0, 0)),
            pl.BlockSpec((BLOCK // 2, 2 * COLS), lambda i: (0, 0)),
            part,
            part,
        ],
        out_specs=[
            pl.BlockSpec((COLS, SPAN), lambda i: (0, i)),
            pl.BlockSpec((8, SPAN), lambda i: (0, i)),
        ],
        out_shape=[shape((COLS, ROWS)), shape((8, ROWS), f32)],
        scratch_shapes=[
            pltpu.VMEM((2, KEYS, SPAN), f32),
            pltpu.VMEM((COLS, KEYS), bf16),
            pltpu.VMEM((4, SPAN, 128), bf16),
            pltpu.VMEM((4, SPAN, 128), bf16),
        ],
        compiler_params=params(60),
        cost_estimate=cost(4 * 3 * 4 * ROWS * KEYS * 64, 4 * MIB),
        name="attend",
    )(*entries, queries, d_attended)


def block_grads(key_rows, value_rows, keys_t, offset, qm, dm, stat, inner):
    t = dot_nt(key_rows, qm) * SCORE_SCALE
    attention = jnp.exp2(t + (offset - stat))
    weights = attention.astype(bf16)
    p = dot_nt(value_rows, dm)
    scores = (attention * (p - inner)).astype(bf16)
    return dot_nn(keys_t, scores), dot_nn(scores, qm), dot_nn(weights, dm)


def far_kernel(l2, l3a, l3b, q_ref, da_ref, stat_ref, qgt_ref, g2_ref, g3a_ref, g3b_ref,
               kt_s, qm_s, dm_s, grad_s):
    step = pl.program_id(0)
    refs = (None, None, None, l2, l3a, l3b)

    @pl.when(step == 0)
    def _():
        for kb in (3, 4):
            rows = slice((kb - 3) * BLOCK, (kb - 2) * BLOCK)
            for pair in range(2):
                part = entry_rows(refs[1:], kb, pair * 128)
                kt_s[pair * 128 : pair * 128 + 128, rows] = part.T
        grad_s[...] = jnp.zeros_like(grad_s)

    for head in range(4):
        qm_s[head] = only_head(q_ref, head)
        dm_s[head] = only_head(da_ref, head)
    for pair in range(2):
        lo = pair * 128
        query_grad = [jnp.zeros((HEAD_DIM, SPAN), f32)] * 2
        for kb in (3, 4):
            rows = slice((kb - 3) * BLOCK, (kb - 2) * BLOCK)
            key_grad = value_grad = 0.0
            for side in range(2):
                head = 2 * pair + side
                dq, dk, dv = block_grads(
                    entry_rows(refs[1:], kb, lo),
                    entry_rows(refs[1:], kb, COLS + lo),
                    kt_s[head * HEAD_DIM : (head + 1) * HEAD_DIM, rows],
                    OFFSETS[kb],
                    qm_s[head],
                    dm_s[head],
                    stat_ref[head : head + 1],
                    stat_ref[head + 4 : head + 5],
                )
                query_grad[side] = query_grad[side] + dq
                key_grad, value_grad = key_grad + dk, value_grad + dv
            grad_s[rows, lo : lo + 128] += key_grad
            grad_s[rows, COLS + lo : COLS + lo + 128] += value_grad
        for side in range(2):
            start = (2 * pair + side) * HEAD_DIM
            qgt_ref[start : start + HEAD_DIM] = query_grad[side]

    @pl.when(step == 1)
    def _():
        for ref, first, count in ((g2_ref, 0, 256), (g3a_ref, 256, 128), (g3b_ref, 384, 128)):
            rows = slice(first, first + count)
            ref[:, :COLS] = (grad_s[rows, :COLS] * INV_ROOT).astype(bf16)
            ref[:, COLS:] = grad_s[rows, COLS:].astype(bf16)


def far_grads(level_two, three_a, three_b, queries, d_attended, stats):
    part = pl.BlockSpec((SPAN, COLS), lambda i: (i, 0))
    two = pl.BlockSpec((BLOCK, 2 * COLS), lambda i: (0, 0))
    three = pl.BlockSpec((BLOCK // 2, 2 * COLS), lambda i: (0, 0))
    return pl.pallas_call(
        far_kernel,
        grid=(2,),
        in_specs=[two, three, three, part, part, pl.BlockSpec((8, SPAN), lambda i: (0, i))],
        out_specs=[pl.BlockSpec((COLS, SPAN), lambda i: (0, i)), two, three, three],
        out_shape=[
            shape((COLS, ROWS), f32),
            shape((BLOCK, 2 * COLS)),
            shape((BLOCK // 2, 2 * COLS)),
            shape((BLOCK // 2, 2 * COLS)),
        ],
        scratch_shapes=[
            pltpu.VMEM((COLS, 2 * BLOCK), bf16),
            pltpu.VMEM((4, SPAN, 128), bf16),
            pltpu.VMEM((4, SPAN, 128), bf16),
            pltpu.VMEM((2 * BLOCK, 2 * COLS), f32),
        ],
        compiler_params=params(60),
        cost_estimate=cost(4 * 5 * 4 * ROWS * 2 * BLOCK * 64, 4 * MIB),
        name="far_grads",
    )(level_two, three_a, three_b, queries, d_attended, stats)


def near_kernel(near, c2, q_ref, da_ref, stat_ref, part_ref, qgt_ref, own_ref, sib_ref,
                kt_s, qm_s, dm_s):
    refs = (near, c2, None, None, None)
    for kb in range(3):
        rows = slice(kb * BLOCK, (kb + 1) * BLOCK)
        for pair in range(2):
            part = entry_rows(refs, kb, pair * 128)
            kt_s[pair * 128 : pair * 128 + 128, rows] = part.T
    for head in range(4):
        qm_s[head] = only_head(q_ref, head)
        dm_s[head] = only_head(da_ref, head)
    for pair in range(2):
        lo = pair * 128
        query_grad = []
        for side in range(2):
            start = (2 * pair + side) * HEAD_DIM
            query_grad.append(part_ref[start : start + HEAD_DIM])
        for kb in range(3):
            rows = slice(kb * BLOCK, (kb + 1) * BLOCK)
            key_grad = value_grad = 0.0
            for side in range(2):
                head = 2 * pair + side
                dq, dk, dv = block_grads(
                    entry_rows(refs, kb, lo),
                    entry_rows(refs, kb, COLS + lo),
                    kt_s[head * HEAD_DIM : (head + 1) * HEAD_DIM, rows],
                    OFFSETS[kb],
                    qm_s[head],
                    dm_s[head],
                    stat_ref[head : head + 1],
                    stat_ref[head + 4 : head + 5],
                )
                query_grad[side] = query_grad[side] + dq
                key_grad, value_grad = key_grad + dk, value_grad + dv
            key_grad = key_grad * INV_ROOT
            if kb < 2:
                own_ref[rows, lo : lo + 128] = key_grad
                own_ref[rows, COLS + lo : COLS + lo + 128] = value_grad
            else:
                sib_ref[:, lo : lo + 128] = key_grad
                sib_ref[:, COLS + lo : COLS + lo + 128] = value_grad
        for side in range(2):
            start = (2 * pair + side) * HEAD_DIM
            qgt_ref[start : start + HEAD_DIM] = (query_grad[side] * INV_ROOT).astype(bf16)


def near_grads(key_value, own_2, queries, d_attended, stats, query_part):
    part = pl.BlockSpec((SPAN, COLS), lambda i: (i, 0))
    turned = pl.BlockSpec((COLS, SPAN), lambda i: (0, i))
    near = pl.BlockSpec((SPAN, 2 * COLS), lambda i: (i, 0))
    sibling = pl.BlockSpec((BLOCK, 2 * COLS), lambda i: (1 - i, 0))
    return pl.pallas_call(
        near_kernel,
        grid=(2,),
        in_specs=[near, sibling, part, part, pl.BlockSpec((8, SPAN), lambda i: (0, i)), turned],
        out_specs=[turned, near, sibling],
        out_shape=[
            shape((COLS, ROWS)),
            shape((ROWS, 2 * COLS), f32),
            shape((SPAN, 2 * COLS), f32),
        ],
        scratch_shapes=[
            pltpu.VMEM((COLS, 3 * BLOCK), bf16),
            pltpu.VMEM((4, SPAN, 128), bf16),
            pltpu.VMEM((4, SPAN, 128), bf16),
        ],
        compiler_params=params(60),
        cost_estimate=cost(4 * 5 * 4 * ROWS * 3 * BLOCK * 64, 8 * MIB),
        name="near_grads",
    )(key_value, own_2, queries, d_attended, stats, query_part)


def split_product(matrix, values):
    high = values.astype(bf16)
    low = (values - high.astype(f32)).astype(bf16)
    return dot_nn(matrix, high) + dot_nn(matrix, low)


def out_kernel(ot_ref, w_ref, out_ref):
    out_ref[...] = dot_nn(ot_ref[...].T, w_ref[...]).astype(bf16)


def project_out(attended_t, w_out):
    return pl.pallas_call(
        out_kernel,
        grid=(2,),
        in_specs=[
            pl.BlockSpec((COLS, SPAN), lambda i: (0, i)),
            pl.BlockSpec((COLS, WIDTH), lambda i: (0, 0)),
        ],
        out_specs=pl.BlockSpec((SPAN, WIDTH), lambda i: (i, 0)),
        out_shape=shape((ROWS, WIDTH)),
        compiler_params=params(24),
        cost_estimate=cost(ROWS * WIDTH * COLS, 4 * MIB),
        name="project_out",
    )(attended_t, w_out)


def swapped(value, bits):
    return lax.ppermute(value, "seq", [(i, i ^ bits) for i in range(lax.axis_size("seq"))])


def add(*terms):
    return sum(term.astype(f32) for term in terms).astype(bf16)


def head_sum(part):
    return lax.psum_scatter(part, "head", scatter_dimension=1, tiled=True)


def tail_kernel(
    at_ref, own_hbm, sib_hbm, got2_hbm, got3_hbm, qgt_hbm, ot_hbm, x_hbm, c_hbm,
    wq_hbm, wk_hbm, wv_hbm, part_hbm, mine_hbm, other_hbm,
    own_s, sib_s, got2_s, got3_s, qgt_s, ot_s, x_s, c_s, wq_s, wk_s, wv_s,
    part_s, kvg_s, g_s, in_sems, out_sems,
):
    core = at_ref[0]
    fetch, store = Copies(in_sems), Copies(out_sems)

    def halves(source, target):
        count = source.shape[0] // 2
        return [
            fetch.start(row_block(source, i, count), row_block(target, i, count)) for i in range(2)
        ]

    def wait(*copies):
        for copy in copies:
            copy.wait()

    ot = halves(ot_hbm, ot_s)
    c = halves(c_hbm, c_s)
    qgt = halves(qgt_hbm, qgt_s)
    x = halves(x_hbm, x_s)
    got = halves(got2_hbm, got2_s) + halves(got3_hbm, got3_s)
    sib = halves(sib_hbm, sib_s)
    own = halves(own_hbm, own_s)
    wq, wk, wv = halves(wq_hbm, wq_s), halves(wk_hbm, wk_s), halves(wv_hbm, wv_s)
    stores = []

    def finish(index, grad_t):
        g_s[index] = grad_t.astype(bf16).T.reshape(32, 2, 16, COLS)
        rows = pl.ds(index * 16, 16)
        stores.append(store.start(g_s.at[index, :, 1 - core], other_hbm.at[:, rows]))
        stores.append(store.start(g_s.at[index, :, core], mine_hbm.at[:, rows]))

    wait(*ot, *c)
    finish(0, dot_nn(ot_s[...], c_s[...]))
    wait(*qgt, *x)
    finish(1, dot_nn(qgt_s[...], x_s[...]))
    wait(*got, *sib)
    spread2 = run_matrix(SPAN, SPAN >> 1, 1, True)
    spread4 = run_matrix(SPAN, SPAN >> 2, 2, True)
    spread8 = run_matrix(SPAN, SPAN >> 3, 3, True)
    for half in range(2):
        own[half].wait()
        rows = slice(half * SPAN, (half + 1) * SPAN)
        total = own_s[rows] + split_product(spread2, sib_s[half * 256 : half * 256 + 256])
        total = total + dot_nn(spread4, got2_s[half * 128 : half * 128 + 128])
        total = total + dot_nn(spread8, got3_s[half * 64 : half * 64 + 64])
        kvg_s[rows] = total.astype(bf16)
    for index in range(2):
        finish(2 + index, dot_nn(kvg_s[:, index * COLS : (index + 1) * COLS].T, x_s[...]))
    wait(*wq, *wk, *wv)
    for half in range(2):
        rows = slice(half * SPAN, (half + 1) * SPAN)
        query_grad = qgt_s[:, rows].T
        for start in range(0, WIDTH, COLS):
            cols = slice(start, start + COLS)
            part = dot_nt(query_grad, wq_s[cols, :])
            part = part + dot_nt(kvg_s[rows, :COLS], wk_s[cols, :])
            part = part + dot_nt(kvg_s[rows, COLS:], wv_s[cols, :])
            part_s[rows, cols] = part.astype(bf16)
        stores.append(store.start(row_block(part_s, half, SPAN), row_block(part_hbm, half, SPAN)))
    wait(*stores)


def tail(at, *operands):
    dims = [operand.shape for operand in operands]
    return pl.pallas_call(
        tail_kernel,
        in_specs=[pl.BlockSpec(memory_space=pltpu.SMEM)] + [any_spec()] * len(operands),
        out_specs=[any_spec()] * 3,
        out_shape=[shape((ROWS, WIDTH))] + [shape((32, 64, COLS))] * 2,
        scratch_shapes=[pltpu.VMEM(o.shape, o.dtype) for o in operands]
        + [
            pltpu.VMEM((ROWS, WIDTH), bf16),
            pltpu.VMEM((ROWS, 2 * COLS), bf16),
            pltpu.VMEM((4, 32, 2, 16, COLS), bf16),
            pltpu.SemaphoreType.DMA((2 * len(dims),)),
            pltpu.SemaphoreType.DMA((10,)),
        ],
        compiler_params=params(60),
        cost_estimate=cost(7 * ROWS * WIDTH * COLS, 14 * MIB),
        name="tail",
    )(at, *operands)


def stage_kernel(at_ref, *refs, terms, picks):
    total_s = refs[-1]
    total_s[...] = sum(ref[...].astype(f32) for ref in refs[:terms]).astype(bf16)
    for pick, ref in zip(picks, refs[terms:-1]):
        for block, source in enumerate(pick(at_ref)):
            ref[block] = total_s[source]


def stage(at, terms, picks, counts, name):
    vmem = pl.BlockSpec(memory_space=pltpu.VMEM)
    dims = terms[0].shape
    return pl.pallas_call(
        functools.partial(stage_kernel, terms=len(terms), picks=picks),
        in_specs=[pl.BlockSpec(memory_space=pltpu.SMEM)] + [vmem] * len(terms),
        out_specs=[vmem] * len(counts),
        out_shape=[shape((count, *dims[1:])) for count in counts],
        scratch_shapes=[pltpu.VMEM(dims, bf16)],
        compiler_params=params(24),
        name=name,
    )(at, *terms)


def x_blocks(offset, first, count):
    return lambda at: [((at[1] + offset) & 3) * 8 + first + block for block in range(count)]


def z_blocks(bit, count, flip):
    def pick(at):
        mine = (at[2] >> bit) & 1
        return [2 * block + (1 - mine if flip else mine) for block in range(count)]

    return pick


def moved(value, by):
    size = lax.axis_size("seq")
    return lax.ppermute(value, "seq", [(i, (i + by) % size) for i in range(size)])


def seq_sum(at, mine, other):
    far_a, far_b, ahead, behind, here = stage(
        at,
        (mine, swapped(other, 1)),
        [x_blocks(2, 0, 4), x_blocks(2, 4, 4), x_blocks(1, 0, 8), x_blocks(3, 0, 8)]
        + [x_blocks(0, 0, 8)],
        [4, 4, 8, 8, 8],
        "sum_cores",
    )
    got_a, got_b = moved(far_a, 16), moved(far_b, -16)
    ahead = jnp.concatenate([add(ahead[:4], got_a), ahead[4:]], axis=0)
    behind = jnp.concatenate([behind[:4], add(behind[4:], got_b)], axis=0)
    terms = (here, moved(ahead, 16), moved(behind, -16))
    for bit, count in ((0, 4), (1, 2), (2, 1)):
        kept, away = stage(
            at,
            terms,
            [z_blocks(bit, count, False), z_blocks(bit, count, True)],
            [count, count],
            f"sum_z{bit}",
        )
        terms = (kept, swapped(away, 2 << bit))
    return terms[0][0].astype(f32) + terms[1][0].astype(f32)


def on_device(tokens, cotangent, w_query, w_key, w_value, w_out):
    place = lax.axis_index("seq")
    at = jnp.stack([place % 2, place // 16, place // 2 % 8]).astype(jnp.int32)
    key_value, own_2, own_4, own_8 = project_kv(tokens, w_key, w_value)
    three_a = swapped(own_8, 2)
    level_two = swapped(own_4, 1)
    queries, d_attended = project_q(tokens, cotangent, w_query, w_out)
    queries, three_a = lax.optimization_barrier((queries, three_a))
    three_b = swapped(three_a, 1)
    entries = (key_value, own_2, level_two, three_a, three_b)
    attended_t, stats = attend(entries, queries, d_attended)
    query_part, grad_2, grad_3a, grad_3b = far_grads(
        level_two, three_a, three_b, queries, d_attended, stats
    )
    got_2 = swapped(grad_2, 1)
    got_3b = swapped(grad_3b, 1)
    attended_t, grad_3b = lax.optimization_barrier((attended_t, grad_3b))
    layer_out = head_sum(project_out(attended_t, w_out))
    got_3 = swapped(add(grad_3a, got_3b), 2)
    query_grad_t, own, sibling = near_grads(
        key_value, own_2, queries, d_attended, stats, query_part
    )
    part, mine, other = tail(
        at, own, sibling, got_2, got_3, query_grad_t, attended_t, tokens, cotangent,
        w_query, w_key, w_value,
    )
    grad_tokens = head_sum(part)
    scale = 1.0 / math.sqrt(lax.axis_size("seq") * tokens.shape[0])
    summed = seq_sum(at, mine, other) * scale
    return (
        layer_out,
        grad_tokens,
        summed[16:32],
        summed[32:48],
        summed[48:],
        summed[:16].T,
    )


def solution(mesh):
    return jax.shard_map(
        on_device,
        mesh=mesh,
        in_specs=(
            P("seq", None),
            P("seq", None),
            P(None, "head"),
            P(None, "head"),
            P(None, "head"),
            P("head", None),
        ),
        out_specs=(
            P("seq", "head"),
            P("seq", "head"),
            P("seq", "head"),
            P("seq", "head"),
            P("seq", "head"),
            P("head", "seq"),
        ),
        check_vma=False,
    )
```

time: 132 us -> 127 us (0.962)
  Pallas kernels: 45.3 us -> 62.5 us
  waiting for transfers between devices: 37.4 us -> 22.5 us
  between operations: 0.87 us -> 14.3 us
  starting transfers between devices: 33.9 us -> 23.6 us
  local copies, waits for them, and re-layouts: 10.7 us -> 3.31 us
  other arithmetic: 2.61 us -> 0.75 us
    pallas_call x11, Pallas kernels: 45.3 us -> 62.5 us  [the longest x1 14.7 us: attend(): pl.pallas_call(forward_kernel, grid=(2,), in_specs=[pl.BlockSpec((SPAN, 2...]
    ppermute x12 -> x4, starting transfers between devices: 16.6 us -> 7.03 us  [moved(): lax.ppermute(value, 'seq', [(i, (i + by) % size) for i in range(size)])]
    ppermute x12 -> x4, waiting for transfers between devices: 19.9 us -> 11.4 us  [moved(): lax.ppermute(value, 'seq', [(i, (i + by) % size) for i in range(size)])]
    unnamed x28 -> x26, local copies, waits for them, and re-layouts: 9.31 us -> 2.66 us
    ppermute x10, waiting for transfers between devices: 17.5 us -> 11.1 us  [swapped(): lax.ppermute(value, 'seq', [(i, i ^ bits) for i in range(lax.axis_size('s...]
    concatenate x2 -> x0, other arithmetic: 1.66 us -> none  [head_sum(): jnp.concatenate([add(mine[:half], got_left[:half], more_right), add(mine[...]
  transfers between devices with their start and end apart: 22 -> 16, of which waited for: 12 -> 9; matrix products, arithmetic and copies ran while one was open for 3% -> 1% of each run, Pallas kernels for 4% -> 25%
where the time goes in v2:
time: 127 us
  Pallas kernels  62.5 us (49%)
  starting transfers between devices  23.6 us (19%)
  waiting for transfers between devices  22.5 us (18%)
  between operations  14.3 us (11%)
  local copies, waits for them, and re-layouts  3.31 us (3%)
    ppermute x10, starting transfers between devices, swapped(): lax.ppermute(value, 'seq', [(i, i ^ bits) for i in range(lax.axis_size('s...  16.5 us
    pallas_call x1, Pallas kernels, attend(): pl.pallas_call(forward_kernel, grid=(2,), in_specs=[pl.BlockSpec((SPAN, 2...  14.7 us
    pallas_call x1, Pallas kernels, near_grads(): pl.pallas_call(near_kernel, grid=(2,), in_specs=[near, sibling, part, par...  13.3 us
    ppermute x4, waiting for transfers between devices, moved(): lax.ppermute(value, 'seq', [(i, (i + by) % size) for i in range(size)])  11.4 us
    ppermute x10, waiting for transfers between devices, swapped(): lax.ppermute(value, 'seq', [(i, i ^ bits) for i in range(lax.axis_size('s...  11.1 us
    pallas_call x1, Pallas kernels, tail(): pl.pallas_call(tail_kernel, in_specs=[pl.BlockSpec(memory_space=pltpu.SME...  9.88 us
    pallas_call x1, Pallas kernels, far_grads(): pl.pallas_call(far_kernel, grid=(2,), in_specs=[two, three, three, part,...  9.35 us
    ppermute x4, starting transfers between devices, moved(): lax.ppermute(value, 'seq', [(i, (i + by) % size) for i in range(size)])  7.03 us
  transfers between devices with their start and end apart: 16, of which 9 were waited for; matrix products, arithmetic and copies ran while one was open for 1% of the time, Pallas kernels for 25%

profile of v2, /device:TPU:24, one launch (start us, length us, event | category | flops | bytes accessed | tf_op | source)
XLA Modules:
  0.0 127.0 jit_solution(10470527330667377625)
XLA Ops:
  7.2 5.2 %project_kv.1 = (bf16[1024,512]{1,0:T(8,128)(2,1)}, bf16[512,512]{1,0:T(8,128)(2,1)}, bf16[256,512]{1,0:T(8,128)(2,1)}, bf16[128,512]{1,0:T(8,128)(2,1)}) custom-call(bf16[1024,1024]{1,0:T(8,128)(2,1)} %x_hbm.5, bf16[1024,256]{1,0:T(8,128)(2,1)} %wk_hbm.3, bf16[1024,256]{1,0:T(8,128)(2,1)} %wv_hbm.3), custom_call_target="tpu_custom_call" | custom-call | flops 1073741824 | bytes 6291456 | tf_op jit(solution)/shard_map/project_kv/pallas_call | solution.py:112
  12.4 2.0 %collective-permute-start.1 = (bf16[128,512]{1,0:T(8,128)(2,1)}, bf16[128,512]{1,0:T(8,128)(2,1)S(1)}, u32[]{:S(2)}, u32[]{:S(2)}) collective-permute-start(bf16[128,512]{1,0:T(8,128)(2,1)} %get-tuple-element.42), channel_id=1, source_target_pairs={{0,8},{4,12},{8,0},{12,4},{16,24},{20,28},{24,16},{28,20},{32,40},... | collective-permute-start | bytes 393224 | tf_op jit(solution)/shard_map/ppermute | solution.py:456
  14.4 5.0 %project_q.1 = (bf16[1024,256]{1,0:T(8,128)(2,1)}, bf16[1024,256]{1,0:T(8,128)(2,1)}) custom-call(bf16[1024,1024]{1,0:T(8,128)(2,1)} %x_hbm.5, bf16[1024,1024]{1,0:T(8,128)(2,1)} %c_hbm.3, bf16[1024,256]{1,0:T(8,128)(2,1)} %wq_hbm.3, bf16[256,1024]{1,0:T(8,128)(2,1)} %w_ref.1), custom_call_target="tpu_custom_call" | custom-call | flops 1073741824 | bytes 7340032 | tf_op jit(solution)/shard_map/project_q/pallas_call | solution.py:156
  19.5 0.8 collective-permute-start.2
  20.2 1.0 collective-permute-done.2.refs_4_.l3b
  22.0 14.7 %attend.1 = (bf16[256,1024]{1,0:T(8,128)(2,1)}, f32[8,1024]{1,0:T(8,128)}) custom-call(bf16[1024,512]{1,0:T(8,128)(2,1)} %get-tuple-element.38.refs_0_.near, bf16[512,512]{1,0:T(8,128)(2,1)} %get-tuple-element.39.refs_1_.c2, bf16[256,512]{1,0:T(8,128)(2,1)} %copy-done.8, bf16[128,512]{1,0:T(8,128)(2,1)} %copy-done.10, bf16[128,512]{1,0:T(8,128)(2,1)} %copy-done.12, ...), custom_call_target="tpu_custom_call" | custom-call | flops 8053063680 | bytes 4194304 | tf_op jit(solution)/shard_map/attend/pallas_call | solution.py:241
  36.7 9.4 %far_grads.1 = (f32[256,1024]{1,0:T(8,128)}, bf16[256,512]{1,0:T(8,128)(2,1)}, bf16[128,512]{1,0:T(8,128)(2,1)}, bf16[128,512]{1,0:T(8,128)(2,1)}) custom-call(bf16[256,512]{1,0:T(8,128)(2,1)} %copy-done.8, bf16[128,512]{1,0:T(8,128)(2,1)} %copy-done.10, bf16[128,512]{1,0:T(8,128)(2,1)} %copy-done.12, bf16[1024,256]{1,0:T(8,128)(2,1)} %get-tuple-element.44.refs_5_.q_ref, ...), custom_call_target="tpu_custom_call" | custom-call | flops 5368709120 | bytes 4194304 | tf_op jit(solution)/shard_map/far_grads/pallas_call | solution.py:334
  46.1 2.0 %project_out.1 = bf16[1024,1024]{1,0:T(8,128)(2,1)} custom-call(bf16[256,1024]{1,0:T(8,128)(2,1)S(1)} %copy-done.2, bf16[256,1024]{1,0:T(8,128)(2,1)S(1)} %copy-done), custom_call_target="tpu_custom_call" | custom-call | flops 536870912 | bytes 4194304 | tf_op jit(solution)/shard_map/project_out/pallas_call | solution.py:440
  50.1 13.3 %near_grads.1 = (bf16[256,1024]{1,0:T(8,128)(2,1)}, f32[1024,512]{1,0:T(8,128)}, f32[512,512]{1,0:T(8,128)}) custom-call(bf16[1024,512]{1,0:T(8,128)(2,1)} %get-tuple-element.38.refs_0_.near, bf16[512,512]{1,0:T(8,128)(2,1)} %get-tuple-element.39.refs_1_.c2, bf16[1024,256]{1,0:T(8,128)(2,1)} %get-tuple-element.44.refs_5_.q_ref, ...), custom_call_target="tpu_custom_call" | custom-call | flops 8053063680 | bytes 8388608 | tf_op jit(solution)/shard_map/near_grads/pallas_call | solution.py:408
  64.2 9.9 %tail.1 = (bf16[1024,1024]{1,0:T(8,128)(2,1)}, bf16[32,64,256]{2,1,0:T(8,128)(2,1)}, bf16[32,64,256]{2,1,0:T(8,128)(2,1)}) custom-call(s32[3]{0:T(128)} %pad_add_fusion.at_ref, f32[1024,512]{1,0:T(8,128)} %get-tuple-element.51.own_hbm, f32[512,512]{1,0:T(8,128)} %get-tuple-element.52.sib_hbm, bf16[256,512]{1,0:T(8,128)(2,1)} %copy-done.7, ...), custom_call_target="tpu_custom_call" | custom-call | flops 3758096384 | bytes 14680064 | tf_op jit(solution)/shard_map/tail/pallas_call | solution.py:535
  74.1 1.2 copy-done.5
  75.5 2.4 %collective-permute-done.6.refs_1_ = bf16[32,64,256]{2,1,0:T(8,128)(2,1)S(1)} collective-permute-done((bf16[32,64,256]{2,1,0:T(8,128)(2,1)S(1)}, bf16[32,64,256]{2,1,0:T(8,128)(2,1)S(1)}, u32[]{:S(2)}, u32[]{:S(2)}) %collective-permute-start.6) | collective-permute-done | bytes 1048608 | tf_op jit(solution)/shard_map/ppermute | solution.py:456
  77.9 1.2 sum_cores.1
  79.1 2.8 %collective-permute-start.9 = (bf16[4,64,256]{2,1,0:T(8,128)(2,1)S(1)}, bf16[4,64,256]{2,1,0:T(8,128)(2,1)S(1)}, u32[]{:S(2)}, u32[]{:S(2)}) collective-permute-start(bf16[4,64,256]{2,1,0:T(8,128)(2,1)S(1)} %get-tuple-element.63), channel_id=1, source_target_pairs={{0,192},{4,196},{8,200},{12,204},{16,208},{20,212},{24,216},{28,22... | collective-permute-start | bytes 393224 | tf_op jit(solution)/shard_map/ppermute | solution.py:590
  82.3 2.8 %collective-permute-done.9 = bf16[4,64,256]{2,1,0:T(8,128)(2,1)S(1)} collective-permute-done((bf16[4,64,256]{2,1,0:T(8,128)(2,1)S(1)}, bf16[4,64,256]{2,1,0:T(8,128)(2,1)S(1)}, u32[]{:S(2)}, u32[]{:S(2)}) %collective-permute-start.9) | collective-permute-done | bytes 131104 | tf_op jit(solution)/shard_map/ppermute | solution.py:590
  85.2 3.8 %collective-permute-start.10 = (bf16[8,64,256]{2,1,0:T(8,128)(2,1)S(1)}, bf16[8,64,256]{2,1,0:T(8,128)(2,1)S(1)}, u32[]{:S(2)}, u32[]{:S(2)}) collective-permute-start(bf16[8,64,256]{2,1,0:T(8,128)(2,1)S(1)} %pad_maximum_fusion.1), channel_id=1, source_target_pairs={{0,192},{4,196},{8,200},{12,204},{16,208},{20,212},{24,216},{28,22... | collective-permute-start | bytes 786440 | tf_op jit(solution)/shard_map/ppermute | solution.py:590
  89.1 5.0 %collective-permute-done.10.refs_2_ = bf16[8,64,256]{2,1,0:T(8,128)(2,1)S(1)} collective-permute-done((bf16[8,64,256]{2,1,0:T(8,128)(2,1)S(1)}, bf16[8,64,256]{2,1,0:T(8,128)(2,1)S(1)}, u32[]{:S(2)}, u32[]{:S(2)}) %collective-permute-start.10) | collective-permute-done | bytes 262176 | tf_op jit(solution)/shard_map/ppermute | solution.py:590
  94.1 3.6 %collective-permute-done.8.refs_1_ = bf16[8,64,256]{2,1,0:T(8,128)(2,1)S(1)} collective-permute-done((bf16[8,64,256]{2,1,0:T(8,128)(2,1)S(1)}, bf16[8,64,256]{2,1,0:T(8,128)(2,1)S(1)}, u32[]{:S(2)}, u32[]{:S(2)}) %collective-permute-start.8) | collective-permute-done | bytes 262176 | tf_op jit(solution)/shard_map/ppermute | solution.py:590
  98.4 1.7 %collective-permute-start.11 = (bf16[4,64,256]{2,1,0:T(8,128)(2,1)S(1)}, bf16[4,64,256]{2,1,0:T(8,128)(2,1)S(1)}, u32[]{:S(2)}, u32[]{:S(2)}) collective-permute-start(bf16[4,64,256]{2,1,0:T(8,128)(2,1)S(1)} %get-tuple-element.65), channel_id=1, source_target_pairs={{0,8},{4,12},{8,0},{12,4},{16,24},{20,28},{24,16},{28,20},{32,40},... | collective-permute-start | bytes 393224 | tf_op jit(solution)/shard_map/ppermute | solution.py:456
  100.2 3.3 %collective-permute-done.11.refs_1_ = bf16[4,64,256]{2,1,0:T(8,128)(2,1)S(1)} collective-permute-done((bf16[4,64,256]{2,1,0:T(8,128)(2,1)S(1)}, bf16[4,64,256]{2,1,0:T(8,128)(2,1)S(1)}, u32[]{:S(2)}, u32[]{:S(2)}) %collective-permute-start.11) | collective-permute-done | bytes 131104 | tf_op jit(solution)/shard_map/ppermute | solution.py:456
  104.1 3.4 %collective-permute-start.12 = (bf16[2,64,256]{2,1,0:T(8,128)(2,1)S(1)}, bf16[2,64,256]{2,1,0:T(8,128)(2,1)S(1)}, u32[]{:S(2)}, u32[]{:S(2)}) collective-permute-start(bf16[2,64,256]{2,1,0:T(8,128)(2,1)S(1)} %get-tuple-element.67), channel_id=1, source_target_pairs={{0,16},{4,20},{8,24},{12,28},{16,0},{20,4},{24,8},{28,12},{32,48},... | collective-permute-start | bytes 196616 | tf_op jit(solution)/shard_map/ppermute | solution.py:456
  107.5 2.2 %collective-permute-done.12.refs_1_ = bf16[2,64,256]{2,1,0:T(8,128)(2,1)S(1)} collective-permute-done((bf16[2,64,256]{2,1,0:T(8,128)(2,1)S(1)}, bf16[2,64,256]{2,1,0:T(8,128)(2,1)S(1)}, u32[]{:S(2)}, u32[]{:S(2)}) %collective-permute-start.12) | collective-permute-done | bytes 65568 | tf_op jit(solution)/shard_map/ppermute | solution.py:456
  110.3 7.3 %collective-permute-start.13 = (bf16[1,64,256]{2,1,0:T(8,128)(2,1)S(1)}, bf16[1,64,256]{2,1,0:T(8,128)(2,1)S(1)}, u32[]{:S(2)}, u32[]{:S(2)}) collective-permute-start(bf16[1,64,256]{2,1,0:T(8,128)(2,1)S(1)} %get-tuple-element.69), channel_id=1, source_target_pairs={{0,32},{4,36},{8,40},{12,44},{16,48},{20,52},{24,56},{28,60},{32,0... | collective-permute-start | bytes 98312 | tf_op jit(solution)/shard_map/ppermute | solution.py:456
  117.7 1.9 %collective-permute-done.13 = bf16[1,64,256]{2,1,0:T(8,128)(2,1)S(1)} collective-permute-done((bf16[1,64,256]{2,1,0:T(8,128)(2,1)S(1)}, bf16[1,64,256]{2,1,0:T(8,128)(2,1)S(1)}, u32[]{:S(2)}, u32[]{:S(2)}) %collective-permute-start.13) | collective-permute-done | bytes 32800 | tf_op jit(solution)/shard_map/ppermute | solution.py:456
  (57 shorter events, 6.9 us)
Async XLA Ops:
  7.2 113.0 %reduce-scatter.3.cloned.1.call-start = ((), (), s32[]{:S(2)}) async-start(), calls=%async_computation.2 | async-start | bytes 2621440 | tf_op jit(solution)/shard_map/reduce_scatter | solution.py:464
  12.4 7.1 %collective-permute-start.1 = (bf16[128,512]{1,0:T(8,128)(2,1)}, bf16[128,512]{1,0:T(8,128)(2,1)S(1)}, u32[]{:S(2)}, u32[]{:S(2)}) collective-permute-start(bf16[128,512]{1,0:T(8,128)(2,1)} %get-tuple-element.42), channel_id=1, source_target_pairs={{0,8},{4,12},{8,0},{12,4},{16,24},{20,28},{24,16},{28,20},{32,40},... | collective-permute-start | bytes 393224 | tf_op jit(solution)/shard_map/ppermute | solution.py:456
  14.4 6.8 %collective-permute-start = (bf16[256,512]{1,0:T(8,128)(2,1)}, bf16[256,512]{1,0:T(8,128)(2,1)S(1)}, u32[]{:S(2)}, u32[]{:S(2)}) collective-permute-start(bf16[256,512]{1,0:T(8,128)(2,1)} %get-tuple-element.40), channel_id=1, source_target_pairs={{0,4},{4,0},{8,12},{12,8},{16,20},{20,16},{24,28},{28,24},{32,36},... | collective-permute-start | bytes 786440 | tf_op jit(solution)/shard_map/ppermute | solution.py:456
  19.5 1.8 %copy-start.10 = (bf16[128,512]{1,0:T(8,128)(2,1)}, bf16[128,512]{1,0:T(8,128)(2,1)S(1)}, u32[]{:S(2)}) copy-start(bf16[128,512]{1,0:T(8,128)(2,1)S(1)} %collective-permute-done.1.refs_3_.l3a) | copy-start | bytes 393220
  19.5 1.8 %collective-permute-start.2 = (bf16[128,512]{1,0:T(8,128)(2,1)S(1)}, bf16[128,512]{1,0:T(8,128)(2,1)S(1)}, u32[]{:S(2)}, u32[]{:S(2)}) collective-permute-start(bf16[128,512]{1,0:T(8,128)(2,1)S(1)} %collective-permute-done.1.refs_3_.l3a), channel_id=1, source_target_pairs={{0,4},{4,0},{8,12},{12,8},{16,20},{20,16},{24,28},{28,24},{32,36},... | collective-permute-start | bytes 393224 | tf_op jit(solution)/shard_map/ppermute | solution.py:456
  36.7 9.4 %copy-start = (bf16[256,1024]{1,0:T(8,128)(2,1)S(1)}, bf16[256,1024]{1,0:T(8,128)(2,1)}, u32[]{:S(2)}) copy-start(bf16[256,1024]{1,0:T(8,128)(2,1)} %w_ref.1) | copy-start | bytes 1572868
  36.7 9.4 %copy-start.2 = (bf16[256,1024]{1,0:T(8,128)(2,1)S(1)}, bf16[256,1024]{1,0:T(8,128)(2,1)}, u32[]{:S(2)}) copy-start(bf16[256,1024]{1,0:T(8,128)(2,1)} %get-tuple-element.49.ot_ref.ot_hbm) | copy-start | bytes 1572868
  46.1 2.1 %copy-start.9 = (bf16[128,512]{1,0:T(8,128)(2,1)S(1)}, bf16[128,512]{1,0:T(8,128)(2,1)}, u32[]{:S(2)}) copy-start(bf16[128,512]{1,0:T(8,128)(2,1)} %get-tuple-element.48) | copy-start | bytes 393220
  46.1 3.1 %copy-start.6 = (bf16[256,512]{1,0:T(8,128)(2,1)S(1)}, bf16[256,512]{1,0:T(8,128)(2,1)}, u32[]{:S(2)}) copy-start(bf16[256,512]{1,0:T(8,128)(2,1)} %get-tuple-element.53) | copy-start | bytes 786436
  46.1 3.5 %copy-start.4 = (bf16[128,512]{1,0:T(8,128)(2,1)S(1)}, bf16[128,512]{1,0:T(8,128)(2,1)}, u32[]{:S(2)}) copy-start(bf16[128,512]{1,0:T(8,128)(2,1)} %get-tuple-element.54) | copy-start | bytes 393220
  48.1 72.1 %reduce-scatter.5.cloned.1.call-start = ((), (), s32[]{:S(2)}) async-start(), calls=%async_computation.3 | async-start | bytes 2621440 | tf_op jit(solution)/shard_map/reduce_scatter | solution.py:464
  48.2 1.4 %collective-permute-start.4 = (bf16[128,512]{1,0:T(8,128)(2,1)S(1)}, bf16[128,512]{1,0:T(8,128)(2,1)S(1)}, u32[]{:S(2)}, u32[]{:S(2)}) collective-permute-start(bf16[128,512]{1,0:T(8,128)(2,1)S(1)} %copy-done.9), channel_id=1, source_target_pairs={{0,4},{4,0},{8,12},{12,8},{16,20},{20,16},{24,28},{28,24},{32,36},... | collective-permute-start | bytes 393224 | tf_op jit(solution)/shard_map/ppermute | solution.py:456
  49.2 14.2 %collective-permute-start.3 = (bf16[256,512]{1,0:T(8,128)(2,1)S(1)}, bf16[256,512]{1,0:T(8,128)(2,1)S(1)}, u32[]{:S(2)}, u32[]{:S(2)}) collective-permute-start(bf16[256,512]{1,0:T(8,128)(2,1)S(1)} %copy-done.6), channel_id=1, source_target_pairs={{0,4},{4,0},{8,12},{12,8},{16,20},{20,16},{24,28},{28,24},{32,36},... | collective-permute-start | bytes 786440 | tf_op jit(solution)/shard_map/ppermute | solution.py:456
  49.7 13.7 %collective-permute-start.5 = (bf16[128,512]{1,0:T(8,128)(2,1)S(1)}, bf16[128,512]{1,0:T(8,128)(2,1)S(1)}, u32[]{:S(2)}, u32[]{:S(2)}) collective-permute-start(bf16[128,512]{1,0:T(8,128)(2,1)S(1)} %add_convert_fusion.2), channel_id=1, source_target_pairs={{0,8},{4,12},{8,0},{12,4},{16,24},{20,28},{24,16},{28,20},{32,40},... | collective-permute-start | bytes 393224 | tf_op jit(solution)/shard_map/ppermute | solution.py:456
  74.1 3.9 %copy-start.1 = (bf16[32,64,256]{2,1,0:T(8,128)(2,1)S(1)}, bf16[32,64,256]{2,1,0:T(8,128)(2,1)}, u32[]{:S(2)}) copy-start(bf16[32,64,256]{2,1,0:T(8,128)(2,1)} %get-tuple-element.57.refs_0_) | copy-start | bytes 3145732
  74.1 3.9 %copy-start.3 = (s32[3]{0:T(128)S(1)}, s32[3]{0:T(128)}, u32[]{:S(2)}) copy-start(s32[3]{0:T(128)} %pad_add_fusion.at_ref) | copy-start | bytes 40
  75.3 2.7 %collective-permute-start.6 = (bf16[32,64,256]{2,1,0:T(8,128)(2,1)S(1)}, bf16[32,64,256]{2,1,0:T(8,128)(2,1)S(1)}, u32[]{:S(2)}, u32[]{:S(2)}) collective-permute-start(bf16[32,64,256]{2,1,0:T(8,128)(2,1)S(1)} %copy-done.5), channel_id=1, source_target_pairs={{0,4},{4,0},{8,12},{12,8},{16,20},{20,16},{24,28},{28,24},{32,36},... | collective-permute-start | bytes 3145736 | tf_op jit(solution)/shard_map/ppermute | solution.py:456
  79.1 6.0 %collective-permute-start.9 = (bf16[4,64,256]{2,1,0:T(8,128)(2,1)S(1)}, bf16[4,64,256]{2,1,0:T(8,128)(2,1)S(1)}, u32[]{:S(2)}, u32[]{:S(2)}) collective-permute-start(bf16[4,64,256]{2,1,0:T(8,128)(2,1)S(1)} %get-tuple-element.63), channel_id=1, source_target_pairs={{0,192},{4,196},{8,200},{12,204},{16,208},{20,212},{24,216},{28,22... | collective-permute-start | bytes 393224 | tf_op jit(solution)/shard_map/ppermute | solution.py:590
  82.0 7.0 %collective-permute-start.7 = (bf16[4,64,256]{2,1,0:T(8,128)(2,1)S(1)}, bf16[4,64,256]{2,1,0:T(8,128)(2,1)S(1)}, u32[]{:S(2)}, u32[]{:S(2)}) collective-permute-start(bf16[4,64,256]{2,1,0:T(8,128)(2,1)S(1)} %get-tuple-element.61), channel_id=1, source_target_pairs={{0,64},{4,68},{8,72},{12,76},{16,80},{20,84},{24,88},{28,92},{32,9... | collective-permute-start | bytes 393224 | tf_op jit(solution)/shard_map/ppermute | solution.py:590
  85.2 8.9 %collective-permute-start.10 = (bf16[8,64,256]{2,1,0:T(8,128)(2,1)S(1)}, bf16[8,64,256]{2,1,0:T(8,128)(2,1)S(1)}, u32[]{:S(2)}, u32[]{:S(2)}) collective-permute-start(bf16[8,64,256]{2,1,0:T(8,128)(2,1)S(1)} %pad_maximum_fusion.1), channel_id=1, source_target_pairs={{0,192},{4,196},{8,200},{12,204},{16,208},{20,212},{24,216},{28,22... | collective-permute-start | bytes 786440 | tf_op jit(solution)/shard_map/ppermute | solution.py:590
  89.0 8.7 %collective-permute-start.8 = (bf16[8,64,256]{2,1,0:T(8,128)(2,1)S(1)}, bf16[8,64,256]{2,1,0:T(8,128)(2,1)S(1)}, u32[]{:S(2)}, u32[]{:S(2)}) collective-permute-start(bf16[8,64,256]{2,1,0:T(8,128)(2,1)S(1)} %pad_maximum_fusion), channel_id=1, source_target_pairs={{0,64},{4,68},{8,72},{12,76},{16,80},{20,84},{24,88},{28,92},{32,9... | collective-permute-start | bytes 786440 | tf_op jit(solution)/shard_map/ppermute | solution.py:590
  98.4 5.1 %collective-permute-start.11 = (bf16[4,64,256]{2,1,0:T(8,128)(2,1)S(1)}, bf16[4,64,256]{2,1,0:T(8,128)(2,1)S(1)}, u32[]{:S(2)}, u32[]{:S(2)}) collective-permute-start(bf16[4,64,256]{2,1,0:T(8,128)(2,1)S(1)} %get-tuple-element.65), channel_id=1, source_target_pairs={{0,8},{4,12},{8,0},{12,4},{16,24},{20,28},{24,16},{28,20},{32,40},... | collective-permute-start | bytes 393224 | tf_op jit(solution)/shard_map/ppermute | solution.py:456
  104.1 5.7 %collective-permute-start.12 = (bf16[2,64,256]{2,1,0:T(8,128)(2,1)S(1)}, bf16[2,64,256]{2,1,0:T(8,128)(2,1)S(1)}, u32[]{:S(2)}, u32[]{:S(2)}) collective-permute-start(bf16[2,64,256]{2,1,0:T(8,128)(2,1)S(1)} %get-tuple-element.67), channel_id=1, source_target_pairs={{0,16},{4,20},{8,24},{12,28},{16,0},{20,4},{24,8},{28,12},{32,48},... | collective-permute-start | bytes 196616 | tf_op jit(solution)/shard_map/ppermute | solution.py:456
  110.3 9.2 %collective-permute-start.13 = (bf16[1,64,256]{2,1,0:T(8,128)(2,1)S(1)}, bf16[1,64,256]{2,1,0:T(8,128)(2,1)S(1)}, u32[]{:S(2)}, u32[]{:S(2)}) collective-permute-start(bf16[1,64,256]{2,1,0:T(8,128)(2,1)S(1)} %get-tuple-element.69), channel_id=1, source_target_pairs={{0,32},{4,36},{8,40},{12,44},{16,48},{20,52},{24,56},{28,60},{32,0... | collective-permute-start | bytes 98312 | tf_op jit(solution)/shard_map/ppermute | solution.py:456
  (5 other events, 4.0 us)
Sparse Core Ops, SparseCore 0:
  48.3 32.1 reduce-scatter.2
  83.8 31.9 reduce-scatter.4

commit v3 on v2

v3 whole, which is shorter than its diff:
```python
import functools
import math

import jax
import jax.numpy as jnp
from jax import lax
from jax.experimental import pallas as pl
from jax.experimental.pallas import tpu as pltpu
from jax.sharding import PartitionSpec as P

HEAD_DIM = 64
BLOCK = 256
SPAN = 2 * BLOCK
KEYS = 5 * BLOCK
ROWS = 4 * BLOCK
WIDTH = 1024
COLS = 256
MIB = 1024 * 1024
OFFSETS = (0.0, 0.0, 1.0, 2.0, 3.0)
SCORE_SCALE = 1.0 / (math.log(2.0) * math.sqrt(HEAD_DIM))
INV_ROOT = 1.0 / math.sqrt(HEAD_DIM)
bf16 = jnp.bfloat16
f32 = jnp.float32


def dot_nn(a, b):
    return lax.dot_general(a, b, (((1,), (0,)), ((), ())), preferred_element_type=f32)


def dot_nt(a, b):
    return lax.dot_general(a, b, (((1,), (1,)), ((), ())), preferred_element_type=f32)


def params(mib):
    return pltpu.CompilerParams(vmem_limit_bytes=mib * MIB)


def shape(dims, dtype=bf16):
    return jax.ShapeDtypeStruct(dims, dtype)


def cost(macs, nbytes):
    return pl.CostEstimate(flops=2 * macs, bytes_accessed=nbytes, transcendentals=0)


def run_matrix(rows, cols, shift, expand):
    i = lax.broadcasted_iota(jnp.int32, (rows, cols), 0)
    j = lax.broadcasted_iota(jnp.int32, (rows, cols), 1)
    inside = (i >> shift) == j if expand else i == (j >> shift)
    return jnp.where(inside, 2.0**-shift, 0.0).astype(bf16)


class Copies:
    def __init__(self, sems):
        self.sems = sems
        self.count = 0

    def start(self, source, target):
        copy = pltpu.make_async_copy(source, target, self.sems.at[self.count])
        self.count += 1
        copy.start()
        return copy


def row_block(ref, index, count):
    return ref.at[pl.ds(index * count, count)]


def any_spec():
    return pl.BlockSpec(memory_space=pl.ANY)


def kv_kernel(
    x_hbm, wk_hbm, wv_hbm, kv_hbm, c2_hbm, c4_hbm, c8_hbm,
    x_s, wk_s, wv_s, kv_s, c2_s, c4_s, c8_s, in_sems, out_sems,
):
    fetch, store = Copies(in_sems), Copies(out_sems)
    wk = [fetch.start(row_block(wk_hbm, i, SPAN), row_block(wk_s, i, SPAN)) for i in range(2)]
    x = [fetch.start(row_block(x_hbm, i, BLOCK), row_block(x_s, i, BLOCK)) for i in range(2)]
    wv = [fetch.start(row_block(wv_hbm, i, SPAN), row_block(wv_s, i, SPAN)) for i in range(2)]
    x += [fetch.start(row_block(x_hbm, i, BLOCK), row_block(x_s, i, BLOCK)) for i in (2, 3)]
    averages = [run_matrix(BLOCK >> shift, BLOCK, shift, False) for shift in range(4)]
    stores = []
    for half in range(2):
        if half == 0:
            for copy in wk:
                copy.wait()
        for copy in x[2 * half : 2 * half + 2]:
            copy.wait()
        rows = slice(half * SPAN, (half + 1) * SPAN)
        kv_s[rows, :COLS] = dot_nn(x_s[rows], wk_s[...]).astype(bf16)
        if half == 0:
            for copy in wv:
                copy.wait()
        kv_s[rows, COLS:] = dot_nn(x_s[rows], wv_s[...]).astype(bf16)
        for shift, ref, out in ((3, c8_s, c8_hbm), (2, c4_s, c4_hbm), (1, c2_s, c2_hbm)):
            count = BLOCK >> shift
            for index in (2 * half, 2 * half + 1):
                kv = kv_s[index * BLOCK : (index + 1) * BLOCK]
                mean = dot_nn(averages[shift], kv).astype(bf16)
                ref[index * count : (index + 1) * count] = mean
            stores.append(
                store.start(row_block(ref, half, 2 * count), row_block(out, half, 2 * count))
            )
        stores.append(store.start(row_block(kv_s, half, SPAN), row_block(kv_hbm, half, SPAN)))
    for copy in stores:
        copy.wait()


def project_kv(tokens, w_key, w_value):
    outs = [(ROWS >> s, 2 * COLS) for s in range(4)]
    return pl.pallas_call(
        kv_kernel,
        in_specs=[any_spec()] * 3,
        out_specs=[any_spec()] * 4,
        out_shape=[shape(dims) for dims in outs],
        scratch_shapes=[
            pltpu.VMEM((ROWS, WIDTH), bf16),
            pltpu.VMEM((WIDTH, COLS), bf16),
            pltpu.VMEM((WIDTH, COLS), bf16),
        ]
        + [pltpu.VMEM(dims, bf16) for dims in outs]
        + [pltpu.SemaphoreType.DMA((8,)), pltpu.SemaphoreType.DMA((8,))],
        compiler_params=params(60),
        cost_estimate=cost(ROWS * WIDTH * 2 * COLS, 6 * MIB),
        name="project_kv",
    )(tokens, w_key, w_value)


def q_kernel(
    x_hbm, c_hbm, wq_hbm, wo_hbm, q_hbm, da_hbm,
    x_s, c_s, wq_s, wo_s, q_s, da_s, in_sems, out_sems,
):
    fetch, store = Copies(in_sems), Copies(out_sems)
    wq = [fetch.start(row_block(wq_hbm, i, SPAN), row_block(wq_s, i, SPAN)) for i in range(2)]
    x = [fetch.start(row_block(x_hbm, i, SPAN), row_block(x_s, i, SPAN)) for i in range(2)]
    wo = [fetch.start(row_block(wo_hbm, i, 128), row_block(wo_s, i, 128)) for i in range(2)]
    c = [fetch.start(row_block(c_hbm, i, SPAN), row_block(c_s, i, SPAN)) for i in range(2)]
    stores = []
    for weights, inputs, w_s, in_s, out_s, out, dot in (
        (wq, x, wq_s, x_s, q_s, q_hbm, dot_nn),
        (wo, c, wo_s, c_s, da_s, da_hbm, dot_nt),
    ):
        for copy in weights:
            copy.wait()
        for half in range(2):
            inputs[half].wait()
            rows = slice(half * SPAN, (half + 1) * SPAN)
            out_s[rows] = dot(in_s[rows], w_s[...]).astype(bf16)
            stores.append(store.start(row_block(out_s, half, SPAN), row_block(out, half, SPAN)))
    for copy in stores:
        copy.wait()


def project_q(tokens, cotangent, w_query, w_out):
    return pl.pallas_call(
        q_kernel,
        in_specs=[any_spec()] * 4,
        out_specs=[any_spec()] * 2,
        out_shape=[shape((ROWS, COLS))] * 2,
        scratch_shapes=[
            pltpu.VMEM((ROWS, WIDTH), bf16),
            pltpu.VMEM((ROWS, WIDTH), bf16),
            pltpu.VMEM((WIDTH, COLS), bf16),
            pltpu.VMEM((COLS, WIDTH), bf16),
            pltpu.VMEM((ROWS, COLS), bf16),
            pltpu.VMEM((ROWS, COLS), bf16),
            pltpu.SemaphoreType.DMA((8,)),
            pltpu.SemaphoreType.DMA((4,)),
        ],
        compiler_params=params(60),
        cost_estimate=cost(ROWS * WIDTH * 2 * COLS, 7 * MIB),
        name="project_q",
    )(tokens, cotangent, w_query, w_out)


def entry_rows(refs, kb, lo):
    near, c2, l2, l3a, l3b = refs
    if kb < 2:
        return near[kb * BLOCK : (kb + 1) * BLOCK, lo : lo + 128]
    if kb == 2:
        return c2[:, lo : lo + 128]
    if kb == 3:
        return l2[:, lo : lo + 128]
    return jnp.concatenate([l3a[:, lo : lo + 128], l3b[:, lo : lo + 128]], axis=0)


def only_head(ref, head):
    lane = lax.broadcasted_iota(jnp.int32, (SPAN, 128), 1)
    keep = lane < HEAD_DIM if head % 2 == 0 else lane >= HEAD_DIM
    pair = head // 2 * 128
    return jnp.where(keep, ref[:, pair : pair + 128], jnp.zeros((), bf16))


def fold(values, combine):
    return combine(values.reshape(BLOCK // 8, 8, SPAN), axis=0)


def forward_kernel(*refs):
    entries, q_ref, da_ref = refs[:5], refs[5], refs[6]
    ot_ref, stat_ref, qgt_ref, g2_ref, g3a_ref, g3b_ref = refs[7:13]
    k_s, v_s, w_s, vt_s, kt_s, qm_s, dm_s, grad_s = refs[13:]
    step = pl.program_id(0)
    for kb in range(5):
        rows = slice(kb * BLOCK, (kb + 1) * BLOCK)
        for pair in range(2):
            lanes = slice(pair * 128, pair * 128 + 128)
            key = entry_rows(entries, kb, pair * 128)
            value = entry_rows(entries, kb, COLS + pair * 128)
            k_s[rows, lanes] = key
            v_s[rows, lanes] = value
            vt_s[lanes, rows] = value.T
            if kb >= 3:
                kt_s[lanes, (kb - 3) * BLOCK : (kb - 2) * BLOCK] = key.T
    for head in range(4):
        qm_s[head] = only_head(q_ref, head)
        dm_s[head] = only_head(da_ref, head)

    @pl.when(step == 0)
    def _():
        grad_s[...] = jnp.zeros_like(grad_s)

    for pair in range(2):
        lo = pair * 128
        key_grad = value_grad = 0.0
        for side in range(2):
            head = 2 * pair + side
            t = dot_nt(k_s[:, lo : lo + 128], qm_s[head])
            p = dot_nt(v_s[:, lo : lo + 128], dm_s[head])
            tops = []
            for kb in range(5):
                rows = slice(kb * BLOCK, (kb + 1) * BLOCK)
                tops.append(fold(t[rows], jnp.max) * SCORE_SCALE + OFFSETS[kb])
            top = jnp.max(functools.reduce(jnp.maximum, tops), axis=0, keepdims=True)
            total = inner = jnp.zeros((8, SPAN), f32)
            far = []
            for kb in range(5):
                rows = slice(kb * BLOCK, (kb + 1) * BLOCK)
                raised = jnp.exp2(t[rows] * SCORE_SCALE + (OFFSETS[kb] - top))
                w_s[side, rows] = raised.astype(bf16)
                total = total + fold(raised, jnp.sum)
                inner = inner + fold(raised * p[rows], jnp.sum)
                if kb >= 3:
                    far.append((raised, p[rows]))
            total = jnp.sum(total, axis=0, keepdims=True)
            inverse = 1.0 / total
            inner = jnp.sum(inner, axis=0, keepdims=True) * inverse
            mine = slice(head * HEAD_DIM, (head + 1) * HEAD_DIM)
            ot_ref[mine] = (dot_nn(vt_s[mine, :], w_s[side]) * inverse).astype(bf16)
            stat_ref[head : head + 1] = top + jnp.log2(total)
            stat_ref[head + 4 : head + 5] = inner
            weights, scores = [], []
            for raised, p_far in far:
                attention = raised * inverse
                weights.append(attention.astype(bf16))
                scores.append((attention * (p_far - inner)).astype(bf16))
            weights, scores = jnp.concatenate(weights, axis=0), jnp.concatenate(scores, axis=0)
            qgt_ref[mine] = dot_nn(kt_s[mine, :], scores)
            key_grad = key_grad + dot_nn(scores, qm_s[head])
            value_grad = value_grad + dot_nn(weights, dm_s[head])
        grad_s[:, lo : lo + 128] += key_grad
        grad_s[:, COLS + lo : COLS + lo + 128] += value_grad

    @pl.when(step == 1)
    def _():
        for ref, first, count in ((g2_ref, 0, 256), (g3a_ref, 256, 128), (g3b_ref, 384, 128)):
            rows = slice(first, first + count)
            ref[:, :COLS] = (grad_s[rows, :COLS] * INV_ROOT).astype(bf16)
            ref[:, COLS:] = grad_s[rows, COLS:].astype(bf16)


def attend(entries, queries, d_attended):
    part = pl.BlockSpec((SPAN, COLS), lambda i: (i, 0))
    turned = pl.BlockSpec((COLS, SPAN), lambda i: (0, i))
    two = pl.BlockSpec((BLOCK, 2 * COLS), lambda i: (0, 0))
    three = pl.BlockSpec((BLOCK // 2, 2 * COLS), lambda i: (0, 0))
    return pl.pallas_call(
        forward_kernel,
        grid=(2,),
        in_specs=[
            pl.BlockSpec((SPAN, 2 * COLS), lambda i: (i, 0)),
            pl.BlockSpec((BLOCK, 2 * COLS), lambda i: (1 - i, 0)),
            two,
            three,
            three,
            part,
            part,
        ],
        out_specs=[turned, pl.BlockSpec((8, SPAN), lambda i: (0, i)), turned, two, three, three],
        out_shape=[
            shape((COLS, ROWS)),
            shape((8, ROWS), f32),
            shape((COLS, ROWS), f32),
            shape((BLOCK, 2 * COLS)),
            shape((BLOCK // 2, 2 * COLS)),
            shape((BLOCK // 2, 2 * COLS)),
        ],
        scratch_shapes=[
            pltpu.VMEM((KEYS, COLS), bf16),
            pltpu.VMEM((KEYS, COLS), bf16),
            pltpu.VMEM((2, KEYS, SPAN), bf16),
            pltpu.VMEM((COLS, KEYS), bf16),
            pltpu.VMEM((COLS, 2 * BLOCK), bf16),
            pltpu.VMEM((4, SPAN, 128), bf16),
            pltpu.VMEM((4, SPAN, 128), bf16),
            pltpu.VMEM((2 * BLOCK, 2 * COLS), f32),
        ],
        compiler_params=params(60),
        cost_estimate=cost(4 * 4 * 4 * ROWS * KEYS * 64, 6 * MIB),
        name="attend",
    )(*entries, queries, d_attended)


def block_grads(key_rows, value_rows, keys_t, offsets, qm, dm, stat, inner):
    t = dot_nt(key_rows, qm) * SCORE_SCALE
    p = dot_nt(value_rows, dm)
    weights, scores = [], []
    for index, offset in enumerate(offsets):
        rows = slice(index * BLOCK, (index + 1) * BLOCK)
        attention = jnp.exp2(t[rows] + (offset - stat))
        weights.append(attention.astype(bf16))
        scores.append((attention * (p[rows] - inner)).astype(bf16))
    weights, scores = jnp.concatenate(weights, axis=0), jnp.concatenate(scores, axis=0)
    return dot_nn(keys_t, scores), dot_nn(scores, qm), dot_nn(weights, dm)


def near_kernel(near, c2, q_ref, da_ref, stat_ref, part_ref, qgt_ref, own_ref, sib_ref,
                kt_s, qm_s, dm_s):
    refs = (near, c2, None, None, None)
    for kb in range(3):
        rows = slice(kb * BLOCK, (kb + 1) * BLOCK)
        for pair in range(2):
            part = entry_rows(refs, kb, pair * 128)
            kt_s[pair * 128 : pair * 128 + 128, rows] = part.T
    for head in range(4):
        qm_s[head] = only_head(q_ref, head)
        dm_s[head] = only_head(da_ref, head)
    for pair in range(2):
        lo = pair * 128
        key_grad = value_grad = 0.0
        stack = [
            jnp.concatenate([entry_rows(refs, kb, first + lo) for kb in range(3)], axis=0)
            for first in (0, COLS)
        ]
        for side in range(2):
            head = 2 * pair + side
            mine = slice(head * HEAD_DIM, (head + 1) * HEAD_DIM)
            dq, dk, dv = block_grads(
                *stack, kt_s[mine, :], OFFSETS[:3], qm_s[head], dm_s[head],
                stat_ref[head : head + 1], stat_ref[head + 4 : head + 5],
            )
            qgt_ref[mine] = ((part_ref[mine] + dq) * INV_ROOT).astype(bf16)
            key_grad, value_grad = key_grad + dk, value_grad + dv
        key_grad = key_grad * INV_ROOT
        own_ref[:, lo : lo + 128] = key_grad[:SPAN]
        own_ref[:, COLS + lo : COLS + lo + 128] = value_grad[:SPAN]
        sib_ref[:, lo : lo + 128] = key_grad[SPAN:]
        sib_ref[:, COLS + lo : COLS + lo + 128] = value_grad[SPAN:]


def near_grads(key_value, own_2, queries, d_attended, stats, query_part):
    part = pl.BlockSpec((SPAN, COLS), lambda i: (i, 0))
    turned = pl.BlockSpec((COLS, SPAN), lambda i: (0, i))
    near = pl.BlockSpec((SPAN, 2 * COLS), lambda i: (i, 0))
    sibling = pl.BlockSpec((BLOCK, 2 * COLS), lambda i: (1 - i, 0))
    return pl.pallas_call(
        near_kernel,
        grid=(2,),
        in_specs=[near, sibling, part, part, pl.BlockSpec((8, SPAN), lambda i: (0, i)), turned],
        out_specs=[turned, near, sibling],
        out_shape=[
            shape((COLS, ROWS)),
            shape((ROWS, 2 * COLS), f32),
            shape((SPAN, 2 * COLS), f32),
        ],
        scratch_shapes=[
            pltpu.VMEM((COLS, 3 * BLOCK), bf16),
            pltpu.VMEM((4, SPAN, 128), bf16),
            pltpu.VMEM((4, SPAN, 128), bf16),
        ],
        compiler_params=params(60),
        cost_estimate=cost(4 * 5 * 4 * ROWS * 3 * BLOCK * 64, 8 * MIB),
        name="near_grads",
    )(key_value, own_2, queries, d_attended, stats, query_part)


def split_product(matrix, values):
    high = values.astype(bf16)
    low = (values - high.astype(f32)).astype(bf16)
    return dot_nn(matrix, high) + dot_nn(matrix, low)


def ring_columns(half):
    return (2, 3, 1, 0) if half == 0 else (1, 2, 3, 0)


def column_group(here, offset):
    return pl.ds(pl.multiple_of(((here + offset) & 3) * COLS, COLS), COLS)


def out_kernel(at_ref, ot_ref, w_ref, right_ref, left_ref, hold_ref, mine_ref):
    outs = (right_ref, left_ref, hold_ref, mine_ref)
    for half in range(2):
        rows = slice(half * SPAN, (half + 1) * SPAN)
        attended = ot_ref[:, rows].T
        for offset, ref in zip(ring_columns(half), outs):
            part = dot_nn(attended, w_ref[:, column_group(at_ref[1], offset)])
            ref[rows] = part.astype(bf16)


def project_out(at, attended_t, w_out):
    vmem = pl.BlockSpec(memory_space=pltpu.VMEM)
    return pl.pallas_call(
        out_kernel,
        in_specs=[pl.BlockSpec(memory_space=pltpu.SMEM), vmem, vmem],
        out_specs=[vmem] * 4,
        out_shape=[shape((ROWS, COLS))] * 4,
        compiler_params=params(24),
        cost_estimate=cost(ROWS * WIDTH * COLS, 4 * MIB),
        name="project_out",
    )(at, attended_t, w_out)


def shifted(value, by):
    size = lax.axis_size("head")
    return lax.ppermute(value, "head", [(i, (i + by) % size) for i in range(size)])


def swapped(value, bits):
    return lax.ppermute(value, "seq", [(i, i ^ bits) for i in range(lax.axis_size("seq"))])


def add(*terms):
    return sum(term.astype(f32) for term in terms).astype(bf16)


def head_sum_first(right, left, hold, mine):
    return shifted(right, 1), shifted(left, -1)


def head_sum_second(got_right, got_left, right, left, hold, mine):
    half = ROWS // 2
    more_right = shifted(add(hold[:half], got_right[:half]), 1)
    more_left = shifted(add(hold[half:], got_left[half:]), -1)
    return more_right, more_left


def head_sum_last(more_right, more_left, got_right, got_left, right, left, hold, mine):
    half = ROWS // 2
    return jnp.concatenate(
        [
            add(mine[:half], got_left[:half], more_right),
            add(mine[half:], got_right[half:], more_left),
        ],
        axis=0,
    )


def head_sum(*parts):
    got = head_sum_first(*parts)
    more = head_sum_second(*got, *parts)
    return head_sum_last(*more, *got, *parts)


def tail_kernel(
    at_ref, own_hbm, sib_hbm, got2_hbm, got3_hbm, qgt_hbm, ot_hbm, x_hbm, c_hbm,
    wq_hbm, wk_hbm, wv_hbm, right_hbm, left_hbm, hold_hbm, stay_hbm, mine_hbm, other_hbm,
    own_s, sib_s, got2_s, got3_s, qgt_s, ot_s, x_s, c_s, wq_s, wk_s, wv_s,
    part_s, kvg_s, g_s, in_sems, out_sems,
):
    core = at_ref[0]
    fetch, store = Copies(in_sems), Copies(out_sems)

    def halves(source, target):
        count = source.shape[0] // 2
        return [
            fetch.start(row_block(source, i, count), row_block(target, i, count)) for i in range(2)
        ]

    def wait(*copies):
        for copy in copies:
            copy.wait()

    ot = halves(ot_hbm, ot_s)
    c = halves(c_hbm, c_s)
    qgt = halves(qgt_hbm, qgt_s)
    x = halves(x_hbm, x_s)
    got = halves(got2_hbm, got2_s) + halves(got3_hbm, got3_s)
    sib = halves(sib_hbm, sib_s)
    own = halves(own_hbm, own_s)
    wq, wk, wv = halves(wq_hbm, wq_s), halves(wk_hbm, wk_s), halves(wv_hbm, wv_s)
    stores = []

    def finish(index, grad_t):
        g_s[index] = grad_t.astype(bf16).T.reshape(32, 2, 16, COLS)
        rows = pl.ds(index * 16, 16)
        stores.append(store.start(g_s.at[index, :, 1 - core], other_hbm.at[:, rows]))
        stores.append(store.start(g_s.at[index, :, core], mine_hbm.at[:, rows]))

    wait(*ot, *c)
    finish(0, dot_nn(ot_s[...], c_s[...]))
    wait(*qgt, *x)
    finish(1, dot_nn(qgt_s[...], x_s[...]))
    wait(*got, *sib)
    spread2 = run_matrix(SPAN, SPAN >> 1, 1, True)
    spread4 = run_matrix(SPAN, SPAN >> 2, 2, True)
    spread8 = run_matrix(SPAN, SPAN >> 3, 3, True)
    for half in range(2):
        own[half].wait()
        rows = slice(half * SPAN, (half + 1) * SPAN)
        total = own_s[rows] + split_product(spread2, sib_s[half * 256 : half * 256 + 256])
        total = total + dot_nn(spread4, got2_s[half * 128 : half * 128 + 128])
        total = total + dot_nn(spread8, got3_s[half * 64 : half * 64 + 64])
        kvg_s[rows] = total.astype(bf16)
    for index in range(2):
        finish(2 + index, dot_nn(kvg_s[:, index * COLS : (index + 1) * COLS].T, x_s[...]))
    wait(*wq, *wk, *wv)
    outs = (right_hbm, left_hbm, hold_hbm, stay_hbm)
    for half in range(2):
        rows = slice(half * SPAN, (half + 1) * SPAN)
        query_grad = qgt_s[:, rows].T
        for index, (offset, out) in enumerate(zip(ring_columns(half), outs)):
            cols = column_group(at_ref[1], offset)
            part = dot_nt(query_grad, wq_s[cols, :])
            part = part + dot_nt(kvg_s[rows, :COLS], wk_s[cols, :])
            part = part + dot_nt(kvg_s[rows, COLS:], wv_s[cols, :])
            part_s[index, rows] = part.astype(bf16)
            stores.append(
                store.start(part_s.at[index, pl.ds(half * SPAN, SPAN)], row_block(out, half, SPAN))
            )
    wait(*stores)


def tail(at, *operands):
    dims = [operand.shape for operand in operands]
    return pl.pallas_call(
        tail_kernel,
        in_specs=[pl.BlockSpec(memory_space=pltpu.SMEM)] + [any_spec()] * len(operands),
        out_specs=[any_spec()] * 6,
        out_shape=[shape((ROWS, COLS))] * 4 + [shape((32, 64, COLS))] * 2,
        scratch_shapes=[pltpu.VMEM(o.shape, o.dtype) for o in operands]
        + [
            pltpu.VMEM((4, ROWS, COLS), bf16),
            pltpu.VMEM((ROWS, 2 * COLS), bf16),
            pltpu.VMEM((4, 32, 2, 16, COLS), bf16),
            pltpu.SemaphoreType.DMA((2 * len(dims),)),
            pltpu.SemaphoreType.DMA((16,)),
        ],
        compiler_params=params(60),
        cost_estimate=cost(7 * ROWS * WIDTH * COLS, 14 * MIB),
        name="tail",
    )(at, *operands)


def seq_sum(mine, got):
    size = lax.axis_size("seq")
    along_x = [list(range(first, size, 16)) for first in range(16)]
    along_z = [list(range(16 * x + core, 16 * x + 16, 2)) for x in range(4) for core in range(2)]
    blocks = add(mine, got).reshape(4, 8, 64, COLS)
    blocks = lax.all_to_all(blocks, "seq", 0, 0, axis_index_groups=along_x)
    blocks = jnp.sum(blocks.astype(f32), axis=0).astype(bf16)
    blocks = lax.all_to_all(blocks, "seq", 0, 0, axis_index_groups=along_z)
    return jnp.sum(blocks.astype(f32), axis=0)


def on_device(tokens, cotangent, w_query, w_key, w_value, w_out):
    at = jnp.stack([lax.axis_index("seq") % 2, lax.axis_index("head")]).astype(jnp.int32)
    key_value, own_2, own_4, own_8 = project_kv(tokens, w_key, w_value)
    three_a = swapped(own_8, 2)
    level_two = swapped(own_4, 1)
    queries, d_attended = project_q(tokens, cotangent, w_query, w_out)
    queries, three_a = lax.optimization_barrier((queries, three_a))
    three_b = swapped(three_a, 1)
    entries = (key_value, own_2, level_two, three_a, three_b)
    attended_t, stats, query_part, grad_2, grad_3a, grad_3b = attend(
        entries, queries, d_attended
    )
    got_2 = swapped(grad_2, 1)
    got_3b = swapped(grad_3b, 1)
    out_parts = project_out(at, attended_t, w_out)
    out_got = head_sum_first(*out_parts)
    grad_3 = add(grad_3a, got_3b)
    near = (key_value, own_2, queries, d_attended, stats, query_part)
    near, out_parts, grad_3 = lax.optimization_barrier((near, out_parts, grad_3))
    got_3 = swapped(grad_3, 2)
    near = near_grads(*near)
    near, out_got = lax.optimization_barrier((near, out_got))
    out_more = head_sum_second(*out_got, *out_parts)
    query_grad_t, own, sibling = near
    *parts, mine, other = tail(
        at, own, sibling, got_2, got_3, query_grad_t, attended_t, tokens, cotangent,
        w_query, w_key, w_value,
    )
    (parts, mine, other), out_more = lax.optimization_barrier(((parts, mine, other), out_more))
    layer_out = head_sum_last(*out_more, *out_got, *out_parts)
    grad_tokens = head_sum(*parts)
    scale = 1.0 / math.sqrt(lax.axis_size("seq") * tokens.shape[0])
    summed = seq_sum(mine, swapped(other, 1)) * scale
    return (
        layer_out,
        grad_tokens,
        summed[16:32],
        summed[32:48],
        summed[48:],
        summed[:16].T,
    )


def solution(mesh):
    return jax.shard_map(
        on_device,
        mesh=mesh,
        in_specs=(
            P("seq", None),
            P("seq", None),
            P(None, "head"),
            P(None, "head"),
            P(None, "head"),
            P("head", None),
        ),
        out_specs=(
            P("seq", "head"),
            P("seq", "head"),
            P("seq", "head"),
            P("seq", "head"),
            P("seq", "head"),
            P("head", "seq"),
        ),
        check_vma=False,
    )
```

time: 127 us -> 114 us (0.90)
  between operations: 14.3 us -> 0.79 us
  Pallas kernels: 62.5 us -> 51.5 us
  other arithmetic: 0.75 us -> 11 us
  waiting for transfers between devices: 22.5 us -> 18.5 us
  starting transfers between devices: 23.6 us -> 27.4 us
    pallas_call x6 -> x1, Pallas kernels: 14.4 us -> 1.29 us  [project_out(): pl.pallas_call(out_kernel, in_specs=[pl.BlockSpec(memory_space=pltpu.SMEM...]
    ppermute x10 -> x7, starting transfers between devices: 16.5 us -> 3.81 us  [swapped(): lax.ppermute(value, 'seq', [(i, i ^ bits) for i in range(lax.axis_size('s...]
    all_to_all x0 -> x2, starting transfers between devices: none -> 12 us  [the longest x1 7.75 us: seq_sum(): blocks = lax.all_to_all(blocks, 'seq', 0, 0, axis_index_groups=along_z)]
    all_to_all x0 -> x2, waiting for transfers between devices: none -> 11.1 us  [the longest x1 7.77 us: seq_sum(): blocks = lax.all_to_all(blocks, 'seq', 0, 0, axis_index_groups=along_z)]
    ppermute x10 -> x7, waiting for transfers between devices: 11.1 us -> 1 us  [swapped(): lax.ppermute(value, 'seq', [(i, i ^ bits) for i in range(lax.axis_size('s...]
    convert_element_type x3 -> x6, other arithmetic: 0.1 us -> 8.35 us  [add(): return sum((term.astype(f32) for term in terms)).astype(bf16)]
    ppermute x4 -> x8, waiting for transfers between devices: 11.4 us -> 6.43 us  [shifted(): lax.ppermute(value, 'head', [(i, (i + by) % size) for i in range(size)])]
    ppermute x4 -> x8, starting transfers between devices: 7.03 us -> 11.5 us  [shifted(): lax.ppermute(value, 'head', [(i, (i + by) % size) for i in range(size)])]
  transfers between devices with their start and end apart: 16 -> 17, of which waited for: 9 -> 5; matrix products, arithmetic and copies ran while one was open for 1% -> 10% of each run, Pallas kernels for 25% -> 24%
where the time goes in v3:
time: 114 us
  Pallas kernels  51.5 us (45%)
  starting transfers between devices  27.4 us (24%)
  waiting for transfers between devices  18.5 us (16%)
  other arithmetic  11 us (10%)
  local copies, waits for them, and re-layouts  4.48 us (4%)
    pallas_call x1, Pallas kernels, attend(): pl.pallas_call(forward_kernel, grid=(2,), in_specs=[pl.BlockSpec((SPAN, 2...  19 us
    ppermute x8, starting transfers between devices, shifted(): lax.ppermute(value, 'head', [(i, (i + by) % size) for i in range(size)])  11.5 us
    pallas_call x1, Pallas kernels, near_grads(): pl.pallas_call(near_kernel, grid=(2,), in_specs=[near, sibling, part, par...  11.3 us
    pallas_call x1, Pallas kernels, tail(): pl.pallas_call(tail_kernel, in_specs=[pl.BlockSpec(memory_space=pltpu.SME...  9.72 us
    convert_element_type x6, other arithmetic, add(): return sum((term.astype(f32) for term in terms)).astype(bf16)  8.35 us
    all_to_all x1, waiting for transfers between devices, seq_sum(): blocks = lax.all_to_all(blocks, 'seq', 0, 0, axis_index_groups=along_z)  7.77 us
    all_to_all x1, starting transfers between devices, seq_sum(): blocks = lax.all_to_all(blocks, 'seq', 0, 0, axis_index_groups=along_z)  7.75 us
    ppermute x8, waiting for transfers between devices, shifted(): lax.ppermute(value, 'head', [(i, (i + by) % size) for i in range(size)])  6.43 us
  transfers between devices with their start and end apart: 17, of which 5 were waited for; matrix products, arithmetic and copies ran while one was open for 10% of the time, Pallas kernels for 24%

profile of v3, /device:TPU:24, one launch (start us, length us, event | category | flops | bytes accessed | tf_op | source)
XLA Modules:
  0.0 113.7 jit_solution(17131686502054027574)
XLA Ops:
  0.6 5.2 %project_kv.1 = (bf16[1024,512]{1,0:T(8,128)(2,1)}, bf16[512,512]{1,0:T(8,128)(2,1)}, bf16[256,512]{1,0:T(8,128)(2,1)}, bf16[128,512]{1,0:T(8,128)(2,1)}) custom-call(bf16[1024,1024]{1,0:T(8,128)(2,1)} %x_hbm.5, bf16[1024,256]{1,0:T(8,128)(2,1)} %wk_hbm.3, bf16[1024,256]{1,0:T(8,128)(2,1)} %wv_hbm.3), custom_call_target="tpu_custom_call" | custom-call | flops 1073741824 | bytes 6291456 | tf_op jit(solution)/shard_map/project_kv/pallas_call | solution.py:112
  5.8 2.0 %collective-permute-start = (bf16[128,512]{1,0:T(8,128)(2,1)}, bf16[128,512]{1,0:T(8,128)(2,1)S(1)}, u32[]{:S(2)}, u32[]{:S(2)}) collective-permute-start(bf16[128,512]{1,0:T(8,128)(2,1)} %get-tuple-element.58), channel_id=1, source_target_pairs={{0,8},{4,12},{8,0},{12,4},{16,24},{20,28},{24,16},{28,20},{32,40},... | collective-permute-start | bytes 393224 | tf_op jit(solution)/shard_map/ppermute | solution.py:430
  7.8 5.0 %project_q.1 = (bf16[1024,256]{1,0:T(8,128)(2,1)}, bf16[1024,256]{1,0:T(8,128)(2,1)}) custom-call(bf16[1024,1024]{1,0:T(8,128)(2,1)} %x_hbm.5, bf16[1024,1024]{1,0:T(8,128)(2,1)} %c_hbm.3, bf16[1024,256]{1,0:T(8,128)(2,1)} %wq_hbm.3, bf16[256,1024]{1,0:T(8,128)(2,1)} %w_ref.1), custom_call_target="tpu_custom_call" | custom-call | flops 1073741824 | bytes 7340032 | tf_op jit(solution)/shard_map/project_q/pallas_call | solution.py:156
  13.6 1.0 collective-permute-done.2.refs_4_
  15.4 19.0 %attend.1 = (bf16[256,1024]{1,0:T(8,128)(2,1)}, f32[8,1024]{1,0:T(8,128)}, f32[256,1024]{1,0:T(8,128)}, bf16[256,512]{1,0:T(8,128)(2,1)}, bf16[128,512]{1,0:T(8,128)(2,1)}, /*index=5*/bf16[128,512]{1,0:T(8,128)(2,1)}) custom-call(bf16[1024,512]{1,0:T(8,128)(2,1)} %get-tuple-element.73.refs_0_.near, bf16[512,512]{1,0:T(8,128)(2,1)} %get-tuple-element.74.refs_1_.c2, ...), custom_call_target="tpu_custom_call" | custom-call | flops 10737418240 | bytes 6291456 | tf_op jit(solution)/shard_map/attend/pallas_call | solution.py:277
  35.1 1.0 copy-done.2
  36.1 1.3 %project_out.1 = (bf16[1024,256]{1,0:T(8,128)(2,1)S(1)}, bf16[1024,256]{1,0:T(8,128)(2,1)S(1)}, bf16[1024,256]{1,0:T(8,128)(2,1)S(1)}, bf16[1024,256]{1,0:T(8,128)(2,1)S(1)}) custom-call(s32[2]{0:T(128)S(1)} %pad_add_fusion.at_ref, bf16[256,1024]{1,0:T(8,128)(2,1)S(1)} %copy-done.2, bf16[256,1024]{1,0:T(8,128)(2,1)S(1)} %copy-done), custom_call_target="tpu_custom_call" | custom-call | flops 536870912 | bytes 4194304 | tf_op jit(solution)/shard_map/project_out/pallas_call | solution.py:413
  37.7 1.8 %collective-permute-start.5 = (bf16[1024,256]{1,0:T(8,128)(2,1)S(1)}, bf16[1024,256]{1,0:T(8,128)(2,1)S(1)}, u32[]{:S(2)}, u32[]{:S(2)}) collective-permute-start(bf16[1024,256]{1,0:T(8,128)(2,1)S(1)} %get-tuple-element.67), channel_id=1, source_target_pairs={{0,3},{1,0},{2,1},{3,2},{4,7},{5,4},{6,5},{7,6},{8,11},{9,8},{10,9... | collective-permute-start | bytes 1572872 | tf_op jit(solution)/shard_map/ppermute | solution.py:426
  39.5 0.9 add_convert_fusion.9
  40.9 11.3 %near_grads.1 = (bf16[256,1024]{1,0:T(8,128)(2,1)}, f32[1024,512]{1,0:T(8,128)}, f32[512,512]{1,0:T(8,128)}) custom-call(bf16[1024,512]{1,0:T(8,128)(2,1)} %get-tuple-element.73.refs_0_.near, bf16[512,512]{1,0:T(8,128)(2,1)} %get-tuple-element.74.refs_1_.c2, bf16[1024,256]{1,0:T(8,128)(2,1)} %get-tuple-element.75.refs_5_.q_ref, ...), custom_call_target="tpu_custom_call" | custom-call | flops 8053063680 | bytes 8388608 | tf_op jit(solution)/shard_map/near_grads/pallas_call | solution.py:366
  53.6 2.8 %collective-permute-start.8 = (bf16[512,256]{1,0:T(8,128)(2,1)S(1)}, bf16[512,256]{1,0:T(8,128)(2,1)S(1)}, u32[]{:S(2)}, u32[]{:S(2)}) collective-permute-start(bf16[512,256]{1,0:T(8,128)(2,1)S(1)} %get-tuple-element.111), channel_id=1, source_target_pairs={{0,1},{1,2},{2,3},{3,0},{4,5},{5,6},{6,7},{7,4},{8,9},{9,10},{10,1... | collective-permute-start | bytes 786440 | tf_op jit(solution)/shard_map/ppermute | solution.py:426
  57.7 9.7 %tail.1 = (bf16[1024,256]{1,0:T(8,128)(2,1)}, bf16[1024,256]{1,0:T(8,128)(2,1)}, bf16[1024,256]{1,0:T(8,128)(2,1)}, bf16[1024,256]{1,0:T(8,128)(2,1)}, bf16[32,6...) custom-call(s32[2]{0:T(128)} %copy-done.1, f32[1024,512]{1,0:T(8,128)} %get-tuple-element.83.own_hbm, ...), custom_call_target="tpu_custom_call" | custom-call | flops 3758096384 | bytes 14680064 | tf_op jit(solution)/shard_map/tail/pallas_call | solution.py:536
  68.2 3.2 %collective-permute-start.11 = (bf16[1024,256]{1,0:T(8,128)(2,1)}, bf16[1024,256]{1,0:T(8,128)(2,1)}, u32[]{:S(2)}, u32[]{:S(2)}) collective-permute-start(bf16[1024,256]{1,0:T(8,128)(2,1)} %get-tuple-element.101), channel_id=1, source_target_pairs={{0,1},{1,2},{2,3},{3,0},{4,5},{5,6},{6,7},{7,4},{8,9},{9,10},{10,1... | collective-permute-start | bytes 1572872 | tf_op jit(solution)/shard_map/ppermute | solution.py:426
  71.5 2.6 %add_convert_fusion = bf16[32,64,256]{2,1,0:T(8,128)(2,1)} fusion(bf16[32,64,256]{2,1,0:T(8,128)(2,1)S(1)} %collective-permute-done.14, bf16[32,64,256]{2,1,0:T(8,128)(2,1)} %get-tuple-element.102), kind=kLoop, calls=%fused_computation | loop fusion | flops 2097152 | bytes 3145728 | tf_op jit(solution)/shard_map/convert_element_type | solution.py:434
  74.0 4.3 %all-to-all-start = ((bf16[4,8,64,256]{3,2,1,0:T(8,128)(2,1)}), bf16[4,8,64,256]{3,2,1,0:T(8,128)(2,1)S(1)}, u32[]{:S(2)}, u32[]{:S(2)}) async-start(bf16[4,8,64,256]{3,2,1,0:T(8,128)(2,1)} %bitcast.2), calls=%async_computation | async-start | bytes 2097152 | tf_op jit(solution)/shard_map/all_to_all | solution.py:560
  78.3 5.7 %collective-permute-done.10 = bf16[1024,256]{1,0:T(8,128)(2,1)S(1)} collective-permute-done((bf16[1024,256]{1,0:T(8,128)(2,1)}, bf16[1024,256]{1,0:T(8,128)(2,1)S(1)}, u32[]{:S(2)}, u32[]{:S(2)}) %collective-permute-start.10) | collective-permute-done | bytes 524320 | tf_op jit(solution)/shard_map/ppermute | solution.py:426
  84.0 2.0 %add_convert_fusion.4 = (bf16[512,256]{1,0:T(8,128)(2,1)}, bf16[512,256]{1,0:T(8,128)(2,1)S(1)}) fusion(bf16[1024,256]{1,0:T(8,128)(2,1)} %collective-permute-done.11, bf16[1024,256]{1,0:T(8,128)(2,1)S(1)} %copy-done.3, bf16[1024,256]{1,0:T(8,128)(2,1)S(1)} %collective-permute-done.10), kind=kLoop, calls=%fused_computation.7 | loop fusion | flops 1048576 | bytes 1572864 | tf_op jit(solution)/shard_map/convert_element_type | solution.py:434
  86.0 2.9 %collective-permute-start.12 = (bf16[512,256]{1,0:T(8,128)(2,1)}, bf16[512,256]{1,0:T(8,128)(2,1)}, u32[]{:S(2)}, u32[]{:S(2)}) collective-permute-start(bf16[512,256]{1,0:T(8,128)(2,1)} %get-tuple-element.106), channel_id=1, source_target_pairs={{0,1},{1,2},{2,3},{3,0},{4,5},{5,6},{6,7},{7,4},{8,9},{9,10},{10,1... | collective-permute-start | bytes 786440 | tf_op jit(solution)/shard_map/ppermute | solution.py:426
  88.8 1.4 %add_convert_fusion.6 = (bf16[512,256]{1,0:T(8,128)(2,1)S(1)}, bf16[512,256]{1,0:T(8,128)(2,1)S(1)}) fusion(bf16[512,256]{1,0:T(8,128)(2,1)} %copy-done.7, bf16[1024,256]{1,0:T(8,128)(2,1)} %copy-done.5, bf16[1024,256]{1,0:T(8,128)(2,1)S(1)} %get-tuple-element.72, bf16[512,256]{1,0:T(8,128)(2,1)} %collective-permute-done.9, ...), kind=kLoop, calls=%fused_computation.9 | loop fusion | flops 1572864 | bytes 2097152 | tf_op jit(solution)/shard_map/convert_element_type | solution.py:434
  90.2 3.3 %all-to-all-done = bf16[4,8,64,256]{3,2,1,0:T(8,128)(2,1)S(1)} async-done(((bf16[4,8,64,256]{3,2,1,0:T(8,128)(2,1)}), bf16[4,8,64,256]{3,2,1,0:T(8,128)(2,1)S(1)}, u32[]{:S(2)}, u32[]{:S(2)}) %all-to-all-start) | async-done | bytes 1048608 | tf_op jit(solution)/shard_map/all_to_all | solution.py:560
  93.5 0.9 reduce_sum.21
  94.4 7.7 %all-to-all-start.1 = ((bf16[8,64,256]{2,1,0:T(8,128)(2,1)}), bf16[8,64,256]{2,1,0:T(8,128)(2,1)S(1)}, u32[]{:S(2)}, u32[]{:S(2)}) async-start(bf16[8,64,256]{2,1,0:T(8,128)(2,1)} %reduce_sum.21), calls=%async_computation.1 | async-start | bytes 524288 | tf_op jit(solution)/shard_map/all_to_all | solution.py:562
  103.0 1.4 %add_convert_fusion.3 = (bf16[512,256]{1,0:T(8,128)(2,1)S(1)}, bf16[512,256]{1,0:T(8,128)(2,1)S(1)}) fusion(bf16[512,256]{1,0:T(8,128)(2,1)} %collective-permute-done.12, bf16[1024,256]{1,0:T(8,128)(2,1)} %copy-done.6, bf16[1024,256]{1,0:T(8,128)(2,1)S(1)} %copy-done.4, bf16[512,256]{1,0:T(8,128)(2,1)} %collective-permute-done.13, ...), kind=kLoop, calls=%fused_computation.6 | loop fusion | flops 1572864 | bytes 2097152 | tf_op jit(solution)/shard_map/convert_element_type | solution.py:434
  105.2 7.8 %all-to-all-done.1 = bf16[8,64,256]{2,1,0:T(8,128)(2,1)S(1)} async-done(((bf16[8,64,256]{2,1,0:T(8,128)(2,1)}), bf16[8,64,256]{2,1,0:T(8,128)(2,1)S(1)}, u32[]{:S(2)}, u32[]{:S(2)}) %all-to-all-start.1) | async-done | bytes 262176 | tf_op jit(solution)/shard_map/all_to_all | solution.py:562
  (55 shorter events, 8.8 us)
Async XLA Ops:
  5.8 7.0 %collective-permute-start = (bf16[128,512]{1,0:T(8,128)(2,1)}, bf16[128,512]{1,0:T(8,128)(2,1)S(1)}, u32[]{:S(2)}, u32[]{:S(2)}) collective-permute-start(bf16[128,512]{1,0:T(8,128)(2,1)} %get-tuple-element.58), channel_id=1, source_target_pairs={{0,8},{4,12},{8,0},{12,4},{16,24},{20,28},{24,16},{28,20},{32,40},... | collective-permute-start | bytes 393224 | tf_op jit(solution)/shard_map/ppermute | solution.py:430
  7.8 6.8 %collective-permute-start.1 = (bf16[256,512]{1,0:T(8,128)(2,1)}, bf16[256,512]{1,0:T(8,128)(2,1)S(1)}, u32[]{:S(2)}, u32[]{:S(2)}) collective-permute-start(bf16[256,512]{1,0:T(8,128)(2,1)} %get-tuple-element.61), channel_id=1, source_target_pairs={{0,4},{4,0},{8,12},{12,8},{16,20},{20,16},{24,28},{28,24},{32,36},... | collective-permute-start | bytes 786440 | tf_op jit(solution)/shard_map/ppermute | solution.py:430
  12.8 1.8 %copy-start.10 = (bf16[128,512]{1,0:T(8,128)(2,1)}, bf16[128,512]{1,0:T(8,128)(2,1)S(1)}, u32[]{:S(2)}) copy-start(bf16[128,512]{1,0:T(8,128)(2,1)S(1)} %collective-permute-done.refs_3_) | copy-start | bytes 393220
  12.9 1.8 %collective-permute-start.2 = (bf16[128,512]{1,0:T(8,128)(2,1)S(1)}, bf16[128,512]{1,0:T(8,128)(2,1)S(1)}, u32[]{:S(2)}, u32[]{:S(2)}) collective-permute-start(bf16[128,512]{1,0:T(8,128)(2,1)S(1)} %collective-permute-done.refs_3_), channel_id=1, source_target_pairs={{0,4},{4,0},{8,12},{12,8},{16,20},{20,16},{24,28},{28,24},{32,36},... | collective-permute-start | bytes 393224 | tf_op jit(solution)/shard_map/ppermute | solution.py:430
  15.4 19.7 %copy-start = (bf16[256,1024]{1,0:T(8,128)(2,1)S(1)}, bf16[256,1024]{1,0:T(8,128)(2,1)}, u32[]{:S(2)}) copy-start(bf16[256,1024]{1,0:T(8,128)(2,1)} %w_ref.1) | copy-start | bytes 1572868
  34.3 5.2 %collective-permute-start.3 = (bf16[128,512]{1,0:T(8,128)(2,1)}, bf16[128,512]{1,0:T(8,128)(2,1)S(1)}, u32[]{:S(2)}, u32[]{:S(2)}) collective-permute-start(bf16[128,512]{1,0:T(8,128)(2,1)} %get-tuple-element.71), channel_id=1, source_target_pairs={{0,4},{4,0},{8,12},{12,8},{16,20},{20,16},{24,28},{28,24},{32,36},... | collective-permute-start | bytes 393224 | tf_op jit(solution)/shard_map/ppermute | solution.py:430
  34.9 17.3 %copy-start.1 = (s32[2]{0:T(128)}, s32[2]{0:T(128)S(1)}, u32[]{:S(2)}) copy-start(s32[2]{0:T(128)S(1)} %pad_add_fusion.at_ref) | copy-start | bytes 28
  34.9 21.5 %collective-permute-start.6 = (bf16[256,512]{1,0:T(8,128)(2,1)}, bf16[256,512]{1,0:T(8,128)(2,1)S(1)}, u32[]{:S(2)}, u32[]{:S(2)}) collective-permute-start(bf16[256,512]{1,0:T(8,128)(2,1)} %get-tuple-element.85), channel_id=1, source_target_pairs={{0,4},{4,0},{8,12},{12,8},{16,20},{20,16},{24,28},{28,24},{32,36},... | collective-permute-start | bytes 786440 | tf_op jit(solution)/shard_map/ppermute | solution.py:430
  37.4 14.8 %collective-permute-start.4 = (bf16[1024,256]{1,0:T(8,128)(2,1)S(1)}, bf16[1024,256]{1,0:T(8,128)(2,1)S(1)}, u32[]{:S(2)}, u32[]{:S(2)}) collective-permute-start(bf16[1024,256]{1,0:T(8,128)(2,1)S(1)} %get-tuple-element.66), channel_id=1, source_target_pairs={{0,1},{1,2},{2,3},{3,0},{4,5},{5,6},{6,7},{7,4},{8,9},{9,10},{10,1... | collective-permute-start | bytes 1572872 | tf_op jit(solution)/shard_map/ppermute | solution.py:426
  37.7 15.3 %collective-permute-start.5 = (bf16[1024,256]{1,0:T(8,128)(2,1)S(1)}, bf16[1024,256]{1,0:T(8,128)(2,1)S(1)}, u32[]{:S(2)}, u32[]{:S(2)}) collective-permute-start(bf16[1024,256]{1,0:T(8,128)(2,1)S(1)} %get-tuple-element.67), channel_id=1, source_target_pairs={{0,3},{1,0},{2,1},{3,2},{4,7},{5,4},{6,5},{7,6},{8,11},{9,8},{10,9... | collective-permute-start | bytes 1572872 | tf_op jit(solution)/shard_map/ppermute | solution.py:426
  40.4 16.0 %collective-permute-start.7 = (bf16[128,512]{1,0:T(8,128)(2,1)S(1)}, bf16[128,512]{1,0:T(8,128)(2,1)S(1)}, u32[]{:S(2)}, u32[]{:S(2)}) collective-permute-start(bf16[128,512]{1,0:T(8,128)(2,1)S(1)} %add_convert_fusion.9), channel_id=1, source_target_pairs={{0,8},{4,12},{8,0},{12,4},{16,24},{20,28},{24,16},{28,20},{32,40},... | collective-permute-start | bytes 393224 | tf_op jit(solution)/shard_map/ppermute | solution.py:430
  52.9 14.5 %copy-start.5 = (bf16[1024,256]{1,0:T(8,128)(2,1)}, bf16[1024,256]{1,0:T(8,128)(2,1)S(1)}, u32[]{:S(2)}) copy-start(bf16[1024,256]{1,0:T(8,128)(2,1)S(1)} %collective-permute-done.5) | copy-start | bytes 1572868
  53.1 14.4 %collective-permute-start.9 = (bf16[512,256]{1,0:T(8,128)(2,1)S(1)}, bf16[512,256]{1,0:T(8,128)(2,1)}, u32[]{:S(2)}, u32[]{:S(2)}) collective-permute-start(bf16[512,256]{1,0:T(8,128)(2,1)S(1)} %get-tuple-element.110), channel_id=1, source_target_pairs={{0,3},{1,0},{2,1},{3,2},{4,7},{5,4},{6,5},{7,6},{8,11},{9,8},{10,9... | collective-permute-start | bytes 786440 | tf_op jit(solution)/shard_map/ppermute | solution.py:426
  53.6 13.9 %collective-permute-start.8 = (bf16[512,256]{1,0:T(8,128)(2,1)S(1)}, bf16[512,256]{1,0:T(8,128)(2,1)S(1)}, u32[]{:S(2)}, u32[]{:S(2)}) collective-permute-start(bf16[512,256]{1,0:T(8,128)(2,1)S(1)} %get-tuple-element.111), channel_id=1, source_target_pairs={{0,1},{1,2},{2,3},{3,0},{4,5},{5,6},{6,7},{7,4},{8,9},{9,10},{10,1... | collective-permute-start | bytes 786440 | tf_op jit(solution)/shard_map/ppermute | solution.py:426
  68.2 15.8 %copy-start.3 = (bf16[1024,256]{1,0:T(8,128)(2,1)S(1)}, bf16[1024,256]{1,0:T(8,128)(2,1)}, u32[]{:S(2)}) copy-start(bf16[1024,256]{1,0:T(8,128)(2,1)} %get-tuple-element.100) | copy-start | bytes 1572868
  68.2 3.2 %collective-permute-start.14 = (bf16[32,64,256]{2,1,0:T(8,128)(2,1)}, bf16[32,64,256]{2,1,0:T(8,128)(2,1)S(1)}, u32[]{:S(2)}, u32[]{:S(2)}) collective-permute-start(bf16[32,64,256]{2,1,0:T(8,128)(2,1)} %get-tuple-element.103), channel_id=1, source_target_pairs={{0,4},{4,0},{8,12},{12,8},{16,20},{20,16},{24,28},{28,24},{32,36},... | collective-permute-start | bytes 3145736 | tf_op jit(solution)/shard_map/ppermute | solution.py:430
  68.2 15.8 %collective-permute-start.10 = (bf16[1024,256]{1,0:T(8,128)(2,1)}, bf16[1024,256]{1,0:T(8,128)(2,1)S(1)}, u32[]{:S(2)}, u32[]{:S(2)}) collective-permute-start(bf16[1024,256]{1,0:T(8,128)(2,1)} %get-tuple-element.99), channel_id=1, source_target_pairs={{0,3},{1,0},{2,1},{3,2},{4,7},{5,4},{6,5},{7,6},{8,11},{9,8},{10,9... | collective-permute-start | bytes 1572872 | tf_op jit(solution)/shard_map/ppermute | solution.py:426
  68.2 15.8 %collective-permute-start.11 = (bf16[1024,256]{1,0:T(8,128)(2,1)}, bf16[1024,256]{1,0:T(8,128)(2,1)}, u32[]{:S(2)}, u32[]{:S(2)}) collective-permute-start(bf16[1024,256]{1,0:T(8,128)(2,1)} %get-tuple-element.101), channel_id=1, source_target_pairs={{0,1},{1,2},{2,3},{3,0},{4,5},{5,6},{6,7},{7,4},{8,9},{9,10},{10,1... | collective-permute-start | bytes 1572872 | tf_op jit(solution)/shard_map/ppermute | solution.py:426
  74.0 19.5 %all-to-all-start = ((bf16[4,8,64,256]{3,2,1,0:T(8,128)(2,1)}), bf16[4,8,64,256]{3,2,1,0:T(8,128)(2,1)S(1)}, u32[]{:S(2)}, u32[]{:S(2)}) async-start(bf16[4,8,64,256]{3,2,1,0:T(8,128)(2,1)} %bitcast.2), calls=%async_computation | async-start | bytes 2097152 | tf_op jit(solution)/shard_map/all_to_all | solution.py:560
  84.0 4.8 %copy-start.6 = (bf16[1024,256]{1,0:T(8,128)(2,1)}, bf16[1024,256]{1,0:T(8,128)(2,1)S(1)}, u32[]{:S(2)}) copy-start(bf16[1024,256]{1,0:T(8,128)(2,1)S(1)} %collective-permute-done.10) | copy-start | bytes 1572868
  86.0 17.0 %collective-permute-start.12 = (bf16[512,256]{1,0:T(8,128)(2,1)}, bf16[512,256]{1,0:T(8,128)(2,1)}, u32[]{:S(2)}, u32[]{:S(2)}) collective-permute-start(bf16[512,256]{1,0:T(8,128)(2,1)} %get-tuple-element.106), channel_id=1, source_target_pairs={{0,1},{1,2},{2,3},{3,0},{4,5},{5,6},{6,7},{7,4},{8,9},{9,10},{10,1... | collective-permute-start | bytes 786440 | tf_op jit(solution)/shard_map/ppermute | solution.py:426
  88.8 14.2 %copy-start.4 = (bf16[1024,256]{1,0:T(8,128)(2,1)S(1)}, bf16[1024,256]{1,0:T(8,128)(2,1)}, u32[]{:S(2)}) copy-start(bf16[1024,256]{1,0:T(8,128)(2,1)} %get-tuple-element.98) | copy-start | bytes 1572868
  88.8 14.2 %collective-permute-start.13 = (bf16[512,256]{1,0:T(8,128)(2,1)S(1)}, bf16[512,256]{1,0:T(8,128)(2,1)}, u32[]{:S(2)}, u32[]{:S(2)}) collective-permute-start(bf16[512,256]{1,0:T(8,128)(2,1)S(1)} %get-tuple-element.107), channel_id=1, source_target_pairs={{0,3},{1,0},{2,1},{3,2},{4,7},{5,4},{6,5},{7,6},{8,11},{9,8},{10,9... | collective-permute-start | bytes 786440 | tf_op jit(solution)/shard_map/ppermute | solution.py:426
  94.4 18.6 %all-to-all-start.1 = ((bf16[8,64,256]{2,1,0:T(8,128)(2,1)}), bf16[8,64,256]{2,1,0:T(8,128)(2,1)S(1)}, u32[]{:S(2)}, u32[]{:S(2)}) async-start(bf16[8,64,256]{2,1,0:T(8,128)(2,1)} %reduce_sum.21), calls=%async_computation.1 | async-start | bytes 524288 | tf_op jit(solution)/shard_map/all_to_all | solution.py:562
  (6 other events, 4.5 us)

commit v4 on v3

--- a/solution.py
+++ b/solution.py
@@ -70,15 +70,16 @@
     return pl.BlockSpec(memory_space=pl.ANY)
 
 
-def kv_kernel(
-    x_hbm, wk_hbm, wv_hbm, kv_hbm, c2_hbm, c4_hbm, c8_hbm,
-    x_s, wk_s, wv_s, kv_s, c2_s, c4_s, c8_s, in_sems, out_sems,
+def tokens_kernel(
+    x_hbm, wk_hbm, wv_hbm, wq_hbm, kv_hbm, c2_hbm, c4_hbm, c8_hbm, q_hbm,
+    x_s, wk_s, wv_s, wq_s, kv_s, c2_s, c4_s, c8_s, q_s, in_sems, out_sems,
 ):
     fetch, store = Copies(in_sems), Copies(out_sems)
     wk = [fetch.start(row_block(wk_hbm, i, SPAN), row_block(wk_s, i, SPAN)) for i in range(2)]
     x = [fetch.start(row_block(x_hbm, i, BLOCK), row_block(x_s, i, BLOCK)) for i in range(2)]
     wv = [fetch.start(row_block(wv_hbm, i, SPAN), row_block(wv_s, i, SPAN)) for i in range(2)]
     x += [fetch.start(row_block(x_hbm, i, BLOCK), row_block(x_s, i, BLOCK)) for i in (2, 3)]
+    wq = [fetch.start(row_block(wq_hbm, i, SPAN), row_block(wq_s, i, SPAN)) for i in range(2)]
     averages = [run_matrix(BLOCK >> shift, BLOCK, shift, False) for shift in range(4)]
     stores = []
     for half in range(2):
@@ -93,6 +94,7 @@
             for copy in wv:
                 copy.wait()
         kv_s[rows, COLS:] = dot_nn(x_s[rows], wv_s[...]).astype(bf16)
+        stores.append(store.start(row_block(kv_s, half, SPAN), row_block(kv_hbm, half, SPAN)))
         for shift, ref, out in ((3, c8_s, c8_hbm), (2, c4_s, c4_hbm), (1, c2_s, c2_hbm)):
             count = BLOCK >> shift
             for index in (2 * half, 2 * half + 1):
@@ -102,76 +104,67 @@
             stores.append(
                 store.start(row_block(ref, half, 2 * count), row_block(out, half, 2 * count))
             )
-        stores.append(store.start(row_block(kv_s, half, SPAN), row_block(kv_hbm, half, SPAN)))
+    for copy in wq:
+        copy.wait()
+    for half in range(2):
+        rows = slice(half * SPAN, (half + 1) * SPAN)
+        q_s[rows] = dot_nn(x_s[rows], wq_s[...]).astype(bf16)
+        stores.append(store.start(row_block(q_s, half, SPAN), row_block(q_hbm, half, SPAN)))
     for copy in stores:
         copy.wait()
 
 
-def project_kv(tokens, w_key, w_value):
-    outs = [(ROWS >> s, 2 * COLS) for s in range(4)]
+def project_tokens(tokens, w_key, w_value, w_query):
+    outs = [(ROWS >> s, 2 * COLS) for s in range(4)] + [(ROWS, COLS)]
     return pl.pallas_call(
-        kv_kernel,
-        in_specs=[any_spec()] * 3,
-        out_specs=[any_spec()] * 4,
+        tokens_kernel,
+        in_specs=[any_spec()] * 4,
+        out_specs=[any_spec()] * 5,
         out_shape=[shape(dims) for dims in outs],
+        scratch_shapes=[pltpu.VMEM((ROWS, WIDTH), bf16)]
+        + [pltpu.VMEM((WIDTH, COLS), bf16)] * 3
+        + [pltpu.VMEM(dims, bf16) for dims in outs]
+        + [pltpu.SemaphoreType.DMA((10,)), pltpu.SemaphoreType.DMA((10,))],
+        compiler_params=params(60),
+        cost_estimate=cost(ROWS * WIDTH * 3 * COLS, 7 * MIB),
+        name="project_tokens",
+    )(tokens, w_key, w_value, w_query)
+
+
+def cotangent_kernel(c_hbm, wo_hbm, da_hbm, c_s, wo_s, da_s, in_sems, out_sems):
+    fetch, store = Copies(in_sems), Copies(out_sems)
+    wo = [fetch.start(row_block(wo_hbm, i, 128), row_block(wo_s, i, 128)) for i in range(2)]
+    c = [fetch.start(row_block(c_hbm, i, BLOCK), row_block(c_s, i, BLOCK)) for i in range(4)]
+    for copy in wo:
+        copy.wait()
+    stores = []
+    for half in range(2):
+        for copy in c[2 * half : 2 * half + 2]:
+            copy.wait()
+        rows = slice(half * SPAN, (half + 1) * SPAN)
+        da_s[rows] = dot_nt(c_s[rows], wo_s[...]).astype(bf16)
+        stores.append(store.start(row_block(da_s, half, SPAN), row_block(da_hbm, half, SPAN)))
+    for copy in stores:
+        copy.wait()
+
+
+def project_cotangent(cotangent, w_out):
+    return pl.pallas_call(
+        cotangent_kernel,
+        in_specs=[any_spec()] * 2,
+        out_specs=any_spec(),
+        out_shape=shape((ROWS, COLS)),
         scratch_shapes=[
             pltpu.VMEM((ROWS, WIDTH), bf16),
-            pltpu.VMEM((WIDTH, COLS), bf16),
-            pltpu.VMEM((WIDTH, COLS), bf16),
-        ]
-        + [pltpu.VMEM(dims, bf16) for dims in outs]
-        + [pltpu.SemaphoreType.DMA((8,)), pltpu.SemaphoreType.DMA((8,))],
-        compiler_params=params(60),
-        cost_estimate=cost(ROWS * WIDTH * 2 * COLS, 6 * MIB),
-        name="project_kv",
-    )(tokens, w_key, w_value)
-
-
-def q_kernel(
-    x_hbm, c_hbm, wq_hbm, wo_hbm, q_hbm, da_hbm,
-    x_s, c_s, wq_s, wo_s, q_s, da_s, in_sems, out_sems,
-):
-    fetch, store = Copies(in_sems), Copies(out_sems)
-    wq = [fetch.start(row_block(wq_hbm, i, SPAN), row_block(wq_s, i, SPAN)) for i in range(2)]
-    x = [fetch.start(row_block(x_hbm, i, SPAN), row_block(x_s, i, SPAN)) for i in range(2)]
-    wo = [fetch.start(row_block(wo_hbm, i, 128), row_block(wo_s, i, 128)) for i in range(2)]
-    c = [fetch.start(row_block(c_hbm, i, SPAN), row_block(c_s, i, SPAN)) for i in range(2)]
-    stores = []
-    for weights, inputs, w_s, in_s, out_s, out, dot in (
-        (wq, x, wq_s, x_s, q_s, q_hbm, dot_nn),
-        (wo, c, wo_s, c_s, da_s, da_hbm, dot_nt),
-    ):
-        for copy in weights:
-            copy.wait()
-        for half in range(2):
-            inputs[half].wait()
-            rows = slice(half * SPAN, (half + 1) * SPAN)
-            out_s[rows] = dot(in_s[rows], w_s[...]).astype(bf16)
-            stores.append(store.start(row_block(out_s, half, SPAN), row_block(out, half, SPAN)))
-    for copy in stores:
-        copy.wait()
-
-
-def project_q(tokens, cotangent, w_query, w_out):
-    return pl.pallas_call(
-        q_kernel,
-        in_specs=[any_spec()] * 4,
-        out_specs=[any_spec()] * 2,
-        out_shape=[shape((ROWS, COLS))] * 2,
-        scratch_shapes=[
-            pltpu.VMEM((ROWS, WIDTH), bf16),
-            pltpu.VMEM((ROWS, WIDTH), bf16),
-            pltpu.VMEM((WIDTH, COLS), bf16),
             pltpu.VMEM((COLS, WIDTH), bf16),
             pltpu.VMEM((ROWS, COLS), bf16),
-            pltpu.VMEM((ROWS, COLS), bf16),
-            pltpu.SemaphoreType.DMA((8,)),
-            pltpu.SemaphoreType.DMA((4,)),
+            pltpu.SemaphoreType.DMA((6,)),
+            pltpu.SemaphoreType.DMA((2,)),
         ],
         compiler_params=params(60),
-        cost_estimate=cost(ROWS * WIDTH * 2 * COLS, 7 * MIB),
-        name="project_q",
-    )(tokens, cotangent, w_query, w_out)
+        cost_estimate=cost(ROWS * WIDTH * COLS, 4 * MIB),
+        name="project_cotangent",
+    )(cotangent, w_out)
 
 
 def entry_rows(refs, kb, lo):
@@ -199,18 +192,15 @@
 def forward_kernel(*refs):
     entries, q_ref, da_ref = refs[:5], refs[5], refs[6]
     ot_ref, stat_ref, qgt_ref, g2_ref, g3a_ref, g3b_ref = refs[7:13]
-    k_s, v_s, w_s, vt_s, kt_s, qm_s, dm_s, grad_s = refs[13:]
+    w_s, vt_s, kt_s, qm_s, dm_s, grad_s = refs[13:]
     step = pl.program_id(0)
     for kb in range(5):
         rows = slice(kb * BLOCK, (kb + 1) * BLOCK)
         for pair in range(2):
             lanes = slice(pair * 128, pair * 128 + 128)
-            key = entry_rows(entries, kb, pair * 128)
-            value = entry_rows(entries, kb, COLS + pair * 128)
-            k_s[rows, lanes] = key
-            v_s[rows, lanes] = value
-            vt_s[lanes, rows] = value.T
+            vt_s[lanes, rows] = entry_rows(entries, kb, COLS + pair * 128).T
             if kb >= 3:
+                key = entry_rows(entries, kb, pair * 128)
                 kt_s[lanes, (kb - 3) * BLOCK : (kb - 2) * BLOCK] = key.T
     for head in range(4):
         qm_s[head] = only_head(q_ref, head)
@@ -223,10 +213,14 @@
     for pair in range(2):
         lo = pair * 128
         key_grad = value_grad = 0.0
+        keys, values = [
+            jnp.concatenate([entry_rows(entries, kb, first + lo) for kb in range(5)], axis=0)
+            for first in (0, COLS)
+        ]
         for side in range(2):
             head = 2 * pair + side
-            t = dot_nt(k_s[:, lo : lo + 128], qm_s[head])
-            p = dot_nt(v_s[:, lo : lo + 128], dm_s[head])
+            t = dot_nt(keys, qm_s[head])
+            p = dot_nt(values, dm_s[head])
             tops = []
             for kb in range(5):
                 rows = slice(kb * BLOCK, (kb + 1) * BLOCK)
@@ -296,8 +290,6 @@
             shape((BLOCK // 2, 2 * COLS)),
         ],
         scratch_shapes=[
-            pltpu.VMEM((KEYS, COLS), bf16),
-            pltpu.VMEM((KEYS, COLS), bf16),
             pltpu.VMEM((2, KEYS, SPAN), bf16),
             pltpu.VMEM((COLS, KEYS), bf16),
             pltpu.VMEM((COLS, 2 * BLOCK), bf16),
@@ -440,9 +432,11 @@
 
 def head_sum_second(got_right, got_left, right, left, hold, mine):
     half = ROWS // 2
-    more_right = shifted(add(hold[:half], got_right[:half]), 1)
-    more_left = shifted(add(hold[half:], got_left[half:]), -1)
-    return more_right, more_left
+    return add(hold[:half], got_right[:half]), add(hold[half:], got_left[half:])
+
+
+def head_sum_third(more_right, more_left):
+    return shifted(more_right, 1), shifted(more_left, -1)
 
 
 def head_sum_last(more_right, more_left, got_right, got_left, right, left, hold, mine):
@@ -454,12 +448,6 @@
         ],
         axis=0,
     )
-
-
-def head_sum(*parts):
-    got = head_sum_first(*parts)
-    more = head_sum_second(*got, *parts)
-    return head_sum_last(*more, *got, *parts)
 
 
 def tail_kernel(
@@ -518,12 +506,11 @@
     outs = (right_hbm, left_hbm, hold_hbm, stay_hbm)
     for half in range(2):
         rows = slice(half * SPAN, (half + 1) * SPAN)
-        query_grad = qgt_s[:, rows].T
+        grads = jnp.concatenate([qgt_s[:, rows].T, kvg_s[rows]], axis=1)
         for index, (offset, out) in enumerate(zip(ring_columns(half), outs)):
             cols = column_group(at_ref[1], offset)
-            part = dot_nt(query_grad, wq_s[cols, :])
-            part = part + dot_nt(kvg_s[rows, :COLS], wk_s[cols, :])
-            part = part + dot_nt(kvg_s[rows, COLS:], wv_s[cols, :])
+            weights = jnp.concatenate([wq_s[cols, :], wk_s[cols, :], wv_s[cols, :]], axis=1)
+            part = dot_nt(grads, weights)
             part_s[index, rows] = part.astype(bf16)
             stores.append(
                 store.start(part_s.at[index, pl.ds(half * SPAN, SPAN)], row_block(out, half, SPAN))
@@ -552,24 +539,70 @@
     )(at, *operands)
 
 
-def seq_sum(mine, got):
+def stage_kernel(at_ref, *refs, terms, picks):
+    total_s = refs[-1]
+    total_s[...] = sum(ref[...].astype(f32) for ref in refs[:terms]).astype(bf16)
+    for pick, ref in zip(picks, refs[terms:-1]):
+        for block, source in enumerate(pick(at_ref)):
+            ref[block] = total_s[source]
+
+
+def stage(at, terms, picks, counts, name):
+    vmem = pl.BlockSpec(memory_space=pltpu.VMEM)
+    dims = terms[0].shape
+    return pl.pallas_call(
+        functools.partial(stage_kernel, terms=len(terms), picks=picks),
+        in_specs=[pl.BlockSpec(memory_space=pltpu.SMEM)] + [vmem] * len(terms),
+        out_specs=[vmem] * len(counts),
+        out_shape=[shape((count, *dims[1:])) for count in counts],
+        scratch_shapes=[pltpu.VMEM(dims, bf16)],
+        compiler_params=params(24),
+        name=name,
+    )(at, *terms)
+
+
+def x_blocks(offset, first, count):
+    return lambda at: [((at[2] + offset) & 3) * 8 + first + block for block in range(count)]
+
+
+def moved(value, by):
     size = lax.axis_size("seq")
-    along_x = [list(range(first, size, 16)) for first in range(16)]
-    along_z = [list(range(16 * x + core, 16 * x + 16, 2)) for x in range(4) for core in range(2)]
-    blocks = add(mine, got).reshape(4, 8, 64, COLS)
-    blocks = lax.all_to_all(blocks, "seq", 0, 0, axis_index_groups=along_x)
-    blocks = jnp.sum(blocks.astype(f32), axis=0).astype(bf16)
+    return lax.ppermute(value, "seq", [(i, (i + by) % size) for i in range(size)])
+
+
+def core_sum(at, mine, got):
+    return stage(
+        at,
+        (mine, got),
+        [x_blocks(2, 0, 4), x_blocks(2, 4, 4), x_blocks(1, 0, 8), x_blocks(3, 0, 8)]
+        + [x_blocks(0, 0, 8)],
+        [4, 4, 8, 8, 8],
+        "sum_cores",
+    )
+
+
+def x_first(far_a, far_b, ahead, behind):
+    got_a, got_b = moved(far_a, 16), moved(far_b, -16)
+    ahead = jnp.concatenate([add(ahead[:4], got_a), ahead[4:]], axis=0)
+    behind = jnp.concatenate([behind[:4], add(behind[4:], got_b)], axis=0)
+    return ahead, behind
+
+
+def z_sum(blocks):
+    size = lax.axis_size("seq")
+    along_z = [list(range(16 * x + core, 16 * x + 16, 2)) for x in range(size // 16) for core in range(2)]
     blocks = lax.all_to_all(blocks, "seq", 0, 0, axis_index_groups=along_z)
     return jnp.sum(blocks.astype(f32), axis=0)
 
 
 def on_device(tokens, cotangent, w_query, w_key, w_value, w_out):
-    at = jnp.stack([lax.axis_index("seq") % 2, lax.axis_index("head")]).astype(jnp.int32)
-    key_value, own_2, own_4, own_8 = project_kv(tokens, w_key, w_value)
+    place = lax.axis_index("seq")
+    at = jnp.stack([place % 2, lax.axis_index("head"), place // 16]).astype(jnp.int32)
+    key_value, own_2, own_4, own_8, queries = project_tokens(tokens, w_key, w_value, w_query)
     three_a = swapped(own_8, 2)
     level_two = swapped(own_4, 1)
-    queries, d_attended = project_q(tokens, cotangent, w_query, w_out)
-    queries, three_a = lax.optimization_barrier((queries, three_a))
+    d_attended = project_cotangent(cotangent, w_out)
+    d_attended, three_a = lax.optimization_barrier((d_attended, three_a))
     three_b = swapped(three_a, 1)
     entries = (key_value, own_2, level_two, three_a, three_b)
     attended_t, stats, query_part, grad_2, grad_3a, grad_3b = attend(
@@ -585,7 +618,7 @@
     got_3 = swapped(grad_3, 2)
     near = near_grads(*near)
     near, out_got = lax.optimization_barrier((near, out_got))
-    out_more = head_sum_second(*out_got, *out_parts)
+    out_more = head_sum_third(*head_sum_second(*out_got, *out_parts))
     query_grad_t, own, sibling = near
     *parts, mine, other = tail(
         at, own, sibling, got_2, got_3, query_grad_t, attended_t, tokens, cotangent,
@@ -593,9 +626,18 @@
     )
     (parts, mine, other), out_more = lax.optimization_barrier(((parts, mine, other), out_more))
     layer_out = head_sum_last(*out_more, *out_got, *out_parts)
-    grad_tokens = head_sum(*parts)
+    got = head_sum_first(*parts)
+    far_a, far_b, ahead, behind, here = core_sum(at, mine, swapped(other, 1))
+    ahead, behind = x_first(far_a, far_b, ahead, behind)
+    moved_blocks = moved(ahead, 16), moved(behind, -16)
+    got, _ = lax.optimization_barrier((got, (ahead, behind)))
+    more = head_sum_second(*got, *parts)
+    moved_blocks, _ = lax.optimization_barrier((moved_blocks, more))
+    more = head_sum_third(*more)
+    summed = z_sum(add(here, *moved_blocks))
+    grad_tokens = head_sum_last(*more, *got, *parts)
     scale = 1.0 / math.sqrt(lax.axis_size("seq") * tokens.shape[0])
-    summed = seq_sum(mine, swapped(other, 1)) * scale
+    summed = summed * scale
     return (
         layer_out,
         grad_tokens,

time: 114 us -> 112 us (0.982)
  other arithmetic: 11 us -> 5.29 us
  starting transfers between devices: 27.4 us -> 28.9 us
  waiting for transfers between devices: 18.5 us -> 19.7 us
    ppermute x0 -> x4, starting transfers between devices: none -> 6.71 us  [moved(): lax.ppermute(value, 'seq', [(i, (i + by) % size) for i in range(size)])]
    convert_element_type x6 -> x8, other arithmetic: 8.35 us -> 3.46 us  [add(): return sum((term.astype(f32) for term in terms)).astype(bf16)]
    all_to_all x2 -> x1, starting transfers between devices: 12 us -> 7.59 us  [z_sum(): blocks = lax.all_to_all(blocks, 'seq', 0, 0, axis_index_groups=along_z)]
    all_to_all x2 -> x1, waiting for transfers between devices: 11.1 us -> 7.65 us  [z_sum(): blocks = lax.all_to_all(blocks, 'seq', 0, 0, axis_index_groups=along_z)]
    ppermute x7, waiting for transfers between devices: 1 us -> 3.37 us  [swapped(): lax.ppermute(value, 'seq', [(i, i ^ bits) for i in range(lax.axis_size('s...]
    ppermute x0 -> x4, waiting for transfers between devices: none -> 2.33 us  [moved(): lax.ppermute(value, 'seq', [(i, (i + by) % size) for i in range(size)])]
    ppermute x8, starting transfers between devices: 11.5 us -> 9.48 us  [shifted(): lax.ppermute(value, 'head', [(i, (i + by) % size) for i in range(size)])]
    ppermute x7, starting transfers between devices: 3.81 us -> 5.12 us  [swapped(): lax.ppermute(value, 'seq', [(i, i ^ bits) for i in range(lax.axis_size('s...]
  transfers between devices with their start and end apart: 17 -> 20, of which waited for: 5 -> 9; matrix products, arithmetic and copies ran while one was open for 10% -> 5% of each run, Pallas kernels for 24% -> 23%
where the time goes in v4:
time: 112 us; the launch traced here: 111 us
  Pallas kernels  51.5 us (46%)
  starting transfers between devices  28.9 us (26%)
  waiting for transfers between devices  19.7 us (18%)
  other arithmetic  5.29 us (5%)
  local copies, waits for them, and re-layouts  4.94 us (4%)
    pallas_call x1, Pallas kernels, attend(): pl.pallas_call(forward_kernel, grid=(2,), in_specs=[pl.BlockSpec((SPAN, 2...  18.6 us
    pallas_call x1, Pallas kernels, near_grads(): pl.pallas_call(near_kernel, grid=(2,), in_specs=[near, sibling, part, par...  11.3 us
    pallas_call x1, Pallas kernels, tail(): pl.pallas_call(tail_kernel, in_specs=[pl.BlockSpec(memory_space=pltpu.SME...  9.72 us
    ppermute x8, starting transfers between devices, shifted(): lax.ppermute(value, 'head', [(i, (i + by) % size) for i in range(size)])  9.48 us
    all_to_all x1, waiting for transfers between devices, z_sum(): blocks = lax.all_to_all(blocks, 'seq', 0, 0, axis_index_groups=along_z)  7.65 us
    all_to_all x1, starting transfers between devices, z_sum(): blocks = lax.all_to_all(blocks, 'seq', 0, 0, axis_index_groups=along_z)  7.59 us
    ppermute x4, starting transfers between devices, moved(): lax.ppermute(value, 'seq', [(i, (i + by) % size) for i in range(size)])  6.71 us
    ppermute x8, waiting for transfers between devices, shifted(): lax.ppermute(value, 'head', [(i, (i + by) % size) for i in range(size)])  6.35 us
  transfers between devices with their start and end apart: 20, of which 9 were waited for; matrix products, arithmetic and copies ran while one was open for 5% of the time, Pallas kernels for 23%

profile of v4, /device:TPU:24, one launch (start us, length us, event | category | flops | bytes accessed | tf_op | source)
XLA Modules:
  0.0 111.2 jit_solution(15323583633735625330)
XLA Ops:
  0.6 5.8 %project_tokens.1 = (bf16[1024,512]{1,0:T(8,128)(2,1)}, bf16[512,512]{1,0:T(8,128)(2,1)}, bf16[256,512]{1,0:T(8,128)(2,1)}, bf16[128,512]{1,0:T(8,128)(2,1)}, bf16[1024,256]{1,0:T(8,128)(2,1)}) custom-call(bf16[1024,1024]{1,0:T(8,128)(2,1)} %x_hbm.3, bf16[1024,256]{1,0:T(8,128)(2,1)} %wk_hbm.3, bf16[1024,256]{1,0:T(8,128)(2,1)} %wv_hbm.3, ...), custom_call_target="tpu_custom_call" | custom-call | flops 1610612736 | bytes 7340032 | tf_op jit(solution)/shard_map/project_tokens/pallas_call | solution.py:119
  6.5 2.0 %collective-permute-start = (bf16[128,512]{1,0:T(8,128)(2,1)}, bf16[128,512]{1,0:T(8,128)(2,1)S(1)}, u32[]{:S(2)}, u32[]{:S(2)}) collective-permute-start(bf16[128,512]{1,0:T(8,128)(2,1)} %get-tuple-element.66), channel_id=1, source_target_pairs={{0,8},{4,12},{8,0},{12,4},{16,24},{20,28},{24,16},{28,20},{32,40},... | collective-permute-start | bytes 393224 | tf_op jit(solution)/shard_map/ppermute | solution.py:422
  8.5 3.6 %project_cotangent.1.refs_6_.da_ref = bf16[1024,256]{1,0:T(8,128)(2,1)} custom-call(bf16[1024,1024]{1,0:T(8,128)(2,1)} %c_hbm.3, bf16[256,1024]{1,0:T(8,128)(2,1)} %w_ref.1), custom_call_target="tpu_custom_call" | custom-call | flops 536870912 | bytes 4194304 | tf_op jit(solution)/shard_map/project_cotangent/pallas_call | solution.py:152
  14.6 18.6 %attend.1 = (bf16[256,1024]{1,0:T(8,128)(2,1)}, f32[8,1024]{1,0:T(8,128)}, f32[256,1024]{1,0:T(8,128)}, bf16[256,512]{1,0:T(8,128)(2,1)}, bf16[128,512]{1,0:T(8,128)(2,1)}, /*index=5*/bf16[128,512]{1,0:T(8,128)(2,1)}) custom-call(bf16[1024,512]{1,0:T(8,128)(2,1)} %get-tuple-element.80.refs_0_.near, bf16[512,512]{1,0:T(8,128)(2,1)} %get-tuple-element.81.refs_1_.c2, ...), custom_call_target="tpu_custom_call" | custom-call | flops 10737418240 | bytes 6291456 | tf_op jit(solution)/shard_map/attend/pallas_call | solution.py:271
  33.9 1.0 copy-done.4
  34.9 1.3 %project_out.1 = (bf16[1024,256]{1,0:T(8,128)(2,1)S(1)}, bf16[1024,256]{1,0:T(8,128)(2,1)S(1)}, bf16[1024,256]{1,0:T(8,128)(2,1)S(1)}, bf16[1024,256]{1,0:T(8,128)(2,1)S(1)}) custom-call(s32[3]{0:T(128)S(1)} %pad_add_fusion.at_ref, bf16[256,1024]{1,0:T(8,128)(2,1)S(1)} %copy-done.4, bf16[256,1024]{1,0:T(8,128)(2,1)S(1)} %copy-done.1), custom_call_target="tpu_custom_call" | custom-call | flops 536870912 | bytes 4194304 | tf_op jit(solution)/shard_map/project_out/pallas_call | solution.py:405
  36.2 1.3 %collective-permute-start.4 = (bf16[1024,256]{1,0:T(8,128)(2,1)S(1)}, bf16[1024,256]{1,0:T(8,128)(2,1)S(1)}, u32[]{:S(2)}, u32[]{:S(2)}) collective-permute-start(bf16[1024,256]{1,0:T(8,128)(2,1)S(1)} %get-tuple-element.73), channel_id=1, source_target_pairs={{0,1},{1,2},{2,3},{3,0},{4,5},{5,6},{6,7},{7,4},{8,9},{9,10},{10,1... | collective-permute-start | bytes 1572872 | tf_op jit(solution)/shard_map/ppermute | solution.py:418
  39.3 1.7 %collective-permute-start.7 = (bf16[128,512]{1,0:T(8,128)(2,1)S(1)}, bf16[128,512]{1,0:T(8,128)(2,1)}, u32[]{:S(2)}, u32[]{:S(2)}) collective-permute-start(bf16[128,512]{1,0:T(8,128)(2,1)S(1)} %add_convert_fusion.11), channel_id=1, source_target_pairs={{0,8},{4,12},{8,0},{12,4},{16,24},{20,28},{24,16},{28,20},{32,40},... | collective-permute-start | bytes 393224 | tf_op jit(solution)/shard_map/ppermute | solution.py:422
  41.0 11.3 %near_grads.1 = (bf16[256,1024]{1,0:T(8,128)(2,1)}, f32[1024,512]{1,0:T(8,128)}, f32[512,512]{1,0:T(8,128)}) custom-call(bf16[1024,512]{1,0:T(8,128)(2,1)} %get-tuple-element.80.refs_0_.near, bf16[512,512]{1,0:T(8,128)(2,1)} %get-tuple-element.81.refs_1_.c2, bf16[1024,256]{1,0:T(8,128)(2,1)} %get-tuple-element.82.refs_5_.q_ref, ...), custom_call_target="tpu_custom_call" | custom-call | flops 8053063680 | bytes 8388608 | tf_op jit(solution)/shard_map/near_grads/pallas_call | solution.py:358
  53.3 2.6 %collective-permute-start.8 = (bf16[512,256]{1,0:T(8,128)(2,1)S(1)}, bf16[512,256]{1,0:T(8,128)(2,1)S(1)}, u32[]{:S(2)}, u32[]{:S(2)}) collective-permute-start(bf16[512,256]{1,0:T(8,128)(2,1)S(1)} %get-tuple-element.127), channel_id=1, source_target_pairs={{0,1},{1,2},{2,3},{3,0},{4,5},{5,6},{6,7},{7,4},{8,9},{9,10},{10,1... | collective-permute-start | bytes 786440 | tf_op jit(solution)/shard_map/ppermute | solution.py:418
  55.9 9.7 %tail.1 = (bf16[1024,256]{1,0:T(8,128)(2,1)}, bf16[1024,256]{1,0:T(8,128)(2,1)}, bf16[1024,256]{1,0:T(8,128)(2,1)}, bf16[1024,256]{1,0:T(8,128)(2,1)}, bf16[32,6...) custom-call(s32[3]{0:T(128)} %copy-done.2, f32[1024,512]{1,0:T(8,128)} %get-tuple-element.90.own_hbm, ...), custom_call_target="tpu_custom_call" | custom-call | flops 3758096384 | bytes 14680064 | tf_op jit(solution)/shard_map/tail/pallas_call | solution.py:523
  66.3 2.3 %collective-permute-done.12.refs_1_ = bf16[32,64,256]{2,1,0:T(8,128)(2,1)S(1)} collective-permute-done((bf16[32,64,256]{2,1,0:T(8,128)(2,1)}, bf16[32,64,256]{2,1,0:T(8,128)(2,1)S(1)}, u32[]{:S(2)}, u32[]{:S(2)}) %collective-permute-start.12) | collective-permute-done | bytes 1048608 | tf_op jit(solution)/shard_map/ppermute | solution.py:422
  68.6 1.2 %copy-done = bf16[32,64,256]{2,1,0:T(8,128)(2,1)S(1)} copy-done((bf16[32,64,256]{2,1,0:T(8,128)(2,1)S(1)}, bf16[32,64,256]{2,1,0:T(8,128)(2,1)}, u32[]{:S(2)}) %copy-start) | copy-done | bytes 1048600
  69.8 1.2 %sum_cores.1 = (bf16[4,64,256]{2,1,0:T(8,128)(2,1)S(1)}, bf16[4,64,256]{2,1,0:T(8,128)(2,1)S(1)}, bf16[8,64,256]{2,1,0:T(8,128)(2,1)S(1)}, bf16[8,64,256]{2,1,0:T(8,128)(2,1)S(1)}, bf16[8,64,256]{2,1,0:T(8,128)(2,1)S(1)}) custom-call(s32[3]{0:T(128)S(1)} %copy-done.3, bf16[32,64,256]{2,1,0:T(8,128)(2,1)S(1)} %copy-done, ...), custom_call_target="tpu_custom_call" | custom-call | tf_op jit(solution)/shard_map/sum_cores/pallas_call | solution.py:553
  71.0 2.8 %collective-permute-start.14 = (bf16[4,64,256]{2,1,0:T(8,128)(2,1)S(1)}, bf16[4,64,256]{2,1,0:T(8,128)(2,1)S(1)}, u32[]{:S(2)}, u32[]{:S(2)}) collective-permute-start(bf16[4,64,256]{2,1,0:T(8,128)(2,1)S(1)} %get-tuple-element.113), channel_id=1, source_target_pairs={{0,192},{4,196},{8,200},{12,204},{16,208},{20,212},{24,216},{28,22... | collective-permute-start | bytes 393224 | tf_op jit(solution)/shard_map/ppermute | solution.py:570
  74.0 1.8 %collective-permute-start.11 = (bf16[1024,256]{1,0:T(8,128)(2,1)S(1)}, bf16[1024,256]{1,0:T(8,128)(2,1)S(1)}, u32[]{:S(2)}, u32[]{:S(2)}) collective-permute-start(bf16[1024,256]{1,0:T(8,128)(2,1)S(1)} %copy-done.11), channel_id=1, source_target_pairs={{0,3},{1,0},{2,1},{3,2},{4,7},{5,4},{6,5},{7,6},{8,11},{9,8},{10,9... | collective-permute-start | bytes 1572872 | tf_op jit(solution)/shard_map/ppermute | solution.py:418
  76.9 3.8 %collective-permute-start.18 = (bf16[8,64,256]{2,1,0:T(8,128)(2,1)S(1)}, bf16[8,64,256]{2,1,0:T(8,128)(2,1)S(1)}, u32[]{:S(2)}, u32[]{:S(2)}) collective-permute-start(bf16[8,64,256]{2,1,0:T(8,128)(2,1)S(1)} %pad_maximum_fusion.3), channel_id=1, source_target_pairs={{0,192},{4,196},{8,200},{12,204},{16,208},{20,212},{24,216},{28,22... | collective-permute-start | bytes 786440 | tf_op jit(solution)/shard_map/ppermute | solution.py:570
  80.7 1.4 %collective-permute-done.13 = bf16[4,64,256]{2,1,0:T(8,128)(2,1)S(1)} collective-permute-done((bf16[4,64,256]{2,1,0:T(8,128)(2,1)S(1)}, bf16[4,64,256]{2,1,0:T(8,128)(2,1)S(1)}, u32[]{:S(2)}, u32[]{:S(2)}) %collective-permute-start.13) | collective-permute-done | bytes 131104 | tf_op jit(solution)/shard_map/ppermute | solution.py:570
  82.5 5.0 %collective-permute-done.10 = bf16[1024,256]{1,0:T(8,128)(2,1)S(1)} collective-permute-done((bf16[1024,256]{1,0:T(8,128)(2,1)S(1)}, bf16[1024,256]{1,0:T(8,128)(2,1)S(1)}, u32[]{:S(2)}, u32[]{:S(2)}) %collective-permute-start.10) | collective-permute-done | bytes 524320 | tf_op jit(solution)/shard_map/ppermute | solution.py:418
  87.5 1.3 %collective-permute-done.11 = bf16[1024,256]{1,0:T(8,128)(2,1)S(1)} collective-permute-done((bf16[1024,256]{1,0:T(8,128)(2,1)S(1)}, bf16[1024,256]{1,0:T(8,128)(2,1)S(1)}, u32[]{:S(2)}, u32[]{:S(2)}) %collective-permute-start.11) | collective-permute-done | bytes 524320 | tf_op jit(solution)/shard_map/ppermute | solution.py:418
  89.8 1.8 %collective-permute-start.16 = (bf16[512,256]{1,0:T(8,128)(2,1)S(1)}, bf16[512,256]{1,0:T(8,128)(2,1)}, u32[]{:S(2)}, u32[]{:S(2)}) collective-permute-start(bf16[512,256]{1,0:T(8,128)(2,1)S(1)} %get-tuple-element.123), channel_id=1, source_target_pairs={{0,3},{1,0},{2,1},{3,2},{4,7},{5,4},{6,5},{7,6},{8,11},{9,8},{10,9... | collective-permute-start | bytes 786440 | tf_op jit(solution)/shard_map/ppermute | solution.py:418
  92.4 7.6 %all-to-all-start = ((bf16[8,64,256]{2,1,0:T(8,128)(2,1)}), bf16[8,64,256]{2,1,0:T(8,128)(2,1)S(1)}, u32[]{:S(2)}, u32[]{:S(2)}) async-start(bf16[8,64,256]{2,1,0:T(8,128)(2,1)} %add_convert_fusion), calls=%async_computation | async-start | bytes 524288 | tf_op jit(solution)/shard_map/all_to_all | solution.py:594
  100.8 1.1 %add_convert_fusion.3 = (bf16[512,256]{1,0:T(8,128)(2,1)S(1)}, bf16[512,256]{1,0:T(8,128)(2,1)S(1)}) fusion(bf16[512,256]{1,0:T(8,128)(2,1)S(1)} %collective-permute-done.15, bf16[1024,256]{1,0:T(8,128)(2,1)S(1)} %copy-done.8, bf16[1024,256]{1,0:T(8,128)(2,1)S(1)} %copy-done.6, bf16[512,256]{1,0:T(8,128)(2,1)} %collective-permute-done.16, ...), kind=kLoop, calls=%fused_computation.6 | loop fusion | flops 1572864 | bytes 2097152 | tf_op jit(solution)/shard_map/convert_element_type | solution.py:426
  102.8 7.7 %all-to-all-done = bf16[8,64,256]{2,1,0:T(8,128)(2,1)S(1)} async-done(((bf16[8,64,256]{2,1,0:T(8,128)(2,1)}), bf16[8,64,256]{2,1,0:T(8,128)(2,1)S(1)}, u32[]{:S(2)}, u32[]{:S(2)}) %all-to-all-start) | async-done | bytes 262176 | tf_op jit(solution)/shard_map/all_to_all | solution.py:594
  (73 shorter events, 12.5 us)
Async XLA Ops:
  6.5 5.7 %collective-permute-start = (bf16[128,512]{1,0:T(8,128)(2,1)}, bf16[128,512]{1,0:T(8,128)(2,1)S(1)}, u32[]{:S(2)}, u32[]{:S(2)}) collective-permute-start(bf16[128,512]{1,0:T(8,128)(2,1)} %get-tuple-element.66), channel_id=1, source_target_pairs={{0,8},{4,12},{8,0},{12,4},{16,24},{20,28},{24,16},{28,20},{32,40},... | collective-permute-start | bytes 393224 | tf_op jit(solution)/shard_map/ppermute | solution.py:422
  8.5 5.4 %collective-permute-start.1 = (bf16[256,512]{1,0:T(8,128)(2,1)}, bf16[256,512]{1,0:T(8,128)(2,1)S(1)}, u32[]{:S(2)}, u32[]{:S(2)}) collective-permute-start(bf16[256,512]{1,0:T(8,128)(2,1)} %get-tuple-element.68), channel_id=1, source_target_pairs={{0,4},{4,0},{8,12},{12,8},{16,20},{20,16},{24,28},{28,24},{32,36},... | collective-permute-start | bytes 786440 | tf_op jit(solution)/shard_map/ppermute | solution.py:422
  12.2 1.7 %collective-permute-start.2 = (bf16[128,512]{1,0:T(8,128)(2,1)S(1)}, bf16[128,512]{1,0:T(8,128)(2,1)S(1)}, u32[]{:S(2)}, u32[]{:S(2)}) collective-permute-start(bf16[128,512]{1,0:T(8,128)(2,1)S(1)} %collective-permute-done.refs_3_), channel_id=1, source_target_pairs={{0,4},{4,0},{8,12},{12,8},{16,20},{20,16},{24,28},{28,24},{32,36},... | collective-permute-start | bytes 393224 | tf_op jit(solution)/shard_map/ppermute | solution.py:422
  14.6 19.3 %copy-start.1 = (bf16[256,1024]{1,0:T(8,128)(2,1)S(1)}, bf16[256,1024]{1,0:T(8,128)(2,1)}, u32[]{:S(2)}) copy-start(bf16[256,1024]{1,0:T(8,128)(2,1)} %w_ref.1) | copy-start | bytes 1572868
  33.2 5.2 %collective-permute-start.3 = (bf16[128,512]{1,0:T(8,128)(2,1)}, bf16[128,512]{1,0:T(8,128)(2,1)S(1)}, u32[]{:S(2)}, u32[]{:S(2)}) collective-permute-start(bf16[128,512]{1,0:T(8,128)(2,1)} %get-tuple-element.78), channel_id=1, source_target_pairs={{0,4},{4,0},{8,12},{12,8},{16,20},{20,16},{24,28},{28,24},{32,36},... | collective-permute-start | bytes 393224 | tf_op jit(solution)/shard_map/ppermute | solution.py:422
  33.7 18.6 %copy-start.2 = (s32[3]{0:T(128)}, s32[3]{0:T(128)S(1)}, u32[]{:S(2)}) copy-start(s32[3]{0:T(128)S(1)} %pad_add_fusion.at_ref) | copy-start | bytes 40
  33.7 22.2 %collective-permute-start.6 = (bf16[256,512]{1,0:T(8,128)(2,1)}, bf16[256,512]{1,0:T(8,128)(2,1)}, u32[]{:S(2)}, u32[]{:S(2)}) collective-permute-start(bf16[256,512]{1,0:T(8,128)(2,1)} %get-tuple-element.92), channel_id=1, source_target_pairs={{0,4},{4,0},{8,12},{12,8},{16,20},{20,16},{24,28},{28,24},{32,36},... | collective-permute-start | bytes 786440 | tf_op jit(solution)/shard_map/ppermute | solution.py:422
  36.2 16.1 %collective-permute-start.4 = (bf16[1024,256]{1,0:T(8,128)(2,1)S(1)}, bf16[1024,256]{1,0:T(8,128)(2,1)S(1)}, u32[]{:S(2)}, u32[]{:S(2)}) collective-permute-start(bf16[1024,256]{1,0:T(8,128)(2,1)S(1)} %get-tuple-element.73), channel_id=1, source_target_pairs={{0,1},{1,2},{2,3},{3,0},{4,5},{5,6},{6,7},{7,4},{8,9},{9,10},{10,1... | collective-permute-start | bytes 1572872 | tf_op jit(solution)/shard_map/ppermute | solution.py:418
  37.5 14.9 %collective-permute-start.5 = (bf16[1024,256]{1,0:T(8,128)(2,1)S(1)}, bf16[1024,256]{1,0:T(8,128)(2,1)S(1)}, u32[]{:S(2)}, u32[]{:S(2)}) collective-permute-start(bf16[1024,256]{1,0:T(8,128)(2,1)S(1)} %get-tuple-element.74), channel_id=1, source_target_pairs={{0,3},{1,0},{2,1},{3,2},{4,7},{5,4},{6,5},{7,6},{8,11},{9,8},{10,9... | collective-permute-start | bytes 1572872 | tf_op jit(solution)/shard_map/ppermute | solution.py:418
  39.3 16.6 %collective-permute-start.7 = (bf16[128,512]{1,0:T(8,128)(2,1)S(1)}, bf16[128,512]{1,0:T(8,128)(2,1)}, u32[]{:S(2)}, u32[]{:S(2)}) collective-permute-start(bf16[128,512]{1,0:T(8,128)(2,1)S(1)} %add_convert_fusion.11), channel_id=1, source_target_pairs={{0,8},{4,12},{8,0},{12,4},{16,24},{20,28},{24,16},{28,20},{32,40},... | collective-permute-start | bytes 393224 | tf_op jit(solution)/shard_map/ppermute | solution.py:422
  52.5 13.1 %collective-permute-start.9 = (bf16[512,256]{1,0:T(8,128)(2,1)S(1)}, bf16[512,256]{1,0:T(8,128)(2,1)S(1)}, u32[]{:S(2)}, u32[]{:S(2)}) collective-permute-start(bf16[512,256]{1,0:T(8,128)(2,1)S(1)} %get-tuple-element.126), channel_id=1, source_target_pairs={{0,3},{1,0},{2,1},{3,2},{4,7},{5,4},{6,5},{7,6},{8,11},{9,8},{10,9... | collective-permute-start | bytes 786440 | tf_op jit(solution)/shard_map/ppermute | solution.py:418
  53.3 15.3 %copy-start.3 = (s32[3]{0:T(128)S(1)}, s32[3]{0:T(128)}, u32[]{:S(2)}) copy-start(s32[3]{0:T(128)} %copy-done.2) | copy-start | bytes 40
  53.3 12.3 %collective-permute-start.8 = (bf16[512,256]{1,0:T(8,128)(2,1)S(1)}, bf16[512,256]{1,0:T(8,128)(2,1)S(1)}, u32[]{:S(2)}, u32[]{:S(2)}) collective-permute-start(bf16[512,256]{1,0:T(8,128)(2,1)S(1)} %get-tuple-element.127), channel_id=1, source_target_pairs={{0,1},{1,2},{2,3},{3,0},{4,5},{5,6},{6,7},{7,4},{8,9},{9,10},{10,1... | collective-permute-start | bytes 786440 | tf_op jit(solution)/shard_map/ppermute | solution.py:418
  65.6 3.0 %collective-permute-start.12 = (bf16[32,64,256]{2,1,0:T(8,128)(2,1)}, bf16[32,64,256]{2,1,0:T(8,128)(2,1)S(1)}, u32[]{:S(2)}, u32[]{:S(2)}) collective-permute-start(bf16[32,64,256]{2,1,0:T(8,128)(2,1)} %get-tuple-element.109), channel_id=1, source_target_pairs={{0,4},{4,0},{8,12},{12,8},{16,20},{20,16},{24,28},{28,24},{32,36},... | collective-permute-start | bytes 3145736 | tf_op jit(solution)/shard_map/ppermute | solution.py:422
  71.0 5.8 %collective-permute-start.14 = (bf16[4,64,256]{2,1,0:T(8,128)(2,1)S(1)}, bf16[4,64,256]{2,1,0:T(8,128)(2,1)S(1)}, u32[]{:S(2)}, u32[]{:S(2)}) collective-permute-start(bf16[4,64,256]{2,1,0:T(8,128)(2,1)S(1)} %get-tuple-element.113), channel_id=1, source_target_pairs={{0,192},{4,196},{8,200},{12,204},{16,208},{20,212},{24,216},{28,22... | collective-permute-start | bytes 393224 | tf_op jit(solution)/shard_map/ppermute | solution.py:570
  73.8 13.7 %collective-permute-start.10 = (bf16[1024,256]{1,0:T(8,128)(2,1)S(1)}, bf16[1024,256]{1,0:T(8,128)(2,1)S(1)}, u32[]{:S(2)}, u32[]{:S(2)}) collective-permute-start(bf16[1024,256]{1,0:T(8,128)(2,1)S(1)} %copy-done.12), channel_id=1, source_target_pairs={{0,1},{1,2},{2,3},{3,0},{4,5},{5,6},{6,7},{7,4},{8,9},{9,10},{10,1... | collective-permute-start | bytes 1572872 | tf_op jit(solution)/shard_map/ppermute | solution.py:418
  74.0 14.8 %collective-permute-start.11 = (bf16[1024,256]{1,0:T(8,128)(2,1)S(1)}, bf16[1024,256]{1,0:T(8,128)(2,1)S(1)}, u32[]{:S(2)}, u32[]{:S(2)}) collective-permute-start(bf16[1024,256]{1,0:T(8,128)(2,1)S(1)} %copy-done.11), channel_id=1, source_target_pairs={{0,3},{1,0},{2,1},{3,2},{4,7},{5,4},{6,5},{7,6},{8,11},{9,8},{10,9... | collective-permute-start | bytes 1572872 | tf_op jit(solution)/shard_map/ppermute | solution.py:418
  75.8 6.3 %collective-permute-start.13 = (bf16[4,64,256]{2,1,0:T(8,128)(2,1)S(1)}, bf16[4,64,256]{2,1,0:T(8,128)(2,1)S(1)}, u32[]{:S(2)}, u32[]{:S(2)}) collective-permute-start(bf16[4,64,256]{2,1,0:T(8,128)(2,1)S(1)} %get-tuple-element.111), channel_id=1, source_target_pairs={{0,64},{4,68},{8,72},{12,76},{16,80},{20,84},{24,88},{28,92},{32,9... | collective-permute-start | bytes 393224 | tf_op jit(solution)/shard_map/ppermute | solution.py:570
  76.9 14.7 %collective-permute-start.18 = (bf16[8,64,256]{2,1,0:T(8,128)(2,1)S(1)}, bf16[8,64,256]{2,1,0:T(8,128)(2,1)S(1)}, u32[]{:S(2)}, u32[]{:S(2)}) collective-permute-start(bf16[8,64,256]{2,1,0:T(8,128)(2,1)S(1)} %pad_maximum_fusion.3), channel_id=1, source_target_pairs={{0,192},{4,196},{8,200},{12,204},{16,208},{20,212},{24,216},{28,22... | collective-permute-start | bytes 786440 | tf_op jit(solution)/shard_map/ppermute | solution.py:570
  82.2 9.4 %collective-permute-start.17 = (bf16[8,64,256]{2,1,0:T(8,128)(2,1)S(1)}, bf16[8,64,256]{2,1,0:T(8,128)(2,1)S(1)}, u32[]{:S(2)}, u32[]{:S(2)}) collective-permute-start(bf16[8,64,256]{2,1,0:T(8,128)(2,1)S(1)} %pad_maximum_fusion.2), channel_id=1, source_target_pairs={{0,64},{4,68},{8,72},{12,76},{16,80},{20,84},{24,88},{28,92},{32,9... | collective-permute-start | bytes 786440 | tf_op jit(solution)/shard_map/ppermute | solution.py:570
  82.5 18.3 %copy-start.6 = (bf16[1024,256]{1,0:T(8,128)(2,1)S(1)}, bf16[1024,256]{1,0:T(8,128)(2,1)}, u32[]{:S(2)}) copy-start(bf16[1024,256]{1,0:T(8,128)(2,1)} %get-tuple-element.105) | copy-start | bytes 1572868
  89.6 11.3 %collective-permute-start.15 = (bf16[512,256]{1,0:T(8,128)(2,1)S(1)}, bf16[512,256]{1,0:T(8,128)(2,1)S(1)}, u32[]{:S(2)}, u32[]{:S(2)}) collective-permute-start(bf16[512,256]{1,0:T(8,128)(2,1)S(1)} %get-tuple-element.122), channel_id=1, source_target_pairs={{0,1},{1,2},{2,3},{3,0},{4,5},{5,6},{6,7},{7,4},{8,9},{9,10},{10,1... | collective-permute-start | bytes 786440 | tf_op jit(solution)/shard_map/ppermute | solution.py:418
  89.8 11.1 %collective-permute-start.16 = (bf16[512,256]{1,0:T(8,128)(2,1)S(1)}, bf16[512,256]{1,0:T(8,128)(2,1)}, u32[]{:S(2)}, u32[]{:S(2)}) collective-permute-start(bf16[512,256]{1,0:T(8,128)(2,1)S(1)} %get-tuple-element.123), channel_id=1, source_target_pairs={{0,3},{1,0},{2,1},{3,2},{4,7},{5,4},{6,5},{7,6},{8,11},{9,8},{10,9... | collective-permute-start | bytes 786440 | tf_op jit(solution)/shard_map/ppermute | solution.py:418
  92.4 18.1 %all-to-all-start = ((bf16[8,64,256]{2,1,0:T(8,128)(2,1)}), bf16[8,64,256]{2,1,0:T(8,128)(2,1)S(1)}, u32[]{:S(2)}, u32[]{:S(2)}) async-start(bf16[8,64,256]{2,1,0:T(8,128)(2,1)} %add_convert_fusion), calls=%async_computation | async-start | bytes 524288 | tf_op jit(solution)/shard_map/all_to_all | solution.py:594
  (12 other events, 51.6 us)

commit v5 on v4

--- a/solution.py
+++ b/solution.py
@@ -190,9 +190,10 @@
 
 
 def forward_kernel(*refs):
-    entries, q_ref, da_ref = refs[:5], refs[5], refs[6]
-    ot_ref, stat_ref, qgt_ref, g2_ref, g3a_ref, g3b_ref = refs[7:13]
-    w_s, vt_s, kt_s, qm_s, dm_s, grad_s = refs[13:]
+    entries, q_ref, da_ref, at_ref, wo_ref = refs[:5], *refs[5:9]
+    ot_ref, stat_ref, qgt_ref, g2_ref, g3a_ref, g3b_ref = refs[9:15]
+    out_refs = refs[15:19]
+    w_s, vt_s, kt_s, qm_s, dm_s, grad_s = refs[19:]
     step = pl.program_id(0)
     for kb in range(5):
         rows = slice(kb * BLOCK, (kb + 1) * BLOCK)
@@ -255,6 +256,11 @@
         grad_s[:, lo : lo + 128] += key_grad
         grad_s[:, COLS + lo : COLS + lo + 128] += value_grad
 
+    attended = ot_ref[...].T
+    for first, second, ref in zip(ring_columns(0), ring_columns(1), out_refs):
+        cols = column_group(at_ref[1], jnp.where(step == 0, first, second))
+        ref[...] = dot_nn(attended, wo_ref[:, cols]).astype(bf16)
+
     @pl.when(step == 1)
     def _():
         for ref, first, count in ((g2_ref, 0, 256), (g3a_ref, 256, 128), (g3b_ref, 384, 128)):
@@ -263,7 +269,7 @@
             ref[:, COLS:] = grad_s[rows, COLS:].astype(bf16)
 
 
-def attend(entries, queries, d_attended):
+def attend(entries, queries, d_attended, at, w_out):
     part = pl.BlockSpec((SPAN, COLS), lambda i: (i, 0))
     turned = pl.BlockSpec((COLS, SPAN), lambda i: (0, i))
     two = pl.BlockSpec((BLOCK, 2 * COLS), lambda i: (0, 0))
@@ -279,8 +285,11 @@
             three,
             part,
             part,
+            pl.BlockSpec(memory_space=pltpu.SMEM),
+            pl.BlockSpec((COLS, WIDTH), lambda i: (0, 0)),
         ],
-        out_specs=[turned, pl.BlockSpec((8, SPAN), lambda i: (0, i)), turned, two, three, three],
+        out_specs=[turned, pl.BlockSpec((8, SPAN), lambda i: (0, i)), turned, two, three, three]
+        + [part] * 4,
         out_shape=[
             shape((COLS, ROWS)),
             shape((8, ROWS), f32),
@@ -288,7 +297,8 @@
             shape((BLOCK, 2 * COLS)),
             shape((BLOCK // 2, 2 * COLS)),
             shape((BLOCK // 2, 2 * COLS)),
-        ],
+        ]
+        + [shape((ROWS, COLS))] * 4,
         scratch_shapes=[
             pltpu.VMEM((2, KEYS, SPAN), bf16),
             pltpu.VMEM((COLS, KEYS), bf16),
@@ -300,7 +310,7 @@
         compiler_params=params(60),
         cost_estimate=cost(4 * 4 * 4 * ROWS * KEYS * 64, 6 * MIB),
         name="attend",
-    )(*entries, queries, d_attended)
+    )(*entries, queries, d_attended, at, w_out)
 
 
 def block_grads(key_rows, value_rows, keys_t, offsets, qm, dm, stat, inner):
@@ -390,29 +400,6 @@
     return pl.ds(pl.multiple_of(((here + offset) & 3) * COLS, COLS), COLS)
 
 
-def out_kernel(at_ref, ot_ref, w_ref, right_ref, left_ref, hold_ref, mine_ref):
-    outs = (right_ref, left_ref, hold_ref, mine_ref)
-    for half in range(2):
-        rows = slice(half * SPAN, (half + 1) * SPAN)
-        attended = ot_ref[:, rows].T
-        for offset, ref in zip(ring_columns(half), outs):
-            part = dot_nn(attended, w_ref[:, column_group(at_ref[1], offset)])
-            ref[rows] = part.astype(bf16)
-
-
-def project_out(at, attended_t, w_out):
-    vmem = pl.BlockSpec(memory_space=pltpu.VMEM)
-    return pl.pallas_call(
-        out_kernel,
-        in_specs=[pl.BlockSpec(memory_space=pltpu.SMEM), vmem, vmem],
-        out_specs=[vmem] * 4,
-        out_shape=[shape((ROWS, COLS))] * 4,
-        compiler_params=params(24),
-        cost_estimate=cost(ROWS * WIDTH * COLS, 4 * MIB),
-        name="project_out",
-    )(at, attended_t, w_out)
-
-
 def shifted(value, by):
     size = lax.axis_size("head")
     return lax.ppermute(value, "head", [(i, (i + by) % size) for i in range(size)])
@@ -605,12 +592,11 @@
     d_attended, three_a = lax.optimization_barrier((d_attended, three_a))
     three_b = swapped(three_a, 1)
     entries = (key_value, own_2, level_two, three_a, three_b)
-    attended_t, stats, query_part, grad_2, grad_3a, grad_3b = attend(
-        entries, queries, d_attended
+    attended_t, stats, query_part, grad_2, grad_3a, grad_3b, *out_parts = attend(
+        entries, queries, d_attended, at, w_out
     )
     got_2 = swapped(grad_2, 1)
     got_3b = swapped(grad_3b, 1)
-    out_parts = project_out(at, attended_t, w_out)
     out_got = head_sum_first(*out_parts)
     grad_3 = add(grad_3a, got_3b)
     near = (key_value, own_2, queries, d_attended, stats, query_part)

time: 112 us -> 110 us (0.982)
  local copies, waits for them, and re-layouts: 4.94 us -> 3.42 us
  waiting for transfers between devices: 19.7 us -> 20.9 us
    unnamed x32 -> x26, local copies, waits for them, and re-layouts: 4.3 us -> 2.77 us
    pallas_call x1 -> x0, Pallas kernels: 1.29 us -> none  [project_out(): pl.pallas_call(out_kernel, in_specs=[pl.BlockSpec(memory_space=pltpu.SMEM...]
  transfers between devices with their start and end apart: 20 -> 20, of which waited for: 9 -> 9; matrix products, arithmetic and copies ran while one was open for 5% -> 4% of each run, Pallas kernels for 23% -> 23%
where the time goes in v5:
time: 110 us
  Pallas kernels  51.5 us (47%)
  starting transfers between devices  28.6 us (26%)
  waiting for transfers between devices  20.9 us (19%)
  other arithmetic  4.82 us (4%)
  local copies, waits for them, and re-layouts  3.42 us (3%)
    pallas_call x1, Pallas kernels, attend(): pl.pallas_call(forward_kernel, grid=(2,), in_specs=[pl.BlockSpec((SPAN, 2...  19.7 us
    pallas_call x1, Pallas kernels, near_grads(): pl.pallas_call(near_kernel, grid=(2,), in_specs=[near, sibling, part, par...  11.3 us
    pallas_call x1, Pallas kernels, tail(): pl.pallas_call(tail_kernel, in_specs=[pl.BlockSpec(memory_space=pltpu.SME...  9.87 us
    ppermute x8, starting transfers between devices, shifted(): lax.ppermute(value, 'head', [(i, (i + by) % size) for i in range(size)])  9.48 us
    all_to_all x1, waiting for transfers between devices, z_sum(): blocks = lax.all_to_all(blocks, 'seq', 0, 0, axis_index_groups=along_z)  8.62 us
    all_to_all x1, starting transfers between devices, z_sum(): blocks = lax.all_to_all(blocks, 'seq', 0, 0, axis_index_groups=along_z)  7.57 us
    ppermute x8, waiting for transfers between devices, shifted(): lax.ppermute(value, 'head', [(i, (i + by) % size) for i in range(size)])  6.56 us
    ppermute x4, starting transfers between devices, moved(): lax.ppermute(value, 'seq', [(i, (i + by) % size) for i in range(size)])  6.51 us
  transfers between devices with their start and end apart: 20, of which 9 were waited for; matrix products, arithmetic and copies ran while one was open for 4% of the time, Pallas kernels for 23%

profile of v5, /device:TPU:24, one launch (start us, length us, event | category | flops | bytes accessed | tf_op | source)
XLA Modules:
  0.0 110.1 jit_solution(10446050098964341027)
XLA Ops:
  0.6 5.8 %project_tokens.1 = (bf16[1024,512]{1,0:T(8,128)(2,1)}, bf16[512,512]{1,0:T(8,128)(2,1)}, bf16[256,512]{1,0:T(8,128)(2,1)}, bf16[128,512]{1,0:T(8,128)(2,1)}, bf16[1024,256]{1,0:T(8,128)(2,1)}) custom-call(bf16[1024,1024]{1,0:T(8,128)(2,1)} %x_hbm.3, bf16[1024,256]{1,0:T(8,128)(2,1)} %wk_hbm.3, bf16[1024,256]{1,0:T(8,128)(2,1)} %wv_hbm.3, ...), custom_call_target="tpu_custom_call" | custom-call | flops 1610612736 | bytes 7340032 | tf_op jit(solution)/shard_map/project_tokens/pallas_call | solution.py:119
  6.5 2.0 %collective-permute-start = (bf16[128,512]{1,0:T(8,128)(2,1)}, bf16[128,512]{1,0:T(8,128)(2,1)S(1)}, u32[]{:S(2)}, u32[]{:S(2)}) collective-permute-start(bf16[128,512]{1,0:T(8,128)(2,1)} %get-tuple-element.66), channel_id=1, source_target_pairs={{0,8},{4,12},{8,0},{12,4},{16,24},{20,28},{24,16},{28,20},{32,40},... | collective-permute-start | bytes 393224 | tf_op jit(solution)/shard_map/ppermute | solution.py:409
  8.5 3.6 %project_cotangent.1.refs_6_.da_ref = bf16[1024,256]{1,0:T(8,128)(2,1)} custom-call(bf16[1024,1024]{1,0:T(8,128)(2,1)} %c_hbm.3, bf16[256,1024]{1,0:T(8,128)(2,1)} %refs_8_.1), custom_call_target="tpu_custom_call" | custom-call | flops 536870912 | bytes 4194304 | tf_op jit(solution)/shard_map/project_cotangent/pallas_call | solution.py:152
  14.6 19.7 %attend.1 = (bf16[256,1024]{1,0:T(8,128)(2,1)}, f32[8,1024]{1,0:T(8,128)}, f32[256,1024]{1,0:T(8,128)}, bf16[256,512]{1,0:T(8,128)(2,1)}, bf16[128,512]{1,0:T(8,...) custom-call(bf16[1024,512]{1,0:T(8,128)(2,1)} %get-tuple-element.79., ...), custom_call_target="tpu_custom_call" | custom-call | flops 10737418240 | bytes 6291456 | tf_op jit(solution)/shard_map/attend/pallas_call | solution.py:277
  34.9 1.2 %collective-permute-start.4 = (bf16[1024,256]{1,0:T(8,128)(2,1)}, bf16[1024,256]{1,0:T(8,128)(2,1)S(1)}, u32[]{:S(2)}, u32[]{:S(2)}) collective-permute-start(bf16[1024,256]{1,0:T(8,128)(2,1)} %get-tuple-element.72), channel_id=1, source_target_pairs={{0,1},{1,2},{2,3},{3,0},{4,5},{5,6},{6,7},{7,4},{8,9},{9,10},{10,1... | collective-permute-start | bytes 1572872 | tf_op jit(solution)/shard_map/ppermute | solution.py:405
  36.1 0.8 collective-permute-start.5
  37.0 0.9 add_convert_fusion.11
  37.9 1.7 %collective-permute-start.7 = (bf16[128,512]{1,0:T(8,128)(2,1)S(1)}, bf16[128,512]{1,0:T(8,128)(2,1)S(1)}, u32[]{:S(2)}, u32[]{:S(2)}) collective-permute-start(bf16[128,512]{1,0:T(8,128)(2,1)S(1)} %add_convert_fusion.11), channel_id=1, source_target_pairs={{0,8},{4,12},{8,0},{12,4},{16,24},{20,28},{24,16},{28,20},{32,40},... | collective-permute-start | bytes 393224 | tf_op jit(solution)/shard_map/ppermute | solution.py:409
  39.6 11.3 %near_grads.1 = (bf16[256,1024]{1,0:T(8,128)(2,1)}, f32[1024,512]{1,0:T(8,128)}, f32[512,512]{1,0:T(8,128)}) custom-call(bf16[1024,512]{1,0:T(8,128)(2,1)} %get-tuple-element.79.refs_0_.near, bf16[512,512]{1,0:T(8,128)(2,1)} %get-tuple-element.80.refs_1_.c2, bf16[1024,256]{1,0:T(8,128)(2,1)} %get-tuple-element.81.refs_5_.q_ref, ...), custom_call_target="tpu_custom_call" | custom-call | flops 8053063680 | bytes 8388608 | tf_op jit(solution)/shard_map/near_grads/pallas_call | solution.py:368
  51.9 2.8 %collective-permute-start.8 = (bf16[512,256]{1,0:T(8,128)(2,1)S(1)}, bf16[512,256]{1,0:T(8,128)(2,1)S(1)}, u32[]{:S(2)}, u32[]{:S(2)}) collective-permute-start(bf16[512,256]{1,0:T(8,128)(2,1)S(1)} %get-tuple-element.127), channel_id=1, source_target_pairs={{0,1},{1,2},{2,3},{3,0},{4,5},{5,6},{6,7},{7,4},{8,9},{9,10},{10,1... | collective-permute-start | bytes 786440 | tf_op jit(solution)/shard_map/ppermute | solution.py:405
  55.5 9.9 %tail.1 = (bf16[1024,256]{1,0:T(8,128)(2,1)}, bf16[1024,256]{1,0:T(8,128)(2,1)}, bf16[1024,256]{1,0:T(8,128)(2,1)}, bf16[1024,256]{1,0:T(8,128)(2,1)}, bf16[32,6...) custom-call(s32[3]{0:T(128)} %pad_add_fusion.refs_7_.at_ref, f32[1024,512]{1,0:T(8,128)} %get-tuple-element.89.own_hbm, ...), custom_call_target="tpu_custom_call" | custom-call | flops 3758096384 | bytes 14680064 | tf_op jit(solution)/shard_map/tail/pallas_call | solution.py:510
  65.5 2.9 %collective-permute-done.12.refs_1_ = bf16[32,64,256]{2,1,0:T(8,128)(2,1)S(1)} collective-permute-done((bf16[32,64,256]{2,1,0:T(8,128)(2,1)}, bf16[32,64,256]{2,1,0:T(8,128)(2,1)S(1)}, u32[]{:S(2)}, u32[]{:S(2)}) %collective-permute-start.12) | collective-permute-done | bytes 1048608 | tf_op jit(solution)/shard_map/ppermute | solution.py:409
  68.3 1.2 %copy-done = bf16[32,64,256]{2,1,0:T(8,128)(2,1)S(1)} copy-done((bf16[32,64,256]{2,1,0:T(8,128)(2,1)S(1)}, bf16[32,64,256]{2,1,0:T(8,128)(2,1)}, u32[]{:S(2)}) %copy-start) | copy-done | bytes 1048600
  69.6 1.2 %sum_cores.1 = (bf16[4,64,256]{2,1,0:T(8,128)(2,1)S(1)}, bf16[4,64,256]{2,1,0:T(8,128)(2,1)S(1)}, bf16[8,64,256]{2,1,0:T(8,128)(2,1)S(1)}, bf16[8,64,256]{2,1,0:T(8,128)(2,1)S(1)}, bf16[8,64,256]{2,1,0:T(8,128)(2,1)S(1)}) custom-call(s32[3]{0:T(128)S(1)} %copy-done.1, bf16[32,64,256]{2,1,0:T(8,128)(2,1)S(1)} %copy-done, ...), custom_call_target="tpu_custom_call" | custom-call | tf_op jit(solution)/shard_map/sum_cores/pallas_call | solution.py:540
  70.7 2.6 %collective-permute-start.14 = (bf16[4,64,256]{2,1,0:T(8,128)(2,1)S(1)}, bf16[4,64,256]{2,1,0:T(8,128)(2,1)S(1)}, u32[]{:S(2)}, u32[]{:S(2)}) collective-permute-start(bf16[4,64,256]{2,1,0:T(8,128)(2,1)S(1)} %get-tuple-element.113), channel_id=1, source_target_pairs={{0,192},{4,196},{8,200},{12,204},{16,208},{20,212},{24,216},{28,22... | collective-permute-start | bytes 393224 | tf_op jit(solution)/shard_map/ppermute | solution.py:557
  73.5 1.8 %collective-permute-start.11 = (bf16[1024,256]{1,0:T(8,128)(2,1)S(1)}, bf16[1024,256]{1,0:T(8,128)(2,1)S(1)}, u32[]{:S(2)}, u32[]{:S(2)}) collective-permute-start(bf16[1024,256]{1,0:T(8,128)(2,1)S(1)} %copy-done.6), channel_id=1, source_target_pairs={{0,3},{1,0},{2,1},{3,2},{4,7},{5,4},{6,5},{7,6},{8,11},{9,8},{10,9... | collective-permute-start | bytes 1572872 | tf_op jit(solution)/shard_map/ppermute | solution.py:405
  75.5 0.9 collective-permute-done.14
  76.4 3.8 %collective-permute-start.18 = (bf16[8,64,256]{2,1,0:T(8,128)(2,1)S(1)}, bf16[8,64,256]{2,1,0:T(8,128)(2,1)S(1)}, u32[]{:S(2)}, u32[]{:S(2)}) collective-permute-start(bf16[8,64,256]{2,1,0:T(8,128)(2,1)S(1)} %pad_maximum_fusion.3), channel_id=1, source_target_pairs={{0,192},{4,196},{8,200},{12,204},{16,208},{20,212},{24,216},{28,22... | collective-permute-start | bytes 786440 | tf_op jit(solution)/shard_map/ppermute | solution.py:557
  80.2 1.4 %collective-permute-done.13 = bf16[4,64,256]{2,1,0:T(8,128)(2,1)S(1)} collective-permute-done((bf16[4,64,256]{2,1,0:T(8,128)(2,1)S(1)}, bf16[4,64,256]{2,1,0:T(8,128)(2,1)S(1)}, u32[]{:S(2)}, u32[]{:S(2)}) %collective-permute-start.13) | collective-permute-done | bytes 131104 | tf_op jit(solution)/shard_map/ppermute | solution.py:557
  82.0 5.0 %collective-permute-done.10 = bf16[1024,256]{1,0:T(8,128)(2,1)S(1)} collective-permute-done((bf16[1024,256]{1,0:T(8,128)(2,1)S(1)}, bf16[1024,256]{1,0:T(8,128)(2,1)S(1)}, u32[]{:S(2)}, u32[]{:S(2)}) %collective-permute-start.10) | collective-permute-done | bytes 524320 | tf_op jit(solution)/shard_map/ppermute | solution.py:405
  87.0 1.3 %collective-permute-done.11 = bf16[1024,256]{1,0:T(8,128)(2,1)S(1)} collective-permute-done((bf16[1024,256]{1,0:T(8,128)(2,1)S(1)}, bf16[1024,256]{1,0:T(8,128)(2,1)S(1)}, u32[]{:S(2)}, u32[]{:S(2)}) %collective-permute-start.11) | collective-permute-done | bytes 524320 | tf_op jit(solution)/shard_map/ppermute | solution.py:405
  88.7 1.8 %collective-permute-start.16 = (bf16[512,256]{1,0:T(8,128)(2,1)S(1)}, bf16[512,256]{1,0:T(8,128)(2,1)S(1)}, u32[]{:S(2)}, u32[]{:S(2)}) collective-permute-start(bf16[512,256]{1,0:T(8,128)(2,1)S(1)} %get-tuple-element.123), channel_id=1, source_target_pairs={{0,3},{1,0},{2,1},{3,2},{4,7},{5,4},{6,5},{7,6},{8,11},{9,8},{10,9... | collective-permute-start | bytes 786440 | tf_op jit(solution)/shard_map/ppermute | solution.py:405
  91.4 7.6 %all-to-all-start = ((bf16[8,64,256]{2,1,0:T(8,128)(2,1)}), bf16[8,64,256]{2,1,0:T(8,128)(2,1)S(1)}, u32[]{:S(2)}, u32[]{:S(2)}) async-start(bf16[8,64,256]{2,1,0:T(8,128)(2,1)} %add_convert_fusion), calls=%async_computation | async-start | bytes 524288 | tf_op jit(solution)/shard_map/all_to_all | solution.py:581
  100.8 8.6 %all-to-all-done = bf16[8,64,256]{2,1,0:T(8,128)(2,1)S(1)} async-done(((bf16[8,64,256]{2,1,0:T(8,128)(2,1)}), bf16[8,64,256]{2,1,0:T(8,128)(2,1)S(1)}, u32[]{:S(2)}, u32[]{:S(2)}) %all-to-all-start) | async-done | bytes 262176 | tf_op jit(solution)/shard_map/all_to_all | solution.py:581
  (66 shorter events, 9.5 us)
Async XLA Ops:
  6.5 5.7 %collective-permute-start = (bf16[128,512]{1,0:T(8,128)(2,1)}, bf16[128,512]{1,0:T(8,128)(2,1)S(1)}, u32[]{:S(2)}, u32[]{:S(2)}) collective-permute-start(bf16[128,512]{1,0:T(8,128)(2,1)} %get-tuple-element.66), channel_id=1, source_target_pairs={{0,8},{4,12},{8,0},{12,4},{16,24},{20,28},{24,16},{28,20},{32,40},... | collective-permute-start | bytes 393224 | tf_op jit(solution)/shard_map/ppermute | solution.py:409
  8.5 5.4 %collective-permute-start.1 = (bf16[256,512]{1,0:T(8,128)(2,1)}, bf16[256,512]{1,0:T(8,128)(2,1)S(1)}, u32[]{:S(2)}, u32[]{:S(2)}) collective-permute-start(bf16[256,512]{1,0:T(8,128)(2,1)} %get-tuple-element.68), channel_id=1, source_target_pairs={{0,4},{4,0},{8,12},{12,8},{16,20},{20,16},{24,28},{28,24},{32,36},... | collective-permute-start | bytes 786440 | tf_op jit(solution)/shard_map/ppermute | solution.py:409
  12.2 1.7 %collective-permute-start.2 = (bf16[128,512]{1,0:T(8,128)(2,1)S(1)}, bf16[128,512]{1,0:T(8,128)(2,1)S(1)}, u32[]{:S(2)}, u32[]{:S(2)}) collective-permute-start(bf16[128,512]{1,0:T(8,128)(2,1)S(1)} %collective-permute-done.refs_3_), channel_id=1, source_target_pairs={{0,4},{4,0},{8,12},{12,8},{16,20},{20,16},{24,28},{28,24},{32,36},... | collective-permute-start | bytes 393224 | tf_op jit(solution)/shard_map/ppermute | solution.py:409
  34.3 2.6 %collective-permute-start.3 = (bf16[128,512]{1,0:T(8,128)(2,1)}, bf16[128,512]{1,0:T(8,128)(2,1)S(1)}, u32[]{:S(2)}, u32[]{:S(2)}) collective-permute-start(bf16[128,512]{1,0:T(8,128)(2,1)} %get-tuple-element.77), channel_id=1, source_target_pairs={{0,4},{4,0},{8,12},{12,8},{16,20},{20,16},{24,28},{28,24},{32,36},... | collective-permute-start | bytes 393224 | tf_op jit(solution)/shard_map/ppermute | solution.py:409
  34.8 19.9 %collective-permute-start.6 = (bf16[256,512]{1,0:T(8,128)(2,1)}, bf16[256,512]{1,0:T(8,128)(2,1)S(1)}, u32[]{:S(2)}, u32[]{:S(2)}) collective-permute-start(bf16[256,512]{1,0:T(8,128)(2,1)} %get-tuple-element.91), channel_id=1, source_target_pairs={{0,4},{4,0},{8,12},{12,8},{16,20},{20,16},{24,28},{28,24},{32,36},... | collective-permute-start | bytes 786440 | tf_op jit(solution)/shard_map/ppermute | solution.py:409
  34.9 16.0 %collective-permute-start.4 = (bf16[1024,256]{1,0:T(8,128)(2,1)}, bf16[1024,256]{1,0:T(8,128)(2,1)S(1)}, u32[]{:S(2)}, u32[]{:S(2)}) collective-permute-start(bf16[1024,256]{1,0:T(8,128)(2,1)} %get-tuple-element.72), channel_id=1, source_target_pairs={{0,1},{1,2},{2,3},{3,0},{4,5},{5,6},{6,7},{7,4},{8,9},{9,10},{10,1... | collective-permute-start | bytes 1572872 | tf_op jit(solution)/shard_map/ppermute | solution.py:405
  36.1 15.1 %collective-permute-start.5 = (bf16[1024,256]{1,0:T(8,128)(2,1)}, bf16[1024,256]{1,0:T(8,128)(2,1)S(1)}, u32[]{:S(2)}, u32[]{:S(2)}) collective-permute-start(bf16[1024,256]{1,0:T(8,128)(2,1)} %get-tuple-element.73), channel_id=1, source_target_pairs={{0,3},{1,0},{2,1},{3,2},{4,7},{5,4},{6,5},{7,6},{8,11},{9,8},{10,9... | collective-permute-start | bytes 1572872 | tf_op jit(solution)/shard_map/ppermute | solution.py:405
  37.9 13.3 %copy-start.3 = (bf16[1024,256]{1,0:T(8,128)(2,1)S(1)}, bf16[1024,256]{1,0:T(8,128)(2,1)}, u32[]{:S(2)}) copy-start(bf16[1024,256]{1,0:T(8,128)(2,1)} %get-tuple-element.101) | copy-start | bytes 1572868
  37.9 16.8 %collective-permute-start.7 = (bf16[128,512]{1,0:T(8,128)(2,1)S(1)}, bf16[128,512]{1,0:T(8,128)(2,1)S(1)}, u32[]{:S(2)}, u32[]{:S(2)}) collective-permute-start(bf16[128,512]{1,0:T(8,128)(2,1)S(1)} %add_convert_fusion.11), channel_id=1, source_target_pairs={{0,8},{4,12},{8,0},{12,4},{16,24},{20,28},{24,16},{28,20},{32,40},... | collective-permute-start | bytes 393224 | tf_op jit(solution)/shard_map/ppermute | solution.py:409
  51.4 14.0 %collective-permute-start.9 = (bf16[512,256]{1,0:T(8,128)(2,1)S(1)}, bf16[512,256]{1,0:T(8,128)(2,1)S(1)}, u32[]{:S(2)}, u32[]{:S(2)}) collective-permute-start(bf16[512,256]{1,0:T(8,128)(2,1)S(1)} %get-tuple-element.126), channel_id=1, source_target_pairs={{0,3},{1,0},{2,1},{3,2},{4,7},{5,4},{6,5},{7,6},{8,11},{9,8},{10,9... | collective-permute-start | bytes 786440 | tf_op jit(solution)/shard_map/ppermute | solution.py:405
  51.9 13.4 %collective-permute-start.8 = (bf16[512,256]{1,0:T(8,128)(2,1)S(1)}, bf16[512,256]{1,0:T(8,128)(2,1)S(1)}, u32[]{:S(2)}, u32[]{:S(2)}) collective-permute-start(bf16[512,256]{1,0:T(8,128)(2,1)S(1)} %get-tuple-element.127), channel_id=1, source_target_pairs={{0,1},{1,2},{2,3},{3,0},{4,5},{5,6},{6,7},{7,4},{8,9},{9,10},{10,1... | collective-permute-start | bytes 786440 | tf_op jit(solution)/shard_map/ppermute | solution.py:405
  55.5 12.9 %copy-start.1 = (s32[3]{0:T(128)S(1)}, s32[3]{0:T(128)}, u32[]{:S(2)}) copy-start(s32[3]{0:T(128)} %pad_add_fusion.refs_7_.at_ref) | copy-start | bytes 40
  65.4 3.0 %collective-permute-start.12 = (bf16[32,64,256]{2,1,0:T(8,128)(2,1)}, bf16[32,64,256]{2,1,0:T(8,128)(2,1)S(1)}, u32[]{:S(2)}, u32[]{:S(2)}) collective-permute-start(bf16[32,64,256]{2,1,0:T(8,128)(2,1)} %get-tuple-element.109), channel_id=1, source_target_pairs={{0,4},{4,0},{8,12},{12,8},{16,20},{20,16},{24,28},{28,24},{32,36},... | collective-permute-start | bytes 3145736 | tf_op jit(solution)/shard_map/ppermute | solution.py:409
  70.7 5.6 %collective-permute-start.14 = (bf16[4,64,256]{2,1,0:T(8,128)(2,1)S(1)}, bf16[4,64,256]{2,1,0:T(8,128)(2,1)S(1)}, u32[]{:S(2)}, u32[]{:S(2)}) collective-permute-start(bf16[4,64,256]{2,1,0:T(8,128)(2,1)S(1)} %get-tuple-element.113), channel_id=1, source_target_pairs={{0,192},{4,196},{8,200},{12,204},{16,208},{20,212},{24,216},{28,22... | collective-permute-start | bytes 393224 | tf_op jit(solution)/shard_map/ppermute | solution.py:557
  73.3 13.7 %collective-permute-start.10 = (bf16[1024,256]{1,0:T(8,128)(2,1)S(1)}, bf16[1024,256]{1,0:T(8,128)(2,1)S(1)}, u32[]{:S(2)}, u32[]{:S(2)}) collective-permute-start(bf16[1024,256]{1,0:T(8,128)(2,1)S(1)} %copy-done.7), channel_id=1, source_target_pairs={{0,1},{1,2},{2,3},{3,0},{4,5},{5,6},{6,7},{7,4},{8,9},{9,10},{10,1... | collective-permute-start | bytes 1572872 | tf_op jit(solution)/shard_map/ppermute | solution.py:405
  73.5 14.8 %collective-permute-start.11 = (bf16[1024,256]{1,0:T(8,128)(2,1)S(1)}, bf16[1024,256]{1,0:T(8,128)(2,1)S(1)}, u32[]{:S(2)}, u32[]{:S(2)}) collective-permute-start(bf16[1024,256]{1,0:T(8,128)(2,1)S(1)} %copy-done.6), channel_id=1, source_target_pairs={{0,3},{1,0},{2,1},{3,2},{4,7},{5,4},{6,5},{7,6},{8,11},{9,8},{10,9... | collective-permute-start | bytes 1572872 | tf_op jit(solution)/shard_map/ppermute | solution.py:405
  75.3 12.9 %copy-start.2 = (bf16[1024,256]{1,0:T(8,128)(2,1)S(1)}, bf16[1024,256]{1,0:T(8,128)(2,1)}, u32[]{:S(2)}) copy-start(bf16[1024,256]{1,0:T(8,128)(2,1)} %get-tuple-element.115) | copy-start | bytes 1572868
  75.4 6.3 %collective-permute-start.13 = (bf16[4,64,256]{2,1,0:T(8,128)(2,1)S(1)}, bf16[4,64,256]{2,1,0:T(8,128)(2,1)S(1)}, u32[]{:S(2)}, u32[]{:S(2)}) collective-permute-start(bf16[4,64,256]{2,1,0:T(8,128)(2,1)S(1)} %get-tuple-element.111), channel_id=1, source_target_pairs={{0,64},{4,68},{8,72},{12,76},{16,80},{20,84},{24,88},{28,92},{32,9... | collective-permute-start | bytes 393224 | tf_op jit(solution)/shard_map/ppermute | solution.py:557
  76.4 14.1 %collective-permute-start.18 = (bf16[8,64,256]{2,1,0:T(8,128)(2,1)S(1)}, bf16[8,64,256]{2,1,0:T(8,128)(2,1)S(1)}, u32[]{:S(2)}, u32[]{:S(2)}) collective-permute-start(bf16[8,64,256]{2,1,0:T(8,128)(2,1)S(1)} %pad_maximum_fusion.3), channel_id=1, source_target_pairs={{0,192},{4,196},{8,200},{12,204},{16,208},{20,212},{24,216},{28,22... | collective-permute-start | bytes 786440 | tf_op jit(solution)/shard_map/ppermute | solution.py:557
  81.7 8.8 %collective-permute-start.17 = (bf16[8,64,256]{2,1,0:T(8,128)(2,1)S(1)}, bf16[8,64,256]{2,1,0:T(8,128)(2,1)S(1)}, u32[]{:S(2)}, u32[]{:S(2)}) collective-permute-start(bf16[8,64,256]{2,1,0:T(8,128)(2,1)S(1)} %pad_maximum_fusion.2), channel_id=1, source_target_pairs={{0,64},{4,68},{8,72},{12,76},{16,80},{20,84},{24,88},{28,92},{32,9... | collective-permute-start | bytes 786440 | tf_op jit(solution)/shard_map/ppermute | solution.py:557
  82.0 17.7 %copy-start.5 = (bf16[1024,256]{1,0:T(8,128)(2,1)S(1)}, bf16[1024,256]{1,0:T(8,128)(2,1)}, u32[]{:S(2)}) copy-start(bf16[1024,256]{1,0:T(8,128)(2,1)} %get-tuple-element.105) | copy-start | bytes 1572868
  88.4 11.3 %collective-permute-start.15 = (bf16[512,256]{1,0:T(8,128)(2,1)S(1)}, bf16[512,256]{1,0:T(8,128)(2,1)S(1)}, u32[]{:S(2)}, u32[]{:S(2)}) collective-permute-start(bf16[512,256]{1,0:T(8,128)(2,1)S(1)} %get-tuple-element.122), channel_id=1, source_target_pairs={{0,1},{1,2},{2,3},{3,0},{4,5},{5,6},{6,7},{7,4},{8,9},{9,10},{10,1... | collective-permute-start | bytes 786440 | tf_op jit(solution)/shard_map/ppermute | solution.py:405
  88.7 11.0 %collective-permute-start.16 = (bf16[512,256]{1,0:T(8,128)(2,1)S(1)}, bf16[512,256]{1,0:T(8,128)(2,1)S(1)}, u32[]{:S(2)}, u32[]{:S(2)}) collective-permute-start(bf16[512,256]{1,0:T(8,128)(2,1)S(1)} %get-tuple-element.123), channel_id=1, source_target_pairs={{0,3},{1,0},{2,1},{3,2},{4,7},{5,4},{6,5},{7,6},{8,11},{9,8},{10,9... | collective-permute-start | bytes 786440 | tf_op jit(solution)/shard_map/ppermute | solution.py:405
  91.4 18.1 %all-to-all-start = ((bf16[8,64,256]{2,1,0:T(8,128)(2,1)}), bf16[8,64,256]{2,1,0:T(8,128)(2,1)S(1)}, u32[]{:S(2)}, u32[]{:S(2)}) async-start(bf16[8,64,256]{2,1,0:T(8,128)(2,1)} %add_convert_fusion), calls=%async_computation | async-start | bytes 524288 | tf_op jit(solution)/shard_map/all_to_all | solution.py:581
  (9 other events, 25.7 us)
